TPU v7x, 32 devices: a whole 2x2x4 slice. The times are simulated.
32 devices in a mesh: dp: 8 (over z, y), fsdp: 4 (over x, core).
Axes of the slice: x: 2, y: 2, z: 4, core: 2. Of those that a mesh axis runs over, the one named last changes fastest.
Arguments:
- tokens: bfloat16 [16, 512, 768], P('dp', 'fsdp'), may hold values from -6 to 6
- cotangent: bfloat16 [16, 512, 768], P('dp', 'fsdp'), may hold values from -6 to 6
- lengths: int32 [16], P('dp'), may hold values from 128 to 512, as said below
- routes: int32 [16, 512, 2], P('dp', 'fsdp'), may hold values from 0 to 3, all different within a row; in each aligned block of 128 rows (0 to 127, 128 to 255, ..., all dimensions but the last counted through in order) at most 128 rows name the same one
- gains: float32 [2, 768], P(None, ('dp', 'fsdp')), may hold values from 0.5 to 1.5
- gain_moms: float32 [2, 768], P(None, ('dp', 'fsdp')), may hold values from -256 to 256
- w_dense: float32 [768, 7168], P(('dp', 'fsdp'))
- mom_dense: float32 [768, 7168], P(('dp', 'fsdp')), may hold values from -160 to 160
- w_router: float32 [768, 4], P(('dp', 'fsdp')), may hold values from -0.15625 to 0.15625
- mom_router: float32 [768, 4], P(('dp', 'fsdp')), may hold values from -56 to 56
- w_down: float32 [2048, 768], P(('dp', 'fsdp')), may hold values from -0.125 to 0.125
- mom_down: float32 [2048, 768], P(('dp', 'fsdp')), may hold values from -160 to 160
- e_gate_up: float32 [4, 2, 768, 2048], P('fsdp', None, 'dp'), may hold values from -0.21875 to 0.21875
- e_mom_gate_up: float32 [4, 2, 768, 2048], P('fsdp', None, 'dp'), may hold values from -56 to 56
- e_down: float32 [4, 2048, 768], P('fsdp', 'dp'), may hold values from -0.125 to 0.125
- e_mom_down: float32 [4, 2048, 768], P('fsdp', 'dp'), may hold values from -56 to 56
Outputs:
- output: bfloat16 [16, 512, 768], P('dp', 'fsdp')
- d_tokens: bfloat16 [16, 512, 768], P('dp', 'fsdp')
- new_gain_moms: float32 [2, 768], P(None, ('dp', 'fsdp'))
- new_gains: float32 [2, 768], P(None, ('dp', 'fsdp'))
- new_mom_dense: float32 [768, 7168], P(('dp', 'fsdp'))
- new_dense: float32 [768, 7168], P(('dp', 'fsdp'))
- new_mom_router: float32 [768, 4], P(('dp', 'fsdp'))
- new_router: float32 [768, 4], P(('dp', 'fsdp'))
- new_mom_down: float32 [2048, 768], P(('dp', 'fsdp'))
- new_down: float32 [2048, 768], P(('dp', 'fsdp'))
- new_e_mom_gate_up: float32 [4, 2, 768, 2048], P('fsdp', None, 'dp')
- new_e_gate_up: float32 [4, 2, 768, 2048], P('fsdp', None, 'dp')
- new_e_mom_down: float32 [4, 2048, 768], P('fsdp', 'dp')
- new_e_down: float32 [4, 2048, 768], P('fsdp', 'dp')
Inputs may be any that keep to these rules, and one draw needn't show every extreme that they name: `lengths`: rows 2 i and 2 i + 1 stand together; one of the two, which one drawn from the seed, holds a sequence of all 512 positions. `routes`: in each aligned block of 128 positions of a slot row (the rows of one device) no expert is named by more than 128 tokens, and some block reaches 128; a token names 2 different experts.
All inputs are finite; a program needn't handle non-finite values.
Results may differ from a plain program's by a relative error of at most 0.015.
The roundings to bfloat16 on the way count: a program that leaves them out, or rounds other values in their place, can miss the bound.
Values may be sent and summed in bfloat16 or wider, within the bound.
No kernel may reach another device: no remote copies, remote signals or barrier semaphores. Data moves between devices by JAX's collectives and lax.ppermute only.
A program may use at most 448 MiB of HBM per device.

v0:
```python
import math

import jax
import jax.numpy as jnp
from jax import lax
from jax.sharding import PartitionSpec as P

HEADS = 12
NS_STEPS = 5


NORM_EPSILON = 1e-06
POLY_FIRST = 3.4445
POLY_SECOND = -4.775
POLY_THIRD = 2.0315
HIGHEST_PRECISION = lax.Precision.HIGHEST
MASK_VALUE = -1e30
DENSE_RATES = (0.8, 5.0, 0.8, 0.8)
ROUTER_RATE = 0.4
DOWN_RATE = 0.5
EXPERT_RATES = (0.8, 0.8, 0.5)
GAIN_DECAY = 0.9
MUON_DECAY = 0.5


def bf_dot(left, right):
    return jnp.dot(left, right, preferred_element_type=jnp.float32)


def first_dot(left, right, precision=None):
    return lax.dot_general(
        left,
        right,
        (((0,), (0,)), ((), ())),
        precision=precision,
        preferred_element_type=jnp.float32,
    )


def last_dot(left, right, precision=None):
    return lax.dot_general(
        left,
        right,
        (((1,), (1,)), ((), ())),
        precision=precision,
        preferred_element_type=jnp.float32,
    )


def statistics(values):
    inverse = lax.rsqrt(jnp.mean(values * values, axis=-1, keepdims=True) + NORM_EPSILON)
    return (values * inverse, inverse)


def norm_back(grad_out, scaled, inverse, gain_row):
    gain_grad = jnp.sum(grad_out * scaled, axis=(0, 1))
    through = grad_out * gain_row
    grad_in = inverse * (through - scaled * jnp.mean(through * scaled, axis=-1, keepdims=True))
    return (grad_in, gain_grad)


def rotation_tables(head_size, places):
    half_size = head_size // 2
    frequency = 10000.0 ** (-2.0 * jnp.arange(half_size, dtype=jnp.float32) / head_size)
    angles = places.astype(jnp.float32)[:, None] * frequency[None, :]
    return (jnp.cos(angles)[:, None, :], jnp.sin(angles)[:, None, :], half_size)


def rotate(values, places):
    cosine, sine, half_size = rotation_tables(values.shape[-1], places)
    first_half = values[..., :half_size]
    second_half = values[..., half_size:]
    return jnp.concatenate(
        [first_half * cosine - second_half * sine, second_half * cosine + first_half * sine],
        axis=-1,
    )


def rotate_back(grads, places):
    cosine, sine, half_size = rotation_tables(grads.shape[-1], places)
    first_half = grads[..., :half_size]
    second_half = grads[..., half_size:]
    return jnp.concatenate(
        [first_half * cosine + second_half * sine, second_half * cosine - first_half * sine],
        axis=-1,
    )


def silu_slope(values):
    logistic = jax.nn.sigmoid(values)
    return logistic * (1.0 + values * (1.0 - logistic))


def orthogonal(matrix):
    if matrix.shape[0] > matrix.shape[1]:
        return orthogonal(matrix.T).T
    current = matrix / (jnp.sqrt(jnp.sum(matrix * matrix)) + 1e-07)
    for sweep in range(NS_STEPS):
        gram = jnp.dot(current, current.T, precision=HIGHEST_PRECISION)
        poly = POLY_SECOND * gram + POLY_THIRD * jnp.dot(gram, gram, precision=HIGHEST_PRECISION)
        current = POLY_FIRST * current + jnp.dot(poly, current, precision=HIGHEST_PRECISION)
    return current


def per_device(
    tokens,
    cotangent,
    lengths,
    routes,
    gains,
    gain_moms,
    w_dense,
    mom_dense,
    w_router,
    mom_router,
    w_down,
    mom_down,
    e_gate_up,
    e_mom_gate_up,
    e_down,
    e_mom_down,
):
    seq_rows, local_len, width = tokens.shape
    head_count = HEADS
    head_size = width // head_count
    seq_parts = lax.axis_size("fsdp")
    seq_index = lax.axis_index("fsdp")
    row_len = local_len * seq_parts
    expert_count = w_router.shape[1]
    top_count = routes.shape[2]
    most_rows = 2 * local_len * top_count // expert_count
    capacity = seq_rows * most_rows
    places = seq_index * local_len + jnp.arange(local_len)
    valid = (places[None, :] < lengths[:, None]).astype(jnp.float32)
    dense_copy, router_copy, down_copy, gain_copy = (
        lax.all_gather(w_dense.astype(jnp.bfloat16), ("dp", "fsdp"), axis=0, tiled=True),
        lax.all_gather(w_router.astype(jnp.bfloat16), ("dp", "fsdp"), axis=0, tiled=True),
        lax.all_gather(w_down.astype(jnp.bfloat16), ("dp", "fsdp"), axis=0, tiled=True),
        lax.all_gather(gains.astype(jnp.bfloat16), ("dp", "fsdp"), axis=1, tiled=True),
    )
    gate_up_copy, edown_copy = (
        lax.all_gather(e_gate_up.astype(jnp.bfloat16), "dp", axis=2, tiled=True),
        lax.all_gather(e_down.astype(jnp.bfloat16), "dp", axis=1, tiled=True),
    )
    gain_one = gain_copy[0].astype(jnp.float32)
    gain_two = gain_copy[1].astype(jnp.float32)
    ff_shared = down_copy.shape[0]
    gate_weight = gate_up_copy[0, 0]
    up_weight = gate_up_copy[0, 1]
    down_weight = edown_copy[0]
    ff_width = gate_weight.shape[1]
    inputs = tokens.astype(jnp.float32)
    scaled_one, inverse_one = statistics(inputs)
    normed_one = (scaled_one * gain_one).astype(jnp.bfloat16).reshape(-1, width)
    projected = bf_dot(normed_one, dense_copy[:, : 3 * width]).reshape(
        seq_rows, local_len, 3, head_count, head_size
    )
    queries = rotate(projected[:, :, 0], places).astype(jnp.bfloat16)
    keys_local = rotate(projected[:, :, 1], places).astype(jnp.bfloat16)
    values_local = projected[:, :, 2].astype(jnp.bfloat16)
    keys_all, values_all = (
        lax.all_gather(keys_local, "fsdp", axis=1, tiled=True),
        lax.all_gather(values_local, "fsdp", axis=1, tiled=True),
    )
    block_len = min(512, row_len)
    block_count = row_len // block_len
    stat_shape = (seq_rows, head_count, local_len)
    head_shape = (seq_rows, local_len, head_count, head_size)

    def masked_scores(query_part, query_places, key_part, key_places):
        raw_scores = (
            jnp.einsum("rqhd,rkhd->rhqk", query_part, key_part, preferred_element_type=jnp.float32)
            * 0.125
        )
        allowed = (key_places[None, None, :] <= query_places[None, :, None]) & (
            key_places[None, None, :] < lengths[:, None, None]
        )
        return jnp.where(allowed[:, None], raw_scores, MASK_VALUE)

    def key_block(index):
        start_at = index * block_len
        key_part = lax.dynamic_slice_in_dim(keys_all, start_at, block_len, 1)
        value_part = lax.dynamic_slice_in_dim(values_all, start_at, block_len, 1)
        return (key_part, value_part, start_at + jnp.arange(block_len))

    def running_max(carry, index):
        top_score, exp_total = carry
        key_part, value_part, key_places = key_block(index)
        scores = masked_scores(queries, places, key_part, key_places)
        new_top = jnp.maximum(top_score, jnp.max(scores, axis=-1))
        exp_total = exp_total * jnp.exp(top_score - new_top) + jnp.sum(
            jnp.exp(scores - new_top[..., None]), axis=-1
        )
        return ((new_top, exp_total), None)

    start_stats = (
        jnp.full(stat_shape, MASK_VALUE, jnp.float32),
        jnp.zeros(stat_shape, jnp.float32),
    )
    (top_score, exp_total), _ = lax.scan(running_max, start_stats, jnp.arange(block_count))
    log_total = top_score + jnp.log(exp_total)

    def weigh_values(total_acc, index):
        key_part, value_part, key_places = key_block(index)
        scores = masked_scores(queries, places, key_part, key_places)
        weights = jnp.exp(scores - log_total[..., None]).astype(jnp.bfloat16)
        return (
            total_acc
            + jnp.einsum(
                "rhqk,rkhd->rqhd", weights, value_part, preferred_element_type=jnp.float32
            ),
            None,
        )

    attended, _ = lax.scan(
        weigh_values, jnp.zeros(head_shape, jnp.float32), jnp.arange(block_count)
    )
    attended_copy = attended.reshape(-1, width).astype(jnp.bfloat16)
    branch = bf_dot(attended_copy, dense_copy[:, 3 * width : 4 * width]).reshape(
        seq_rows, local_len, width
    )
    middle = inputs + branch
    scaled_two, inverse_two = statistics(middle)
    normed_two = (scaled_two * gain_two).astype(jnp.bfloat16).reshape(-1, width)
    logits = bf_dot(normed_two, router_copy)
    route_rows = routes.reshape(-1, top_count)
    chosen = jnp.take_along_axis(logits, route_rows, axis=1)
    gates = jax.nn.softmax(chosen, axis=-1)
    shared_pre = bf_dot(normed_two, dense_copy[:, 4 * width :])
    shared_gate = shared_pre[:, :ff_shared]
    shared_up = shared_pre[:, ff_shared:]
    shared_act = (jax.nn.silu(shared_gate) * shared_up).astype(jnp.bfloat16)
    shared_out = bf_dot(shared_act, down_copy)
    pair_experts = routes.reshape(seq_rows, local_len * top_count)
    onehot = (pair_experts[..., None] == jnp.arange(expert_count, dtype=jnp.int32)).astype(
        jnp.int32
    )
    ranking = jnp.sum((jnp.cumsum(onehot, axis=1) - onehot) * onehot, axis=-1)
    slot_local = (jnp.arange(seq_rows, dtype=jnp.int32)[:, None] * most_rows + ranking).reshape(-1)
    slot_ids = pair_experts.reshape(-1) * capacity + slot_local
    pair_count = seq_rows * local_len * top_count
    table = (
        jnp.full((expert_count * capacity,), -1, jnp.int32)
        .at[slot_ids]
        .set(jnp.arange(pair_count, dtype=jnp.int32))
    )
    present = table >= 0
    picked = jnp.where(present, table, 0)
    outgoing = jnp.where(
        present[:, None], normed_two[picked // top_count], jnp.zeros((), jnp.bfloat16)
    ).reshape(expert_count, capacity, width)
    arrived = lax.all_to_all(outgoing, "fsdp", split_axis=0, concat_axis=0, tiled=True)
    sources, item_count, _ = arrived.shape
    arrived_rows = arrived.reshape(sources * item_count, width)
    pre_act = jnp.concatenate(
        [bf_dot(arrived_rows, gate_weight), bf_dot(arrived_rows, up_weight)], axis=-1
    )
    activated = (jax.nn.silu(pre_act[:, :ff_width]) * pre_act[:, ff_width:]).astype(jnp.bfloat16)
    result = bf_dot(activated, down_weight).astype(jnp.bfloat16).reshape(sources, item_count, width)
    returned_rows = lax.all_to_all(result, "fsdp", split_axis=0, concat_axis=0, tiled=True)
    pre_all = pre_act.reshape(sources, item_count, 2 * ff_width)
    pair_out = (
        returned_rows.reshape(expert_count * capacity, width)[slot_ids]
        .reshape(-1, top_count, width)
        .astype(jnp.float32)
    )
    mixed = jnp.sum(gates[..., None] * pair_out, axis=1)
    total = middle + (shared_out + mixed).reshape(seq_rows, local_len, width)
    output = (total * valid[..., None]).astype(jnp.bfloat16)
    d_out = cotangent.astype(jnp.float32) * valid[..., None]
    d_flat = d_out.reshape(-1, width)
    d_flat_copy = d_flat.astype(jnp.bfloat16)
    grad_down = first_dot(shared_act, d_flat_copy)
    d_sact = last_dot(d_flat_copy, down_copy)
    d_shared = jnp.concatenate(
        [d_sact * shared_up * silu_slope(shared_gate), d_sact * jax.nn.silu(shared_gate)], axis=-1
    ).astype(jnp.bfloat16)
    grad_shared = first_dot(normed_two, d_shared)
    d_normed = last_dot(d_shared, dense_copy[:, 4 * width :])
    d_gates = jnp.sum(d_flat[:, None, :] * pair_out, axis=-1)
    d_chosen = gates * (d_gates - jnp.sum(gates * d_gates, axis=-1, keepdims=True))
    route_table = (route_rows[..., None] == jnp.arange(expert_count, dtype=jnp.int32)).astype(
        jnp.float32
    )
    d_logits = jnp.sum(d_chosen[..., None] * route_table, axis=1).astype(jnp.bfloat16)
    grad_router = first_dot(normed_two, d_logits)
    d_normed = d_normed + last_dot(d_logits, router_copy)
    d_pairs = (gates[..., None] * d_flat[:, None, :]).reshape(-1, width).astype(jnp.bfloat16)
    d_outgoing = jnp.where(present[:, None], d_pairs[picked], jnp.zeros((), jnp.bfloat16)).reshape(
        expert_count, capacity, width
    )
    d_arrived = lax.all_to_all(d_outgoing, "fsdp", split_axis=0, concat_axis=0, tiled=True)
    d_result = d_arrived.reshape(-1, width)
    pre_rows = pre_all.reshape(-1, 2 * ff_width)
    expert_gate = pre_rows[:, :ff_width]
    expert_up = pre_rows[:, ff_width:]
    activated = (jax.nn.silu(expert_gate) * expert_up).astype(jnp.bfloat16)
    grad_edown = first_dot(activated, d_result)
    d_activated = last_dot(d_result, down_weight)
    d_pre = jnp.concatenate(
        [d_activated * expert_up * silu_slope(expert_gate), d_activated * jax.nn.silu(expert_gate)],
        axis=-1,
    ).astype(jnp.bfloat16)
    arrived_rows = arrived.reshape(-1, width)
    grad_gate = first_dot(arrived_rows, d_pre[:, :ff_width])
    grad_up = first_dot(arrived_rows, d_pre[:, ff_width:])
    d_inputs = (
        (last_dot(d_pre[:, :ff_width], gate_weight) + last_dot(d_pre[:, ff_width:], up_weight))
        .astype(jnp.bfloat16)
        .reshape(d_arrived.shape)
    )
    d_returned = lax.all_to_all(d_inputs, "fsdp", split_axis=0, concat_axis=0, tiled=True).reshape(
        expert_count * capacity, width
    )
    d_normed = d_normed + jnp.sum(
        d_returned[slot_ids].astype(jnp.float32).reshape(-1, top_count, width), axis=1
    )
    d_mid_norm, grad_gain_two = norm_back(
        d_normed.reshape(seq_rows, local_len, width), scaled_two, inverse_two, gain_two
    )
    d_middle = d_out + d_mid_norm
    d_branch = d_middle.reshape(-1, width).astype(jnp.bfloat16)
    grad_wout = first_dot(attended_copy, d_branch)
    d_attended = (
        last_dot(d_branch, dense_copy[:, 3 * width : 4 * width])
        .reshape(head_shape)
        .astype(jnp.bfloat16)
    )

    def delta_pass(delta_acc, index):
        key_part, value_part, key_places = key_block(index)
        weights = jnp.exp(
            masked_scores(queries, places, key_part, key_places) - log_total[..., None]
        )
        slopes = jnp.einsum(
            "rqhd,rkhd->rhqk", d_attended, value_part, preferred_element_type=jnp.float32
        )
        return (delta_acc + jnp.sum(weights * slopes, axis=-1), None)

    delta, _ = lax.scan(delta_pass, jnp.zeros(stat_shape, jnp.float32), jnp.arange(block_count))

    def make_pass():

        def query_pass(query_acc, index):
            key_part, value_part, key_places = key_block(index)
            weights = jnp.exp(
                masked_scores(queries, places, key_part, key_places) - log_total[..., None]
            )
            slopes = jnp.einsum(
                "rqhd,rkhd->rhqk", d_attended, value_part, preferred_element_type=jnp.float32
            )
            score_grad = (weights * (slopes - delta[..., None])).astype(jnp.bfloat16)
            query_acc = query_acc + 0.125 * jnp.einsum(
                "rhqk,rkhd->rqhd", score_grad, key_part, preferred_element_type=jnp.float32
            )
            key_grad = 0.125 * jnp.einsum(
                "rhqk,rqhd->rkhd", score_grad, queries, preferred_element_type=jnp.float32
            )
            value_grad = jnp.einsum(
                "rhqk,rqhd->rkhd",
                weights.astype(jnp.bfloat16),
                d_attended,
                preferred_element_type=jnp.float32,
            )
            return (query_acc, (key_grad, value_grad))

        return query_pass

    d_query, (key_parts, value_parts) = lax.scan(
        make_pass(), jnp.zeros(head_shape, jnp.float32), jnp.arange(block_count)
    )
    key_whole = jnp.moveaxis(key_parts, 0, 1).reshape(seq_rows, row_len, width)
    value_whole = jnp.moveaxis(value_parts, 0, 1).reshape(seq_rows, row_len, width)
    key_value = lax.psum_scatter(
        jnp.concatenate([key_whole, value_whole], axis=-1), "fsdp", scatter_dimension=1, tiled=True
    )
    d_key = key_value[..., :width].reshape(head_shape)
    d_value = key_value[..., width:].reshape(head_shape)
    d_qkv = (
        jnp.stack([rotate_back(d_query, places), rotate_back(d_key, places), d_value], axis=2)
        .reshape(-1, 3 * width)
        .astype(jnp.bfloat16)
    )
    grad_qkv = first_dot(normed_one, d_qkv)
    d_one = last_dot(d_qkv, dense_copy[:, : 3 * width]).reshape(seq_rows, local_len, width)
    d_in_norm, grad_gain_one = norm_back(d_one, scaled_one, inverse_one, gain_one)
    d_tokens = (d_middle + d_in_norm).astype(jnp.bfloat16)
    grad_dense = jnp.concatenate([grad_qkv, grad_wout, grad_shared], axis=1)
    grad_gains = jnp.stack([grad_gain_one, grad_gain_two])
    part_dense, part_router, part_down, part_gains = (
        lax.psum_scatter(grad_dense, ("dp", "fsdp"), scatter_dimension=0, tiled=True),
        lax.psum_scatter(grad_router, ("dp", "fsdp"), scatter_dimension=0, tiled=True),
        lax.psum_scatter(grad_down, ("dp", "fsdp"), scatter_dimension=0, tiled=True),
        lax.psum_scatter(grad_gains, ("dp", "fsdp"), scatter_dimension=1, tiled=True),
    )
    total_slots = seq_rows * lax.axis_size("dp") * row_len
    gain_rate = 0.1 / math.sqrt(total_slots)
    new_gain_moms = GAIN_DECAY * gain_moms + part_gains
    new_gains = gains - gain_rate * new_gain_moms
    new_mom_dense = MUON_DECAY * mom_dense + part_dense
    new_mom_router = MUON_DECAY * mom_router + part_router
    new_mom_down = MUON_DECAY * mom_down + part_down
    device_index = lax.axis_index(("dp", "fsdp"))
    device_count = lax.axis_size(("dp", "fsdp"))
    owners = [number * device_count // 6 for number in range(6)]

    def owned(number, matrix):
        return lax.cond(device_index == owners[number], orthogonal, jnp.zeros_like, matrix)

    edges = (0, 3 * width, 4 * width, 4 * width + ff_shared, 4 * width + 2 * ff_shared)
    whole_dense, whole_router, whole_down = (
        lax.all_gather(new_mom_dense, ("dp", "fsdp"), axis=0, tiled=True),
        lax.all_gather(new_mom_router, ("dp", "fsdp"), axis=0, tiled=True),
        lax.all_gather(new_mom_down, ("dp", "fsdp"), axis=0, tiled=True),
    )
    orth_dense = jnp.concatenate(
        [owned(number, whole_dense[:, edges[number] : edges[number + 1]]) for number in range(4)],
        axis=1,
    )
    orth_router = owned(4, whole_router)
    orth_down = owned(5, whole_down)
    share_dense, share_router, share_down = (
        lax.psum_scatter(orth_dense, ("dp", "fsdp"), scatter_dimension=0, tiled=True),
        lax.psum_scatter(orth_router, ("dp", "fsdp"), scatter_dimension=0, tiled=True),
        lax.psum_scatter(orth_down, ("dp", "fsdp"), scatter_dimension=0, tiled=True),
    )
    column_rates = jnp.concatenate(
        [
            jnp.full((edges[number + 1] - edges[number],), DENSE_RATES[number], jnp.float32)
            for number in range(4)
        ]
    )
    new_dense = w_dense - column_rates[None, :] * share_dense
    new_router = w_router - ROUTER_RATE * share_router
    new_down = w_down - DOWN_RATE * share_down
    dp_index = lax.axis_index("dp")
    gate_rows = e_gate_up.shape[2]
    down_rows = e_down.shape[1]
    gate_term = jnp.stack([grad_gate, grad_up])[None] + lax.dynamic_update_slice(
        jnp.zeros((1, 2, width, ff_width), jnp.float32),
        MUON_DECAY * e_mom_gate_up,
        (0, 0, dp_index * gate_rows, 0),
    )
    down_term = grad_edown[None] + lax.dynamic_update_slice(
        jnp.zeros((1, ff_width, width), jnp.float32),
        MUON_DECAY * e_mom_down,
        (0, dp_index * down_rows, 0),
    )
    whole_gate_up, whole_edown = lax.psum((gate_term, down_term), "dp")
    orth_gate_up = jnp.stack([orthogonal(whole_gate_up[0, 0]), orthogonal(whole_gate_up[0, 1])])[
        None
    ]
    orth_edown = orthogonal(whole_edown[0])[None]
    new_e_mom_gate_up = lax.dynamic_slice_in_dim(whole_gate_up, dp_index * gate_rows, gate_rows, 2)
    gate_rates = jnp.array(EXPERT_RATES[:2], jnp.float32)[None, :, None, None]
    new_e_gate_up = e_gate_up - gate_rates * lax.dynamic_slice_in_dim(
        orth_gate_up, dp_index * gate_rows, gate_rows, 2
    )
    new_e_mom_down = lax.dynamic_slice_in_dim(whole_edown, dp_index * down_rows, down_rows, 1)
    new_e_down = e_down - EXPERT_RATES[2] * lax.dynamic_slice_in_dim(
        orth_edown, dp_index * down_rows, down_rows, 1
    )
    return (
        output,
        d_tokens,
        new_gain_moms,
        new_gains,
        new_mom_dense,
        new_dense,
        new_mom_router,
        new_router,
        new_mom_down,
        new_down,
        new_e_mom_gate_up,
        new_e_gate_up,
        new_e_mom_down,
        new_e_down,
    )


def solution(mesh):
    placed = (
        P("dp", "fsdp", None),
        P("dp", "fsdp", None),
        P("dp"),
        P("dp", "fsdp", None),
        P(None, ("dp", "fsdp")),
        P(None, ("dp", "fsdp")),
        P(("dp", "fsdp"), None),
        P(("dp", "fsdp"), None),
        P(("dp", "fsdp"), None),
        P(("dp", "fsdp"), None),
        P(("dp", "fsdp"), None),
        P(("dp", "fsdp"), None),
        P("fsdp", None, "dp", None),
        P("fsdp", None, "dp", None),
        P("fsdp", "dp", None),
        P("fsdp", "dp", None),
    )
    return jax.shard_map(
        per_device,
        mesh=mesh,
        in_specs=placed,
        out_specs=(
            P("dp", "fsdp", None),
            P("dp", "fsdp", None),
            P(None, ("dp", "fsdp")),
            P(None, ("dp", "fsdp")),
            P(("dp", "fsdp"), None),
            P(("dp", "fsdp"), None),
            P(("dp", "fsdp"), None),
            P(("dp", "fsdp"), None),
            P(("dp", "fsdp"), None),
            P(("dp", "fsdp"), None),
            P("fsdp", None, "dp", None),
            P("fsdp", None, "dp", None),
            P("fsdp", "dp", None),
            P("fsdp", "dp", None),
        ),
        check_vma=False,
    )
```

profile of v0, /device:TPU:26, one launch (start us, length us, event | category | flops | bytes accessed | tf_op | source)
XLA Modules:
  0.0 2442.5 jit_solution(3615984600457811004)
XLA Ops:
  9.9 32.9 %all-gather.1 = bf16[32,24,2]{1,2,0:T(2,128)(2,1)S(1)} all-gather(bf16[1,24,2]{1,2,0:T(2,128)(2,1)S(1)} %convert_bitcast_fusion.1), channel_id=1, replica_groups=mesh['dp'=8,'fsdp'=4] {'dp','fsdp'}, dimensions={0}, use_global_device_ids=true | all-gather | bytes 3168 | tf_op jit(solution)/shard_map/all_gather | solution.py:139
  47.3 52.4 %all-gather.13.cloned.1.call-done = bf16[768,7168]{1,0:T(8,128)(2,1)} async-done(((bf16[24,7168]{1,0:T(8,128)(2,1)}), bf16[768,7168]{1,0:T(8,128)(2,1)}) %all-gather.13.cloned.1.call-update) | async-done | bytes 11010064 | tf_op jit(solution)/shard_map/all_gather | solution.py:136
  127.4 32.4 %all-gather.2 = bf16[32,24,4]{1,2,0:T(4,128)(2,1)S(1)} all-gather(bf16[1,24,4]{1,2,0:T(4,128)(2,1)S(1)} %convert_bitcast_fusion), channel_id=1, replica_groups=mesh['dp'=8,'fsdp'=4] {'dp','fsdp'}, dimensions={0}, use_global_device_ids=true | all-gather | bytes 6336 | tf_op jit(solution)/shard_map/all_gather | solution.py:137
  223.0 31.6 %all-gather.19.cloned.1.call-done = bf16[1,2,768,2048]{3,2,1,0:T(8,128)(2,1)} async-done(((bf16[1,2,96,2048]{3,2,1,0:T(8,128)(2,1)}), bf16[1,2,768,2048]{3,2,1,0:T(8,128)(2,1)}) %all-gather.19.cloned.1.call-update) | async-done | bytes 6291472 | tf_op jit(solution)/shard_map/all_gather | solution.py:142
  267.9 48.5 %all-gather.21.cloned.1.call-done = bf16[1,2048,768]{2,1,0:T(8,128)(2,1)} async-done(((bf16[1,256,768]{2,1,0:T(8,128)(2,1)}), bf16[1,2048,768]{2,1,0:T(8,128)(2,1)}) %all-gather.21.cloned.1.call-update) | async-done | bytes 3145744 | tf_op jit(solution)/shard_map/all_gather | solution.py:143
  446.4 38.4 %reduce-scatter.9.cloned.1.call-done = f32[2,128,1536]{1,2,0:T(8,128)} async-done(((f32[2,512,1536]{1,2,0:T(8,128)}), f32[2,128,1536]{1,2,0:T(8,128)}) %reduce-scatter.9.cloned.1.call-update) | async-done | bytes 1572880 | tf_op jit(solution)/shard_map/reduce_scatter | solution.py:374
  556.6 49.2 %reduce-scatter.15.cloned.1.call-done = f32[64,768]{1,0:T(8,128)} async-done(((f32[2048,768]{1,0:T(8,128)}), f32[64,768]{1,0:T(8,128)}) %reduce-scatter.15.cloned.1.call-update) | async-done | bytes 196624 | tf_op jit(solution)/shard_map/reduce_scatter | solution.py:393
  607.5 227.4 %reduce-scatter.11.cloned.1.call-done = f32[24,7168]{1,0:T(8,128)} async-done(((f32[768,7168]{1,0:T(8,128)}), f32[24,7168]{1,0:T(8,128)}) %reduce-scatter.11.cloned.1.call-update) | async-done | bytes 688144 | tf_op jit(solution)/shard_map/reduce_scatter | solution.py:391
  838.3 44.7 %all-reduce.1 = f32[768,4]{0,1:T(4,128)S(1)} all-reduce(f32[768,4]{0,1:T(4,128)S(1)} %fusion.538), channel_id=7, replica_groups=mesh['dp'=8,'fsdp'=4] {'dp','fsdp'}, use_global_device_ids=true, to_apply=%region_36.37.clone | all-reduce | flops 3072 | bytes 24576
  883.1 33.9 %all-gather.3 = f32[32,24,4]{1,2,0:T(4,128)S(1)} all-gather(f32[1,24,4]{1,2,0:T(4,128)S(1)} %bitcast.558), channel_id=1, replica_groups=mesh['dp'=8,'fsdp'=4] {'dp','fsdp'}, dimensions={0}, use_global_device_ids=true | all-gather | bytes 12672 | tf_op jit(solution)/shard_map/all_gather | solution.py:413
  926.9 50.5 %all-reduce.3 = (f32[2,768]{1,0:T(2,128)S(1)}, f32[768,4]{0,1:T(4,128)S(1)}) all-reduce(f32[2,768]{1,0:T(2,128)S(1)} %pad_maximum_fusion.11, f32[768,4]{0,1:T(4,128)S(1)} %get-tuple-element.299), channel_id=4, replica_groups=mesh['dp'=8,'fsdp'=4] {'dp','fsdp'}, use_global_device_ids=true, to_apply=%region_21.22.clone | all-reduce | flops 4608 | bytes 36864
  981.3 427.5 %all-reduce.7.cloned.1.call-done = (f32[1,2,768,2048]{3,2,1,0:T(8,128)}, f32[1,2048,768]{1,2,0:T(8,128)}) async-done(((f32[1,2,768,2048]{3,2,1,0:T(8,128)}, f32[1,2048,768]{1,2,0:T(8,128)}), (f32[1,2,768,2048]{3,2,1,0:T(8,128)}, f32[1,2048,768]{1,2,0:T(8,128)})) %all-reduce.7.cloned.1.call-update) | async-done | bytes 18874384 | tf_op jit(solution)/shard_map/psum | solution.py:449
  1414.5 18.9 fusion.230
  1442.0 39.2 %all-gather.25.cloned.1.call-done = f32[2048,768]{1,0:T(8,128)} async-done(((f32[64,768]{1,0:T(8,128)}), f32[2048,768]{1,0:T(8,128)}) %all-gather.25.cloned.1.call-update) | async-done | bytes 6291472 | tf_op jit(solution)/shard_map/all_gather | solution.py:414
  1481.3 249.8 %conditional.11 = (f32[2048,768]{0,1:T(8,128)}) conditional(s32[]{:T(128)} %convert_element_type.245, () %tuple.57, f32[2048,768]{1,0:T(8,128)} %all-gather.25.cloned.1.call-done), branch_computations={%region_42.43_spmd, %region_43.45_spmd} | conditional | flops 172202852352 | bytes 351535296 | solution.py:408
  1493.9 19.3 fusion.224
  1535.3 16.9 fusion.223
  1561.1 24.6 %multiply_add_fusion.29 = (f32[768,2048]{1,0:T(8,128)}, f32[768,2048]{1,0:T(8,128)}) fusion(f32[768,2048]{1,0:T(8,128)} %copy-done.101, f32[2048,768]{0,1:T(8,128)S(1)} %bitcast.517, f32[]{:T(128)S(6)} %add.527, f32[768,768]{1,0:T(8,128)} %fusion.502, f32[768,768]{1,0:T(8,128)} %copy-done.14), kind=kOutput, calls=%fused_computation.227 | convolution fusion | flops 14509867008 | bytes 29884420 | tf_op jit(solution)/shard_map/cond/branch_1_fun/dot_general | solution.py:101
  1585.7 19.2 fusion.503
  1626.8 16.9 fusion.222
  1649.5 17.6 fusion.184
  1667.0 20.7 fusion.180
  1694.9 35.9 %fusion.176 = f32[2048,768]{0,1:T(8,128)} fusion(f32[768,2048]{1,0:T(8,128)} %fusion.184, f32[768,2048]{1,0:T(8,128)} %copy-done.22, f32[768,2048]{1,0:T(8,128)} %get-tuple-element.245, f32[768,2048]{1,0:T(8,128)} %copy-done.101, f32[768,768]{1,0:T(8,128)} %fusion.506, f32[768,768]{1,0:T(8,128)S(1)} %fusion.180, f32[768,2048]{1,0:T(8,128)} %get-tuple-element.244, ...), kind=kOutput, calls=%fused_computation.217 | convolution fusion | flops 14520877056 | bytes 48758788 | tf_op jit(solution)/shard_map/cond/branch_1_fun/dot_general | solution.py:101
  1737.6 21.2 bitcast_add_fusion.13
  1758.8 16.2 fusion.532
  1781.0 20.7 bitcast_add_fusion.12
  1801.7 17.6 fusion.462
  1828.1 25.2 %multiply_add_fusion.37 = (f32[768,2048]{1,0:T(8,128)}, f32[768,2048]{1,0:T(8,128)}) fusion(f32[768,2048]{1,0:T(8,128)} %copy-done.1, f32[768,2048]{1,0:T(8,128)S(1)} %get-tuple-element.281, f32[768,768]{1,0:T(8,128)} %fusion.534, f32[768,768]{1,0:T(8,128)} %copy-done.2), kind=kOutput, calls=%fused_computation.311 | convolution fusion | flops 14506721280 | bytes 29884416 | tf_op jit(solution)/shard_map/dot_general | solution.py:101
  1866.3 19.1 conditional.8
  1885.4 17.0 conditional.7
  1940.1 19.7 fusion.535
  1981.6 16.8 fusion.264
  2004.2 17.2 fusion.263
  2025.9 19.1 fusion.239
  2050.9 19.3 fusion.241
  2070.3 16.2 fusion.513
  2108.5 16.2 fusion.515
  2146.7 16.2 fusion.517
  2184.9 16.2 fusion.519
  2229.0 16.5 fusion.236
  2267.4 17.5 multiply_add_fusion.41
  2284.9 19.4 fusion.524
  2310.1 17.5 multiply_add_fusion.40
  2327.6 19.2 fusion.526
  2352.6 19.2 multiply_add_fusion.39
  2371.8 16.4 fusion.528
  2394.1 16.2 add_bitcast_fusion.1
  2410.3 19.5 add_bitcast_fusion
  (477 shorter events, 679.8 us)
Async XLA Ops:
  7.2 92.5 %all-gather.13.cloned.1.call-start = ((), (), s32[]{:S(2)}) async-start(), calls=%async_computation.9 | async-start | bytes 11354112 | tf_op jit(solution)/shard_map/all_gather | solution.py:136
  9.1 151.4 %all-gather.15.cloned.1.call-start = ((), (), s32[]{:S(2)}) async-start(), calls=%async_computation.10 | async-start | bytes 1966080 | tf_op jit(solution)/shard_map/all_gather | solution.py:162
  45.4 65.2 %copy-start.62 = (f32[128,32]{0,1:T(8,128)}, f32[128,32]{0,1:T(8,128)S(1)}, u32[]{:S(2)}) copy-start(f32[128,32]{0,1:T(8,128)S(1)} %get-tuple-element.272) | copy-start | bytes 49156
  111.8 48.7 %copy-start.42 = (bf16[2,128,12,32]{1,3,2,0:T(8,128)(2,1)}, bf16[2,128,12,32]{1,3,2,0:T(8,128)(2,1)S(1)}, u32[]{:S(2)}) copy-start(bf16[2,128,12,32]{1,3,2,0:T(8,128)(2,1)S(1)} %get-tuple-element.258) | copy-start | bytes 589828
  111.8 48.8 %copy-start.44 = (bf16[2,128,12,32]{1,3,2,0:T(8,128)(2,1)}, bf16[2,128,12,32]{1,3,2,0:T(8,128)(2,1)S(1)}, u32[]{:S(2)}) copy-start(bf16[2,128,12,32]{1,3,2,0:T(8,128)(2,1)S(1)} %get-tuple-element.259) | copy-start | bytes 589828
  112.7 53.3 %all-gather.27.cloned.1.call-start = ((), (), s32[]{:S(2)}) async-start(), calls=%async_computation.21 | async-start | bytes 1966080 | tf_op jit(solution)/shard_map/all_gather | solution.py:163
  114.8 139.9 %all-gather.19.cloned.1.call-start = ((), (), s32[]{:S(2)}) async-start(), calls=%async_computation.12 | async-start | bytes 7077888 | tf_op jit(solution)/shard_map/all_gather | solution.py:142
  115.9 200.5 %all-gather.21.cloned.1.call-start = ((), (), s32[]{:S(2)}) async-start(), calls=%async_computation.13 | async-start | bytes 3538944 | tf_op jit(solution)/shard_map/all_gather | solution.py:143
  194.7 22.9 all-to-all-start
  199.2 180.2 %all-gather.17.cloned.1.call-start = ((), (), s32[]{:S(2)}) async-start(), calls=%async_computation.11 | async-start | bytes 3244032 | tf_op jit(solution)/shard_map/all_gather | solution.py:138
  217.6 44.7 %copy-start.9 = (bf16[4,256,768]{2,1,0:T(8,128)(2,1)}, bf16[4,256,768]{2,1,0:T(8,128)(2,1)S(1)}, u32[]{:S(2)}) copy-start(bf16[4,256,768]{2,1,0:T(8,128)(2,1)S(1)} %all-to-all-done) | copy-start | bytes 4718596
  217.6 98.8 %all-to-all-start.2 = ((bf16[4,256,768]{2,1,0:T(8,128)(2,1)}), bf16[4,256,768]{2,1,0:T(8,128)(2,1)S(1)}, u32[]{:S(2)}, u32[]{:S(2)}) async-start(bf16[4,256,768]{2,1,0:T(8,128)(2,1)} %get-tuple-element.270), calls=%async_computation.2 | async-start | bytes 3145728 | tf_op jit(solution)/shard_map/all_to_all | solution.py:292
  343.1 26.1 %all-to-all-start.3 = ((bf16[4,256,768]{2,1,0:T(8,128)(2,1)}), bf16[4,256,768]{2,1,0:T(8,128)(2,1)S(1)}, u32[]{:S(2)}, u32[]{:S(2)}) async-start(bf16[4,256,768]{2,1,0:T(8,128)(2,1)} %bitcast.44), calls=%async_computation.3 | async-start | bytes 3145728 | tf_op jit(solution)/shard_map/all_to_all | solution.py:312
  369.2 28.7 %all-to-all-start.1 = ((bf16[4,256,768]{2,1,0:T(8,128)(2,1)}), bf16[4,256,768]{2,1,0:T(8,128)(2,1)S(1)}, u32[]{:S(2)}, u32[]{:S(2)}) async-start(bf16[4,256,768]{2,1,0:T(8,128)(2,1)} %bitcast.543), calls=%async_computation.1 | async-start | bytes 3145728 | tf_op jit(solution)/shard_map/all_to_all | solution.py:260
  374.9 110.0 %reduce-scatter.9.cloned.1.call-start = ((), (), s32[]{:S(2)}) async-start(), calls=%async_computation.14 | async-start | bytes 7864320 | tf_op jit(solution)/shard_map/reduce_scatter | solution.py:374
  427.0 178.7 %reduce-scatter.15.cloned.1.call-start = ((), (), s32[]{:S(2)}) async-start(), calls=%async_computation.18 | async-start | bytes 6488064 | tf_op jit(solution)/shard_map/reduce_scatter | solution.py:393
  432.3 402.6 %reduce-scatter.11.cloned.1.call-start = ((), (), s32[]{:S(2)}) async-start(), calls=%async_computation.15 | async-start | bytes 22708224 | tf_op jit(solution)/shard_map/reduce_scatter | solution.py:391
  446.4 39.7 %copy-start.40 = (f32[2,128,12,64]{1,3,2,0:T(8,128)S(1)}, f32[2,128,12,64]{1,3,2,0:T(8,128)}, u32[]{:S(2)}) copy-start(f32[2,128,12,64]{1,3,2,0:T(8,128)} %fusion.330) | copy-start | bytes 2359300
  446.4 39.7 %copy-start.63 = (f32[128,32]{0,1:T(8,128)S(1)}, f32[128,32]{0,1:T(8,128)}, u32[]{:S(2)}) copy-start(f32[128,32]{0,1:T(8,128)} %copy-done.62) | copy-start | bytes 49156
  446.4 39.7 %copy-start.65 = (f32[128,32]{0,1:T(8,128)S(1)}, f32[128,32]{0,1:T(8,128)}, u32[]{:S(2)}) copy-start(f32[128,32]{0,1:T(8,128)} %get-tuple-element.273) | copy-start | bytes 49156
  503.3 905.5 %all-reduce.7.cloned.1.call-start = ((), (), s32[]{:S(2)}) async-start(), calls=%async_computation.22 | async-start | bytes 37748736 | tf_op jit(solution)/shard_map/psum | solution.py:449
  556.5 49.3 %copy-start.61 = (f32[64,768]{1,0:T(8,128)S(1)}, f32[64,768]{1,0:T(8,128)}, u32[]{:S(2)}) copy-start(f32[64,768]{1,0:T(8,128)} %param.40) | copy-start | bytes 589828
  556.5 278.4 %copy-start.57 = (f32[24,7168]{1,0:T(8,128)S(1)}, f32[24,7168]{1,0:T(8,128)}, u32[]{:S(2)}) copy-start(f32[24,7168]{1,0:T(8,128)} %param.36) | copy-start | bytes 2064388
  556.5 280.5 %copy-start.39 = (f32[1,256,768]{2,1,0:T(8,128)S(1)}, f32[1,256,768]{2,1,0:T(8,128)}, u32[]{:S(2)}) copy-start(f32[1,256,768]{2,1,0:T(8,128)} %param.43) | copy-start | bytes 2359300
  556.5 924.7 %all-gather.25.cloned.1.call-start = ((), (), s32[]{:S(2)}) async-start(), calls=%async_computation.19 | async-start | bytes 6488064 | tf_op jit(solution)/shard_map/all_gather | solution.py:414
  607.4 230.8 %copy-start.75 = (f32[768]{0:T(1024)S(1)}, f32[768]{0:T(1024)}, u32[]{:S(2)}) copy-start(f32[768]{0:T(1024)} %get-tuple-element.228) | copy-start | bytes 9220
  607.4 275.6 %copy-start.93 = (f32[24,4]{0,1:T(4,128)S(1)}, f32[24,4]{0,1:T(4,128)}, u32[]{:S(2)}) copy-start(f32[24,4]{0,1:T(4,128)} %param.38) | copy-start | bytes 1156
  607.4 1245.8 %all-gather.23.cloned.1.call-start = ((), (), s32[]{:S(2)}) async-start(), calls=%async_computation.16 | async-start | bytes 22708224 | tf_op jit(solution)/shard_map/all_gather | solution.py:412
  836.9 80.5 %copy-start.55 = (f32[256,768]{1,0:T(8,128)S(1)}, f32[256,768]{1,0:T(8,128)}, u32[]{:S(2)}) copy-start(f32[256,768]{1,0:T(8,128)} %get-tuple-element.225) | copy-start | bytes 2359300
  836.9 1595.1 %reduce-scatter.17.cloned.1.call-start = ((), (), s32[]{:S(2)}) async-start(), calls=%async_computation.20 | async-start | bytes 6488064 | tf_op jit(solution)/shard_map/reduce_scatter | solution.py:425
  883.1 33.9 %copy-start.90 = (f32[24,4]{0,1:T(4,128)}, f32[24,4]{0,1:T(4,128)S(1)}, u32[]{:S(2)}) copy-start(f32[24,4]{0,1:T(4,128)S(1)} %dynamic-slice_add_fusion.3) | copy-start | bytes 1156
  922.5 54.9 %copy-start.92 = (f32[24,4]{0,1:T(4,128)S(1)}, f32[24,4]{0,1:T(4,128)}, u32[]{:S(2)}) copy-start(f32[24,4]{0,1:T(4,128)} %param.37) | copy-start | bytes 1156
  922.5 55.6 %copy-start.95 = (f32[2,24]{1,0:T(2,128)S(1)}, f32[2,24]{1,0:T(2,128)}, u32[]{:S(2)}) copy-start(f32[2,24]{1,0:T(2,128)} %param.33) | copy-start | bytes 580
  922.5 55.6 %copy-start.96 = (f32[2,24]{1,0:T(2,128)S(1)}, f32[2,24]{1,0:T(2,128)}, u32[]{:S(2)}) copy-start(f32[2,24]{1,0:T(2,128)} %param.34) | copy-start | bytes 580
  922.5 56.2 %copy-start.5 = (f32[2,128,768]{2,1,0:T(8,128)S(1)}, f32[2,128,768]{2,1,0:T(8,128)}, u32[]{:S(2)}) copy-start(f32[2,128,768]{2,1,0:T(8,128)} %copy-done.3) | copy-start | bytes 2359300
  922.5 56.2 %copy-start.7 = (f32[256,768]{1,0:T(8,128)S(1)}, f32[256,768]{1,0:T(8,128)}, u32[]{:S(2)}) copy-start(f32[256,768]{1,0:T(8,128)} %copy-done.6) | copy-start | bytes 2359300
  922.5 56.2 %copy-start.34 = (bf16[2,128,768]{2,1,0:T(8,128)(2,1)S(1)}, bf16[2,128,768]{2,1,0:T(8,128)(2,1)}, u32[]{:S(2)}) copy-start(bf16[2,128,768]{2,1,0:T(8,128)(2,1)} %param.30) | copy-start | bytes 1179652
  922.5 56.2 %copy-start.56 = (f32[256,768]{1,0:T(8,128)S(1)}, f32[256,768]{1,0:T(8,128)}, u32[]{:S(2)}) copy-start(f32[256,768]{1,0:T(8,128)} %convolution_add_fusion.3) | copy-start | bytes 2359300
  922.5 56.2 %copy-start.74 = (f32[2,128]{1,0:T(2,128)S(1)}, f32[2,128]{1,0:T(2,128)}, u32[]{:S(2)}) copy-start(f32[2,128]{1,0:T(2,128)} %copy-done.72) | copy-start | bytes 3076
  922.5 56.2 %copy-start.82 = (f32[2,128]{1,0:T(2,128)S(1)}, f32[2,128]{1,0:T(2,128)}, u32[]{:S(2)}) copy-start(f32[2,128]{1,0:T(2,128)} %copy-done.81) | copy-start | bytes 3076
  1488.1 31.1 %slice-start.4 = ((s8[6291456]{0:T(1024)(128)(4,1)}), s8[2097152]{0:T(1024)(128)(4,1)S(1)}, s32[]{:S(2)}) async-start(s8[6291456]{0:T(1024)(128)(4,1)} %bitcast.516), calls=%async_computation.27 | async-start | bytes 4194304 | tf_op jit(solution)/shard_map/cond
  1493.9 25.3 %slice-start.5 = ((s8[6291456]{0:T(1024)(128)(4,1)}), s8[4194304]{0:T(1024)(128)(4,1)S(1)}, s32[]{:S(2)}) async-start(s8[6291456]{0:T(1024)(128)(4,1)} %bitcast.516), calls=%async_computation.28 | async-start | bytes 8388608 | tf_op jit(solution)/shard_map/cond
  1626.8 22.7 copy-start.22
  1737.6 696.1 %reduce-scatter.13.cloned.1.call-start = ((), (), s32[]{:S(2)}) async-start(), calls=%async_computation.17 | async-start | bytes 22708224 | tf_op jit(solution)/shard_map/reduce_scatter | solution.py:423
  1932.5 33.3 %slice-start.2 = ((s8[6291456]{0:T(1024)(128)(4,1)}), s8[2097152]{0:T(1024)(128)(4,1)S(1)}, s32[]{:S(2)}) async-start(s8[6291456]{0:T(1024)(128)(4,1)} %bitcast.514), calls=%async_computation.25 | async-start | bytes 4194304
  1940.1 25.7 %slice-start.3 = ((s8[6291456]{0:T(1024)(128)(4,1)}), s8[4194304]{0:T(1024)(128)(4,1)S(1)}, s32[]{:S(2)}) async-start(s8[6291456]{0:T(1024)(128)(4,1)} %bitcast.514), calls=%async_computation.26 | async-start | bytes 8388608
  2168.8 38.4 %slice-start.6 = ((s8[12582912]{0:T(1024)(128)(4,1)}), s8[4194304]{0:T(1024)(128)(4,1)S(1)}, s32[]{:S(2)}) async-start(s8[12582912]{0:T(1024)(128)(4,1)} %bitcast.520), calls=%async_computation.29 | async-start | bytes 8388608
  2168.8 38.4 %slice-start.7 = ((s8[12582912]{0:T(1024)(128)(4,1)}), s8[4194304]{0:T(1024)(128)(4,1)S(1)}, s32[]{:S(2)}) async-start(s8[12582912]{0:T(1024)(128)(4,1)} %bitcast.520), calls=%async_computation.30 | async-start | bytes 8388608
  (84 other events, 440.4 us)
Sparse Core Ops, SparseCore 0:
  11.5 88.1 all-gather.12
  112.8 19.0 all-gather.14
  134.0 19.9 all-gather.26
  156.6 98.0 all-gather.18
  257.3 59.1 all-gather.20
  319.1 60.1 all-gather.16
  427.2 57.6 reduce-scatter.8
  491.4 114.2 reduce-scatter.14
  612.2 222.6 reduce-scatter.10
  839.0 569.7 all-reduce.6
  1412.2 68.9 all-gather.24
  1484.6 137.6 all-gather.22
  1737.7 113.3 reduce-scatter.16
  1932.6 222.4 reduce-scatter.12
where the time goes:
time: 2450 us; the launch traced here: 2440 us
  matrix products  994 us (41%)
  waiting for transfers between devices  946 us (39%)
  blocking collectives  194 us (8%)
  other arithmetic  113 us (5%)
  local copies, waits for them, and re-layouts  101 us (4%)
  loops' own time  55.2 us (2%)
    psum x1, waiting for transfers between devices, per_device(): whole_gate_up, whole_edown = lax.psum((gate_term, down_term), 'dp')  428 us
    dot_general x20, matrix products, orthogonal(): jnp.dot(poly, current, precision=HIGHEST_PRECISION)  384 us
    dot_general x20, matrix products, orthogonal(): gram = jnp.dot(current, current.T, precision=HIGHEST_PRECISION)  353 us
    reduce_scatter x1, waiting for transfers between devices, per_device(): lax.psum_scatter(grad_dense, ('dp', 'fsdp'), scatter_dimension=0, tiled=T...  227 us
    dot_general x20, matrix products, orthogonal(): jnp.dot(gram, gram, precision=HIGHEST_PRECISION)  123 us
    unnamed x2, blocking collectives  95.2 us
    another operation x6, loops' own time, owned(): lax.cond(device_index == owners[number], orthogonal, jnp.zeros_like, matrix)  55.2 us
    all_gather x1, waiting for transfers between devices, per_device(): lax.all_gather(w_dense.astype(jnp.bfloat16), ('dp', 'fsdp'), axis=0, tile...  52.4 us
  transfers between devices with their start and end apart: 18, of which 11 were waited for; matrix products, arithmetic and copies ran while one was open for 47% of the time, Pallas kernels for 0%

commit v1 on v0

--- a/solution.py
+++ b/solution.py
@@ -1,8 +1,12 @@
+import functools
 import math
 
 import jax
 import jax.numpy as jnp
+import numpy as np
 from jax import lax
+from jax.experimental import pallas as pl
+from jax.experimental.pallas import tpu as pltpu
 from jax.sharding import PartitionSpec as P
 
 HEADS = 12
@@ -95,14 +99,16 @@
     if matrix.shape[0] > matrix.shape[1]:
         return orthogonal(matrix.T).T
     current = matrix / (jnp.sqrt(jnp.sum(matrix * matrix)) + 1e-07)
-    for sweep in range(NS_STEPS):
+
+    def sweep(_, current):
         gram = jnp.dot(current, current.T, precision=HIGHEST_PRECISION)
         poly = POLY_SECOND * gram + POLY_THIRD * jnp.dot(gram, gram, precision=HIGHEST_PRECISION)
-        current = POLY_FIRST * current + jnp.dot(poly, current, precision=HIGHEST_PRECISION)
-    return current
-
-
-def per_device(
+        return POLY_FIRST * current + jnp.dot(poly, current, precision=HIGHEST_PRECISION)
+
+    return lax.fori_loop(0, NS_STEPS, sweep, current)
+
+
+def general_plan(
     tokens,
     cotangent,
     lengths,
@@ -478,6 +484,1167 @@
     )
 
 
+DP = 8
+FS = 4
+AXES = ("dp", "fsdp")
+LANES = 128
+SEQUENCES = 2
+VMEM_BYTES = 60 * 2**20
+LINE = 4
+OWNERS = ((0, 3, 4, 7), (1, 2, 5, 6), (0, 3, 4, 7), (1, 2, 5, 6, 4))
+TALL_SLOTS = (3, 4)
+DOWN_COLUMN = 3
+
+
+def tn_dot(left, right):
+    return lax.dot_general(
+        left, right, (((0,), (0,)), ((), ())), preferred_element_type=jnp.float32
+    )
+
+
+def nt_dot(left, right):
+    return lax.dot_general(
+        left, right, (((1,), (1,)), ((), ())), preferred_element_type=jnp.float32
+    )
+
+
+def kernel_call(body, out_shape, flops, bytes_accessed, **options):
+    return pl.pallas_call(
+        body,
+        out_shape=out_shape,
+        compiler_params=pltpu.CompilerParams(vmem_limit_bytes=VMEM_BYTES),
+        cost_estimate=pl.CostEstimate(
+            flops=int(flops), bytes_accessed=int(bytes_accessed), transcendentals=0
+        ),
+        **options,
+    )
+
+
+def shape_of(shape, dtype=jnp.bfloat16):
+    return jax.ShapeDtypeStruct(shape, dtype)
+
+
+def whole_block(shape):
+    return pl.BlockSpec(shape, lambda *_: (0,) * len(shape))
+
+
+def after(value, *events):
+    return lax.optimization_barrier((value,) + events)[0]
+
+
+def fsdp_hop(value, step):
+    pairs = [(d * FS + f, d * FS + (f ^ step)) for d in range(DP) for f in range(FS)]
+    return lax.ppermute(value, AXES, pairs)
+
+
+def by_source(own, near, far, cross, index):
+    low_x, even = index < 2, index % 2 == 0
+    own_low, own_high = jnp.where(low_x, own, far), jnp.where(low_x, far, own)
+    near_low, near_high = jnp.where(low_x, near, cross), jnp.where(low_x, cross, near)
+    return [
+        jnp.where(even, own_low, near_low),
+        jnp.where(even, near_low, own_low),
+        jnp.where(even, own_high, near_high),
+        jnp.where(even, near_high, own_high),
+    ]
+
+
+def gather_fsdp(block, index):
+    far = fsdp_hop(block, 2)
+    near = fsdp_hop(block, 1)
+    cross = fsdp_hop(far, 1)
+    return by_source(block, near, far, cross, index)
+
+
+def exchange_fsdp(blocks, index):
+    pick = lambda step: lax.dynamic_index_in_dim(blocks, index ^ step, 0, keepdims=False)
+    got = [pick(0)] + [fsdp_hop(pick(step), step) for step in (1, 2, 3)]
+    return by_source(*got, index)
+
+
+class FsdpSum:
+    def __init__(self, keep, send, index):
+        self.place, self.keep = index // 2, keep
+        self.near = fsdp_hop(send, 1)
+
+    def cross(self):
+        both = self.keep.astype(jnp.float32) + self.near.astype(jnp.float32)
+        away = lax.dynamic_index_in_dim(both, 1 - self.place, 0, keepdims=False)
+        self.here = lax.dynamic_index_in_dim(both, self.place, 0, keepdims=False)
+        self.far = fsdp_hop(away.astype(self.keep.dtype), 2)
+        return self
+
+    def last(self):
+        return self.here + self.far.astype(jnp.float32)
+
+
+def by_core(blocks, index, *events):
+    if events:
+        blocks = after(blocks, *events)
+    pairs, core = blocks.reshape((2, 2) + blocks.shape[1:]), index % 2
+    return [lax.dynamic_index_in_dim(pairs, c, 1, keepdims=False) for c in (core, 1 - core)]
+
+
+def sum_everywhere(value):
+    for d_step, f_step in ((0, 1), (0, 2), (1, 0), (2, 0), (4, 0)):
+        pairs = [
+            (d * FS + f, (d ^ d_step) * FS + (f ^ f_step)) for d in range(DP) for f in range(FS)
+        ]
+        value = value + lax.ppermute(value, AXES, pairs)
+    return value
+
+
+def swap_halves(values, half_size):
+    width = values.shape[1]
+    lane = lax.broadcasted_iota(jnp.int32, values.shape, 1)
+    return jnp.where(
+        lane % (2 * half_size) < half_size,
+        -pltpu.roll(values, width - half_size, 1),
+        pltpu.roll(values, half_size, 1),
+    )
+
+
+def attention_body(
+    lengths_ref, x_ref, gain_ref, w_ref, cos_ref, sin_ref, normed_ref, qkv_ref, prob_ref, att_ref
+):
+    head_count, row_len = prob_ref.shape[1], prob_ref.shape[2]
+    wide = w_ref.shape[1] // 3
+    head_size = wide // head_count
+    x = x_ref[0].astype(jnp.float32)
+    inverse = lax.rsqrt(jnp.mean(x * x, axis=-1, keepdims=True) + NORM_EPSILON)
+    normed = (x * inverse * gain_ref[...]).astype(jnp.bfloat16)
+    normed_ref[...] = normed.T
+    projected = jnp.dot(normed, w_ref[...], preferred_element_type=jnp.float32)
+    both = projected[:, : 2 * wide]
+    both = both * cos_ref[...] + swap_halves(both, head_size // 2) * sin_ref[...]
+    both = both.astype(jnp.bfloat16)
+    values = projected[:, 2 * wide :].astype(jnp.bfloat16)
+    qkv_ref[0, :, : 2 * wide] = both
+    qkv_ref[0, :, 2 * wide :] = values
+    length = lengths_ref[pl.program_id(0)]
+    row = lax.broadcasted_iota(jnp.int32, (row_len, row_len), 0)
+    column = lax.broadcasted_iota(jnp.int32, (row_len, row_len), 1)
+    allowed = (column <= row) & (column < length)
+    parts = []
+    for head in range(head_count):
+        span = slice(head * head_size, (head + 1) * head_size)
+        scores = nt_dot(both[:, span], both[:, wide:][:, span]) * 0.125
+        scores = jnp.where(allowed, scores, MASK_VALUE)
+        weights = jnp.exp(scores - jnp.max(scores, axis=-1, keepdims=True))
+        share = 1.0 / jnp.sum(weights, axis=-1, keepdims=True)
+        probs = (weights * share).astype(jnp.bfloat16)
+        prob_ref[0, head] = probs
+        parts.append(jnp.dot(probs, values[:, span], preferred_element_type=jnp.float32))
+    att_ref[0] = jnp.concatenate(parts, axis=1).astype(jnp.bfloat16)
+
+
+def attention_forward(x, gain, weight, cosine, sine, lengths):
+    rows, row_len, width = x.shape
+    columns = weight.shape[1]
+    heads = columns // 3 // (width // HEADS)
+    return kernel_call(
+        attention_body,
+        (
+            shape_of((width, rows * row_len)),
+            shape_of((rows, row_len, columns)),
+            shape_of((rows, heads, row_len, row_len)),
+            shape_of((rows, row_len, columns // 3)),
+        ),
+        6e9,
+        12e6,
+        grid=(rows,),
+        in_specs=[
+            pl.BlockSpec(memory_space=pltpu.SMEM),
+            pl.BlockSpec((1, row_len, width), lambda r: (r, 0, 0)),
+            whole_block(gain.shape),
+            whole_block(weight.shape),
+            whole_block(cosine.shape),
+            whole_block(sine.shape),
+        ],
+        out_specs=(
+            pl.BlockSpec((width, row_len), lambda r: (0, r)),
+            pl.BlockSpec((1, row_len, columns), lambda r: (r, 0, 0)),
+            pl.BlockSpec((1, heads, row_len, row_len), lambda r: (r, 0, 0, 0)),
+            pl.BlockSpec((1, row_len, columns // 3), lambda r: (r, 0, 0)),
+        ),
+        name="attention_forward",
+    )(lengths, x, gain, weight, cosine, sine)
+
+
+def attention_back_body(
+    normed_ref, qkv_ref, prob_ref, d_att_ref, w_ref, cos_ref, sin_ref, grad_ref, back_ref, total
+):
+    head_count = prob_ref.shape[1]
+    wide = w_ref.shape[1] // 3
+    head_size = wide // head_count
+    qkv = qkv_ref[0]
+    d_att = d_att_ref[0]
+    grads = ([], [], [])
+    for head in range(head_count):
+        span = slice(head * head_size, (head + 1) * head_size)
+        query, key, value = (qkv[:, i * wide : (i + 1) * wide][:, span] for i in range(3))
+        probs = prob_ref[0, head]
+        weights = probs.astype(jnp.float32)
+        slopes = nt_dot(d_att[:, span], value)
+        delta = jnp.sum(weights * slopes, axis=-1, keepdims=True)
+        d_scores = (weights * (slopes - delta)).astype(jnp.bfloat16)
+        grads[0].append(0.125 * jnp.dot(d_scores, key, preferred_element_type=jnp.float32))
+        grads[1].append(0.125 * tn_dot(d_scores, query))
+        grads[2].append(tn_dot(probs, d_att[:, span]))
+    both = jnp.concatenate(grads[0] + grads[1], axis=1)
+    both = both * cos_ref[...] - swap_halves(both, head_size // 2) * sin_ref[...]
+    d_qkv = jnp.concatenate([both] + grads[2], axis=1).astype(jnp.bfloat16)
+    grad = jnp.dot(normed_ref[...], d_qkv, preferred_element_type=jnp.float32)
+
+    @pl.when(pl.program_id(0) == 0)
+    def _():
+        total[...] = grad
+
+    @pl.when(pl.program_id(0) > 0)
+    def _():
+        total[...] += grad
+
+    grad_ref[...] = total[...].astype(jnp.bfloat16)
+    back_ref[0] = nt_dot(d_qkv, w_ref[...]).astype(jnp.bfloat16)
+
+
+def attention_backward(normed, qkv, probs, d_att, weight, cosine, sine):
+    rows, row_len, columns = qkv.shape
+    width, heads = weight.shape[0], probs.shape[1]
+    return kernel_call(
+        attention_back_body,
+        (shape_of((width, columns)), shape_of((rows, row_len, width))),
+        8e9,
+        12e6,
+        grid=(rows,),
+        in_specs=[
+            pl.BlockSpec((width, row_len), lambda r: (0, r)),
+            pl.BlockSpec((1, row_len, columns), lambda r: (r, 0, 0)),
+            pl.BlockSpec((1, heads, row_len, row_len), lambda r: (r, 0, 0, 0)),
+            pl.BlockSpec((1, row_len, columns // 3), lambda r: (r, 0, 0)),
+            whole_block(weight.shape),
+            whole_block(cosine.shape),
+            whole_block(sine.shape),
+        ],
+        out_specs=(
+            whole_block((width, columns)),
+            pl.BlockSpec((1, row_len, width), lambda r: (r, 0, 0)),
+        ),
+        scratch_shapes=[pltpu.VMEM((width, columns), jnp.float32)],
+        name="attention_backward",
+    )(normed, qkv, probs, d_att, weight, cosine, sine)
+
+
+def middle_body(
+    att_ref, x_ref, routes_ref, wout_ref, router_ref, gain_ref, mid_ref, normed_ref, turned_ref, gates_ref
+):
+    branch = jnp.dot(att_ref[...], wout_ref[...], preferred_element_type=jnp.float32)
+    mid = x_ref[...].astype(jnp.float32) + branch
+    inverse = lax.rsqrt(jnp.mean(mid * mid, axis=-1, keepdims=True) + NORM_EPSILON)
+    normed = (mid * inverse * gain_ref[...]).astype(jnp.bfloat16)
+    logits = jnp.dot(normed, router_ref[...], preferred_element_type=jnp.float32)
+    lane = lax.broadcasted_iota(jnp.int32, logits.shape, 1)
+    first, second = lane == routes_ref[:, 0:1], lane == routes_ref[:, 1:2]
+    one = jnp.sum(jnp.where(first, logits, 0.0), axis=-1, keepdims=True)
+    two = jnp.sum(jnp.where(second, logits, 0.0), axis=-1, keepdims=True)
+    top = jnp.maximum(one, two)
+    one, two = jnp.exp(one - top), jnp.exp(two - top)
+    share = 1.0 / (one + two)
+    mid_ref[...] = mid
+    normed_ref[...] = normed
+    turned_ref[...] = normed.T
+    gates_ref[...] = jnp.where(first, one * share, 0.0) + jnp.where(second, two * share, 0.0)
+
+
+def middle_forward(attended, x, routes, wout, router, gain):
+    count, width = x.shape
+    tile = min(256, count)
+    rows = lambda i: (i, 0)
+    return kernel_call(
+        middle_body,
+        (
+            shape_of((count, width), jnp.float32),
+            shape_of((count, width)),
+            shape_of((width, count)),
+            shape_of((count, LANES), jnp.float32),
+        ),
+        2 * count * width * width,
+        12e6,
+        grid=(count // tile,),
+        in_specs=[
+            pl.BlockSpec((tile, width), rows),
+            pl.BlockSpec((tile, width), rows),
+            pl.BlockSpec((tile, routes.shape[1]), rows),
+            whole_block(wout.shape),
+            whole_block(router.shape),
+            whole_block(gain.shape),
+        ],
+        out_specs=(
+            pl.BlockSpec((tile, width), rows),
+            pl.BlockSpec((tile, width), rows),
+            pl.BlockSpec((width, tile), lambda i: (0, i)),
+            pl.BlockSpec((tile, LANES), rows),
+        ),
+        name="middle_forward",
+    )(attended, x, routes, wout, router, gain)
+
+
+def middle_back_body(
+    index_ref, mid_ref, d_out_ref, d_sum_ref, gates_ref, routes_ref, att_ref, normed_ref, wout_ref, router_ref,
+    gain_ref, d_mid_ref, grad_wout_ref, grad_router_ref, grad_gain_ref, *d_att_refs,
+):
+    width = mid_ref.shape[1]
+    gates = gates_ref[...]
+    lane = lax.broadcasted_iota(jnp.int32, gates.shape, 1)
+    half = LANES // 2
+    first, second = routes_ref[:, 0:1], routes_ref[:, 1:2]
+    slopes = d_sum_ref[:, width:]
+
+    def pick(table, place):
+        return jnp.sum(jnp.where(lane == place, table, 0.0), axis=-1, keepdims=True)
+
+    gate_one, gate_two = pick(gates, first), pick(gates, second)
+    slope_one = pick(slopes, first) + pick(slopes, first + half)
+    slope_two = pick(slopes, second) + pick(slopes, second + half)
+    common = gate_one * slope_one + gate_two * slope_two
+    d_logits = jnp.where(lane == first, gate_one * (slope_one - common), 0.0)
+    d_logits = d_logits + jnp.where(lane == second, gate_two * (slope_two - common), 0.0)
+    d_logits = d_logits.astype(jnp.bfloat16)
+    grad_router_ref[...] = tn_dot(d_logits, normed_ref[...])
+    d_normed = d_sum_ref[:, :width] + nt_dot(d_logits, router_ref[...])
+    mid = mid_ref[...]
+    inverse = lax.rsqrt(jnp.mean(mid * mid, axis=-1, keepdims=True) + NORM_EPSILON)
+    scaled = mid * inverse
+    grad_gain_ref[...] = jnp.sum(d_normed * scaled, axis=0, keepdims=True)
+    through = d_normed * gain_ref[...]
+    d_norm = inverse * (through - scaled * jnp.mean(through * scaled, axis=-1, keepdims=True))
+    d_mid = d_out_ref[...].astype(jnp.float32) + d_norm
+    d_mid_ref[...] = d_mid
+    d_branch = d_mid.astype(jnp.bfloat16)
+    grad_wout_ref[...] = tn_dot(att_ref[...], d_branch).astype(jnp.bfloat16)
+    d_att = nt_dot(d_branch, wout_ref[...]).astype(jnp.bfloat16)
+    quarter = width // FS
+    for f in range(FS):
+        for step, d_att_ref in enumerate(d_att_refs):
+
+            @pl.when(index_ref[0] == f ^ step)
+            def _():
+                d_att_ref[...] = d_att[:, f * quarter : (f + 1) * quarter]
+
+
+def middle_backward(index, *operands):
+    count, width = operands[0].shape
+    vmem = pl.BlockSpec(memory_space=pltpu.VMEM)
+    return kernel_call(
+        middle_back_body,
+        [
+            shape_of((count, width), jnp.float32),
+            shape_of((width, width)),
+            shape_of((LANES, width), jnp.float32),
+            shape_of((1, width), jnp.float32),
+        ]
+        + [shape_of((count, width // FS))] * FS,
+        4 * count * width * width,
+        8e6,
+        in_specs=[pl.BlockSpec(memory_space=pltpu.SMEM)] + [vmem] * len(operands),
+        name="middle_backward",
+    )(index, *operands)
+
+
+def branch_step(normed_ref, turned_ref, d_out_ref, gate_column, weights, grads):
+    both_weight, down_weight = weights
+    tile = down_weight.shape[0]
+    normed, d_out = normed_ref[...], d_out_ref[...]
+    both = jnp.dot(normed, both_weight, preferred_element_type=jnp.float32)
+    gate, up = both[:, :tile], both[:, tile:]
+    slope = nt_dot(d_out, down_weight)
+    logistic = 1.0 / (1.0 + jnp.exp(-gate))
+    silu = gate * logistic
+    act = silu * up
+    d_gate = None
+    if gate_column is not None:
+        d_gate = jnp.sum(act * slope, axis=-1, keepdims=True)
+        act = act * gate_column
+        slope = slope * gate_column
+    act = act.astype(jnp.bfloat16)
+    d_both = jnp.concatenate(
+        [
+            (slope * up * (logistic * (1.0 + gate * (1.0 - logistic)))).astype(jnp.bfloat16),
+            (slope * silu).astype(jnp.bfloat16),
+        ],
+        axis=1,
+    )
+    grads[0][...] = jnp.dot(
+        turned_ref[...], d_both, preferred_element_type=jnp.float32
+    ).astype(jnp.bfloat16)
+    grads[1][...] = tn_dot(act, d_out).astype(jnp.bfloat16)
+    out = jnp.dot(act, down_weight, preferred_element_type=jnp.float32)
+    return out, nt_dot(d_both, both_weight), d_gate
+
+
+def add_parts(step, totals, parts, first):
+    @pl.when(step == 0)
+    def _():
+        for i, part in enumerate(parts):
+            totals[i][...] = part if first is None else first[i][...] + part
+
+    @pl.when(step > 0)
+    def _():
+        for i, part in enumerate(parts):
+            totals[i][...] += part
+
+
+def shared_body(
+    normed_ref, turned_ref, d_out_ref, gate_ref, up_ref, down_ref, out_ref, back_ref, pair_ref,
+    grad_down_ref,
+):
+    out, back, _ = branch_step(
+        normed_ref,
+        turned_ref,
+        d_out_ref,
+        None,
+        (jnp.concatenate([gate_ref[...], up_ref[...]], axis=1), down_ref[...]),
+        (pair_ref, grad_down_ref),
+    )
+    add_parts(pl.program_id(0), (out_ref, back_ref), (out, back), None)
+
+
+def expert_body(
+    place_ref, normed_ref, turned_ref, d_out_ref, gates_ref, first_out_ref, first_back_ref, gate_ref,
+    up_ref, down_ref, out_keep, out_send, back_keep, back_send, pair_ref, down_keep, down_send,
+    out_total, back_total, slope_total, grad_down,
+):
+    step = pl.program_id(0)
+    expert, side = place_ref[0], place_ref[1]
+    out, back, d_gate = branch_step(
+        normed_ref,
+        turned_ref,
+        d_out_ref,
+        gates_ref[...],
+        (jnp.concatenate([gate_ref[...], up_ref[...]], axis=1), down_ref[...]),
+        (pair_ref, grad_down),
+    )
+    half = grad_down.shape[0] // 2
+    for mine in range(2):
+
+        @pl.when(side == mine)
+        def _():
+            down_keep[...] = grad_down[mine * half : (mine + 1) * half, :]
+            down_send[...] = grad_down[(1 - mine) * half : (2 - mine) * half, :]
+
+    add_parts(step, (out_total, back_total), (out, back), (first_out_ref, first_back_ref))
+    add_parts(step, (slope_total,), (d_gate,), None)
+
+    @pl.when(step == pl.num_programs(0) - 1)
+    def _():
+        width = out_total.shape[1]
+        block = out_keep.shape[1]
+        local = block // SEQUENCES
+        slopes = slope_total[...]
+        high = slopes.astype(jnp.bfloat16).astype(jnp.float32)
+        lane = lax.broadcasted_iota(jnp.int32, (slopes.shape[0], LANES), 1)
+        table = jnp.where(lane == expert, high, 0.0)
+        table = jnp.where(lane == expert + LANES // 2, slopes - high, table).astype(jnp.bfloat16)
+        for f in range(FS):
+            x, core = divmod(f, 2)
+            for r in range(SEQUENCES):
+                start = (r * FS + f) * local
+                here, there = slice(start, start + local), slice(r * local, (r + 1) * local)
+
+                def write(out_ref, back_ref):
+                    out_ref[x, there, :] = out_total[here, :].astype(jnp.bfloat16)
+                    back_ref[x, there, :width] = back_total[here, :].astype(jnp.bfloat16)
+                    back_ref[x, there, width:] = table[here, :]
+
+                pl.when(expert % 2 == core)(functools.partial(write, out_keep, back_keep))
+                pl.when(expert % 2 != core)(functools.partial(write, out_send, back_send))
+
+
+def once(shape):
+    return pl.BlockSpec(shape, lambda *_: (0,) * len(shape), pipeline_mode=pl.Buffered(1))
+
+
+def shared_branch(normed, turned, d_out, both, down, tile):
+    count, width = normed.shape
+    hidden = down.shape[0]
+    tiles = hidden // tile
+    outs = [
+        shape_of((count, width), jnp.float32),
+        shape_of((count, width), jnp.float32),
+        shape_of((width, 2 * hidden)),
+        shape_of((hidden, width)),
+    ]
+    return kernel_call(
+        shared_body,
+        outs,
+        18 * count * width * hidden,
+        12 * width * hidden + 12 * count * width,
+        grid=(tiles,),
+        in_specs=[once(normed.shape), once(turned.shape), once(d_out.shape)]
+        + [
+            pl.BlockSpec((width, tile), lambda j: (0, j)),
+            pl.BlockSpec((width, tile), lambda j: (0, tiles + j)),
+            pl.BlockSpec((tile, width), lambda j: (j, 0)),
+        ],
+        out_specs=[once(out.shape) for out in outs[:2]]
+        + [
+            pl.BlockSpec((width, 2 * tile), lambda j: (0, j)),
+            pl.BlockSpec((tile, width), lambda j: (j, 0)),
+        ],
+        name="shared_branch",
+    )(normed, turned, d_out, both, both, down)
+
+
+def expert_branch(place, normed, turned, d_out, gates, first_out, first_back, gate_up, down, tile):
+    count, width = normed.shape
+    hidden = down.shape[0]
+    operands = [normed, turned, d_out, gates, first_out, first_back]
+    split = lambda columns: [shape_of((2, count // FS, columns))] * 2
+    outs = split(width) + split(width + LANES)
+    halves = shape_of((hidden // tile, tile // 2, width))
+    half_spec = pl.BlockSpec((None, tile // 2, width), lambda j: (j, 0, 0))
+    return kernel_call(
+        expert_body,
+        outs + [shape_of((width, 2 * hidden)), halves, halves],
+        18 * count * width * hidden,
+        12 * width * hidden + 16 * count * width,
+        grid=(hidden // tile,),
+        in_specs=[pl.BlockSpec(memory_space=pltpu.SMEM)]
+        + [once(array.shape) for array in operands]
+        + [
+            pl.BlockSpec((None, width, tile), lambda j: (0, 0, j)),
+            pl.BlockSpec((None, width, tile), lambda j: (1, 0, j)),
+            pl.BlockSpec((tile, width), lambda j: (j, 0)),
+        ],
+        out_specs=[once(out.shape) for out in outs]
+        + [pl.BlockSpec((width, 2 * tile), lambda j: (0, j)), half_spec, half_spec],
+        scratch_shapes=[
+            pltpu.VMEM((count, width), jnp.float32),
+            pltpu.VMEM((count, width), jnp.float32),
+            pltpu.VMEM((count, 1), jnp.float32),
+            pltpu.VMEM((tile, width), jnp.bfloat16),
+        ],
+        name="expert_branch",
+    )(place, *operands, gate_up, gate_up, down)
+
+
+def orthogonal_body(info_ref, *refs):
+    shards, results = refs[:DP], refs[DP : 2 * DP]
+    current, gram, poly = refs[2 * DP :]
+    size, length = current.shape
+    kind, place = info_ref[0], info_ref[1]
+    rows = shards[0].shape[0]
+    columns = 2 * LANES
+    tile = 256
+    tiles = size // tile
+    chunks = length // tile
+
+    def spot(k, extent):
+        return pl.multiple_of(lax.rem(place + k, DP) * extent, extent)
+
+    def folds(k):
+        for j in range(size // rows):
+            yield (
+                (slice(j * rows, (j + 1) * rows), pl.ds(spot(k, columns), columns)),
+                (slice(None), slice(j * columns, (j + 1) * columns)),
+            )
+
+    @pl.when(kind == 1)
+    def _():
+        for k in range(DP):
+            current[pl.ds(spot(k, rows), rows), :] = shards[k][...]
+
+    @pl.when(kind == 2)
+    def _():
+        current[:, DP * columns :] = jnp.zeros((size, length - DP * columns), jnp.bfloat16)
+        for k in range(DP):
+            for there, here in folds(k):
+                current[there] = shards[k][here]
+
+    @pl.when(kind > 0)
+    def _():
+        def square(c, total):
+            part = current[:, pl.ds(pl.multiple_of(c * tile, tile), tile)].astype(jnp.float32)
+            return total + jnp.sum(part * part, axis=0, keepdims=True)
+
+        squares = lax.fori_loop(0, chunks, square, jnp.zeros((1, tile), jnp.float32))
+        scale = 1.0 / (jnp.sqrt(jnp.sum(squares, axis=1, keepdims=True)) + 1e-07)
+
+        def scale_chunk(c, carry):
+            span = pl.ds(pl.multiple_of(c * tile, tile), tile)
+            part = current[:, span].astype(jnp.float32)
+            current[:, span] = (part * scale).astype(jnp.bfloat16)
+            return carry
+
+        lax.fori_loop(0, chunks, scale_chunk, 0)
+
+        def sweep(_, carry):
+            for i in range(tiles):
+                block = nt_dot(current[i * tile : (i + 1) * tile, :], current[i * tile :, :])
+                gram[i * tile : (i + 1) * tile, i * tile :] = block.astype(jnp.bfloat16)
+                poly[i * tile : (i + 1) * tile, i * tile :] = POLY_SECOND * block
+            for i in range(tiles):
+                for j in range(i):
+                    gram[i * tile : (i + 1) * tile, j * tile : (j + 1) * tile] = gram[
+                        j * tile : (j + 1) * tile, i * tile : (i + 1) * tile
+                    ].T
+            for i in range(tiles):
+                block = jnp.dot(
+                    gram[i * tile : (i + 1) * tile, :],
+                    gram[:, i * tile :],
+                    preferred_element_type=jnp.float32,
+                )
+                poly[i * tile : (i + 1) * tile, i * tile :] += POLY_THIRD * block
+            for i in range(tiles):
+                gram[i * tile : (i + 1) * tile, i * tile :] = poly[
+                    i * tile : (i + 1) * tile, i * tile :
+                ].astype(jnp.bfloat16)
+            for i in range(tiles):
+                for j in range(i):
+                    gram[i * tile : (i + 1) * tile, j * tile : (j + 1) * tile] = gram[
+                        j * tile : (j + 1) * tile, i * tile : (i + 1) * tile
+                    ].T
+
+            def update(c, carry):
+                span = pl.ds(pl.multiple_of(c * tile, tile), tile)
+                part = current[:, span]
+                fresh = POLY_FIRST * part.astype(jnp.float32) + jnp.dot(
+                    gram[...], part, preferred_element_type=jnp.float32
+                )
+                current[:, span] = fresh.astype(jnp.bfloat16)
+                return carry
+
+            return lax.fori_loop(0, chunks, update, carry)
+
+        lax.fori_loop(0, NS_STEPS, sweep, 0)
+
+    @pl.when(kind == 1)
+    def _():
+        for k in range(DP):
+            results[k][...] = current[pl.ds(spot(k, rows), rows), :]
+
+    @pl.when(kind == 2)
+    def _():
+        for k in range(DP):
+            for there, here in folds(k):
+                results[k][here] = current[there]
+
+
+def orthogonal_shards(info, shards, size):
+    rows, length = shards[0].shape
+    vmem = pl.BlockSpec(memory_space=pltpu.VMEM)
+    return kernel_call(
+        orthogonal_body,
+        [shape_of((rows, length))] * DP,
+        26e9,
+        8e6,
+        in_specs=[pl.BlockSpec(memory_space=pltpu.SMEM)] + [vmem] * DP,
+        out_specs=[vmem] * DP,
+        scratch_shapes=[
+            pltpu.VMEM((size, length), jnp.bfloat16),
+            pltpu.VMEM((size, size), jnp.bfloat16),
+            pltpu.VMEM((size, size), jnp.float32),
+        ],
+        name="orthogonal_shards",
+    )(info, *shards)
+
+
+def fold_tall(block, rows, length):
+    columns, size = block.shape
+    block = block.T.reshape(size // rows, rows, columns).transpose(1, 0, 2).reshape(rows, -1)
+    return jnp.pad(block, ((0, 0), (0, length - block.shape[1])))
+
+
+def unfold_tall(block, columns):
+    rows = block.shape[0]
+    size = rows * DP
+    block = block[:, : size // rows * columns].reshape(rows, size // rows, columns)
+    return block.transpose(1, 0, 2).reshape(size, columns).T
+
+
+def orthogonal_router_body(matrix_ref, out_ref):
+    current = matrix_ref[...]
+    dot = functools.partial(
+        lax.dot_general, precision=HIGHEST_PRECISION, preferred_element_type=jnp.float32
+    )
+    square = jnp.sum(jnp.sum(current * current, axis=1, keepdims=True), axis=0, keepdims=True)
+    current = current / (jnp.sqrt(square) + 1e-07)
+    for _ in range(NS_STEPS):
+        gram = dot(current, current, (((1,), (1,)), ((), ())))
+        poly = POLY_SECOND * gram + POLY_THIRD * dot(gram, gram, (((1,), (0,)), ((), ())))
+        current = POLY_FIRST * current + dot(poly, current, (((1,), (0,)), ((), ())))
+    out_ref[...] = current
+
+
+def orthogonal_router(matrix):
+    return kernel_call(
+        orthogonal_router_body, shape_of(matrix.shape, jnp.float32), 2e9, 1e6, name="orthogonal_router"
+    )(matrix)
+
+
+def slot_table(owners):
+    table = np.zeros((FS, DP), np.int32)
+    for f, column in enumerate(owners):
+        for slot, d in enumerate(column):
+            table[f, d] = slot
+    return table
+
+
+def owner_pairs(owners, step, back):
+    pairs = []
+    for f, column in enumerate(owners):
+        for d in column:
+            other = (d + step) % DP
+            pair = (other * FS + f, d * FS + f)
+            pairs.append(pair[::-1] if back else pair)
+    return pairs
+
+
+def to_owners(stack, owners, dp_index, index):
+    table = jnp.asarray(slot_table(owners))[index]
+    got = []
+    for step in range(DP):
+        slot = table[lax.rem(dp_index - step + DP, DP)]
+        block = lax.dynamic_index_in_dim(stack, slot, 0, keepdims=False)
+        got.append(
+            block if step == 0 else lax.ppermute(block, AXES, owner_pairs(owners, step, False))
+        )
+    return got
+
+
+def from_owners(blocks, owners, dp_index, index):
+    got = jnp.stack(
+        [
+            block if step == 0 else lax.ppermute(block, AXES, owner_pairs(owners, step, True))
+            for step, block in enumerate(blocks)
+        ]
+    )
+    count = max(len(column) for column in owners)
+    table = np.array([list(column) + [0] * (count - len(column)) for column in owners], np.int32)
+    places = jnp.asarray(table)[index]
+    return [
+        lax.dynamic_index_in_dim(got, lax.rem(dp_index - places[slot] + DP, DP), 0, keepdims=False)
+        for slot in range(count)
+    ]
+
+
+def line_hop(value, step):
+    pairs = [
+        ((z * 2 + y) * FS + f, ((z + step) % LINE * 2 + y) * FS + f)
+        for z in range(LINE)
+        for y in range(2)
+        for f in range(FS)
+    ]
+    return lax.ppermute(value, AXES, pairs)
+
+
+def pair_hop(value):
+    pairs = [(d * FS + f, (d ^ 1) * FS + f) for d in range(DP) for f in range(FS)]
+    return lax.ppermute(value, AXES, pairs)
+
+
+def place_body(places_ref, *refs):
+    out_ref = refs[-1]
+    rows = refs[0].shape[0]
+    other_ref = refs[-2]
+    for i, ref in enumerate(refs[:-2]):
+        out_ref[pl.ds(pl.multiple_of(places_ref[i] * rows, rows), rows), :] = ref[...]
+        start = pl.multiple_of(places_ref[LINE + i] * rows, rows)
+        out_ref[pl.ds(start, rows), :] = other_ref[i]
+
+
+class Gather:
+    def __init__(self, block, place):
+        _, self.side, self.level = place
+        self.blocks = [block] + [line_hop(block, step) for step in range(1, LINE)]
+
+    def cross(self, *events):
+        self.stack = jnp.stack(self.blocks)
+        if events:
+            self.stack = after(self.stack, *events)
+        self.other = pair_hop(self.stack)
+        return self.other
+
+    def last(self):
+        levels = lax.rem(self.level + LINE - jnp.arange(LINE), LINE)
+        places = jnp.concatenate([levels * 2 + self.side, levels * 2 + 1 - self.side])
+        rows, columns = self.blocks[0].shape
+        vmem = pl.BlockSpec(memory_space=pltpu.VMEM)
+        return kernel_call(
+            place_body,
+            shape_of((DP * rows, columns), self.stack.dtype),
+            0,
+            4 * DP * rows * columns,
+            in_specs=[pl.BlockSpec(memory_space=pltpu.SMEM)] + [vmem] * (LINE + 1),
+            out_specs=vmem,
+            name="place_rows",
+        )(places.astype(jnp.int32), *self.blocks, self.other)
+
+
+class Reduce:
+    def __init__(self, grads, place):
+        _, self.side, self.level = place
+        self.grads = grads
+
+    def pick(self, array, i, axis=0):
+        return lax.dynamic_index_in_dim(array, i, axis, keepdims=False)
+
+    def cross(self, *events):
+        rows, columns = self.grads.shape
+        grads = self.grads.reshape(LINE, 2, rows // DP, columns)
+        if events:
+            grads = after(grads, *events)
+        self.mine = self.pick(grads, self.side, 1)
+        self.sent = self.pick(grads, 1 - self.side, 1)
+        self.got = pair_hop(self.sent)
+        return self.got
+
+    def along(self, *events):
+        got = after(self.got, *events) if events else self.got
+        mine = self.mine
+        both = (mine.astype(jnp.float32) + got.astype(jnp.float32)).astype(mine.dtype)
+        self.both = both
+        at = lambda step: self.pick(both, lax.rem(self.level + step, LINE))
+        self.parts = [at(0)] + [line_hop(at(step), step) for step in range(1, LINE)]
+        return self.parts[1]
+
+    def last(self):
+        return sum(part.astype(jnp.float32) for part in self.parts)
+
+
+def split_plan(
+    tokens,
+    cotangent,
+    lengths,
+    routes,
+    gains,
+    gain_moms,
+    w_dense,
+    mom_dense,
+    w_router,
+    mom_router,
+    w_down,
+    mom_down,
+    e_gate_up,
+    e_mom_gate_up,
+    e_down,
+    e_mom_down,
+):
+    index, dp_index = lax.axis_index("fsdp"), lax.axis_index("dp")
+    device_index = dp_index * FS + index
+    rows, local_len, width = tokens.shape
+    row_len = local_len * FS
+    count = rows * row_len
+    experts = w_router.shape[1]
+    head_size = width // HEADS
+    quarter = width // FS
+    block_rows = w_dense.shape[0]
+    down_rows = w_down.shape[0]
+    ff_shared = down_rows * DP * FS
+    ff_part = down_rows * DP
+    bf16 = jnp.bfloat16
+
+    def by_columns(matrix):
+        qkv_parts = [
+            matrix[:, i * width : (i + 1) * width].reshape(block_rows, FS, quarter)
+            for i in range(3)
+        ]
+        shared_parts = [
+            matrix[:, 4 * width + i * ff_shared : 4 * width + (i + 1) * ff_shared]
+            .reshape(block_rows, DP, FS, down_rows)
+            .transpose(0, 2, 1, 3)
+            .reshape(block_rows, FS, ff_part)
+            for i in range(2)
+        ]
+        return jnp.concatenate(qkv_parts + shared_parts, axis=2).transpose(1, 0, 2)
+
+    dense = w_dense.astype(bf16)
+    own_columns = by_columns(dense)
+    qkv_columns = own_columns[..., : 3 * quarter]
+    common = jnp.concatenate(
+        [
+            w_router.astype(bf16),
+            gains.astype(bf16).T,
+            jnp.zeros((block_rows, LANES - experts - 2), bf16),
+        ],
+        axis=1,
+    )
+    spread = lambda array: jnp.broadcast_to(array, (FS,) + array.shape)
+    place = (index, dp_index % 2, dp_index // 2)
+    gate_up_copy = lax.all_gather(e_gate_up[0].astype(bf16), "dp", axis=1, tiled=True)
+    edown_copy = lax.all_gather(e_down[0].astype(bf16), "dp", axis=0, tiled=True)
+    message = jnp.concatenate([qkv_columns, spread(common)], axis=2)
+    message = jnp.concatenate(exchange_fsdp(message, index), axis=0)
+    folds = message.shape[0]
+    fold_down, fold_out = down_rows * width // folds, block_rows * width // folds
+    own_out = dense[:, 3 * width : 4 * width].reshape(folds, fold_out)
+    first_pack = Gather(jnp.concatenate([message, own_out], axis=1), place)
+    routes_low = jnp.concatenate(
+        [routes.astype(bf16), jnp.zeros((rows, local_len, LANES - routes.shape[2]), bf16)], axis=2
+    )
+    inputs = jnp.concatenate(
+        gather_fsdp(jnp.concatenate([tokens, routes_low], axis=2), index), axis=1
+    )
+    message = jnp.concatenate(exchange_fsdp(own_columns[..., 3 * quarter :], index), axis=0)
+    message = after(message, *first_pack.blocks[1:])
+    second_pack = Gather(
+        jnp.concatenate([message, w_down.astype(bf16).reshape(folds, fold_down)], axis=1), place
+    )
+    first_pack.cross()
+    pack = first_pack.last()
+    w_qkv, w_route = pack[:, : 3 * quarter], pack[:, 3 * quarter : 3 * quarter + LANES]
+    w_out = pack[:, 3 * quarter + LANES :].reshape(DP, block_rows, width)
+    gain_rows = w_route[:, experts : experts + 2].astype(jnp.float32).T
+    gain_one, gain_two = gain_rows[0:1], gain_rows[1:2]
+
+    x_all = inputs[..., :width]
+    route_all = inputs[..., width:].astype(jnp.int32).reshape(count, LANES)
+    all_places = jnp.arange(row_len)
+    valid_all = all_places[None, :] < lengths[:, None]
+    half = head_size // 2
+    frequency = 10000.0 ** (-2.0 * jnp.arange(half, dtype=jnp.float32) / head_size)
+    angles = all_places.astype(jnp.float32)[:, None] * frequency[None, :]
+    repeats = (1, 2 * quarter // half)
+    cosine, sine = jnp.tile(jnp.cos(angles), repeats), jnp.tile(jnp.sin(angles), repeats)
+
+    normed_one, qkv, probs, attended = attention_forward(
+        x_all, gain_one, w_qkv, cosine, sine, lengths
+    )
+    cot_all = jnp.concatenate(gather_fsdp(after(cotangent, pack), index), axis=1)
+    d_out_all = jnp.where(valid_all[..., None], cot_all, 0).reshape(count, width)
+    attended_all = jnp.concatenate(gather_fsdp(attended, index), axis=2)
+    w_out = jnp.stack(gather_fsdp(w_out, index), axis=1).reshape(width, width)
+    second_pack.cross()
+    pack = second_pack.last()
+    w_shared = pack[:, : 2 * ff_part]
+    down_copy = pack[:, 2 * ff_part :].reshape(DP * down_rows, width)
+    mid_all, normed_all, turned_all, gates_all = middle_forward(
+        after(attended_all, second_pack.other).reshape(count, width), x_all.reshape(count, width), route_all, w_out, w_route,
+        gain_two,
+    )
+    gate_column = lax.dynamic_slice_in_dim(gates_all, index, 1, 1)
+    tile = 2 * e_down.shape[1]
+    ff_width = e_gate_up.shape[3]
+    first_out, first_back, grad_pair, grad_down = shared_branch(
+        normed_all, turned_all, d_out_all, w_shared, down_copy, tile
+    )
+    sum_shared = Reduce(
+        jnp.concatenate([grad_pair, grad_down.reshape(width, fold_down)], axis=1), place
+    )
+    sum_shared.cross()
+    out_keep, out_send, back_keep, back_send, grad_pairs, edown_keep, edown_send = expert_branch(
+        jnp.stack([index, dp_index % 2]), after(normed_all, sum_shared.got), turned_all, d_out_all,
+        gate_column, first_out, first_back, gate_up_copy, edown_copy, tile,
+    )
+
+    sum_shared.along()
+    part_pairs = lax.psum_scatter(grad_pairs, "dp", scatter_dimension=0, tiled=True)
+    d_sum = FsdpSum(back_keep, after(back_send, *sum_shared.parts[1:]), index)
+    sum_edown = Reduce(None, place)
+    sum_edown.mine, sum_edown.got = edown_keep, pair_hop(edown_send)
+
+    def by_place(values):
+        return values.reshape(rows, FS, local_len, values.shape[-1]).transpose(1, 0, 2, 3)
+
+    def own_rows(values):
+        part = lax.dynamic_slice_in_dim(
+            values.reshape(rows, row_len, values.shape[-1]), index * local_len, local_len, 1
+        )
+        return part.reshape(rows * local_len, values.shape[-1])
+
+    d_sum = d_sum.cross().last().reshape(rows * local_len, width + LANES)
+    mid = own_rows(mid_all)
+    d_out = own_rows(d_out_all)
+    d_mid, grad_wout, grad_router, grad_gain_two, *d_att = middle_backward(
+        index.reshape(1), mid, d_out, d_sum, own_rows(gates_all),
+        routes.reshape(rows * local_len, -1), own_rows(attended_all), own_rows(normed_all), w_out,
+        w_route, gain_two,
+    )
+    d_att = [block.reshape(rows, local_len, quarter) for block in d_att]
+    d_att = [d_att[0]] + [fsdp_hop(d_att[step], step) for step in range(1, FS)]
+    grad_wout = grad_wout.reshape(DP, FS, block_rows, width).transpose(1, 0, 2, 3)
+    sum_wout = FsdpSum(*by_core(grad_wout, index, d_att[1]), index).cross()
+    grad_wout = sum_wout.last().astype(bf16).reshape(width, fold_out)
+    d_att = jnp.concatenate(by_source(*d_att, index), axis=1)
+    grad_qkv, back_part = attention_backward(
+        normed_one, qkv, probs, after(d_att, sum_wout.far), w_qkv, cosine, sine
+    )
+    sum_last = Reduce(jnp.concatenate([grad_qkv, grad_wout], axis=1), place)
+    sum_last.cross()
+    sum_last.along()
+    sum_edown.along(sum_last.both)
+
+    split_pair = lambda part, half: part.reshape(part.shape[0], -1, 2, tile)[:, :, half].reshape(
+        part.shape[0], -1
+    )
+    part_shared = sum_shared.last()
+    part_down = part_shared[:, 2 * ff_part :].reshape(down_rows, width)
+    raw_pairs = part_pairs
+    part_pairs = part_pairs.astype(jnp.float32)
+    part_gate_up = jnp.stack([split_pair(part_pairs, half) for half in range(2)])
+    part_last = sum_last.last()
+    part_edown = sum_edown.last()
+    part_out = part_last[:, 3 * quarter :].reshape(block_rows, width)
+    part_near = jnp.concatenate(
+        [
+            part_last[:, : 3 * quarter],
+            split_pair(part_shared[:, : 2 * ff_part], 0),
+            split_pair(part_shared[:, : 2 * ff_part], 1),
+        ],
+        axis=1,
+    )
+    part_dense = part_near.astype(bf16)
+
+    out_sum = FsdpSum(out_keep, after(out_send, sum_last.got), index).cross().last()
+    out_sum = out_sum.reshape(rows * local_len, width)
+    valid = (
+        (index * local_len + jnp.arange(local_len))[None, :] < lengths[:, None]
+    ).astype(jnp.float32)
+    output = ((mid + out_sum).reshape(tokens.shape) * valid[..., None]).astype(bf16)
+    d_one = FsdpSum(*by_core(by_place(back_part), index, sum_last.sent), index).cross().last()
+    d_one = d_one.reshape(tokens.shape)
+    scaled_one, inverse_one = statistics(tokens.astype(jnp.float32))
+    d_in, grad_gain_one = norm_back(d_one, scaled_one, inverse_one, gain_one)
+    d_tokens = (d_mid.reshape(tokens.shape) + d_in).astype(bf16)
+
+    old_near = exchange_fsdp(by_columns(after(mom_dense, normed_all).astype(bf16)), index)
+    old_near = jnp.concatenate(old_near, axis=0).astype(jnp.float32)
+    got = exchange_fsdp(part_dense.reshape(FS, block_rows, part_dense.shape[1]), index)
+    got = [block.astype(jnp.float32) for block in got]
+    cut = lambda start, size: [block[:, start : start + size] for block in got]
+    interleave = lambda parts: jnp.stack(
+        [part.reshape(block_rows, DP, down_rows) for part in parts], axis=2
+    ).reshape(block_rows, ff_shared)
+    grad_dense = jnp.concatenate(
+        cut(0, quarter)
+        + cut(quarter, quarter)
+        + cut(2 * quarter, quarter)
+        + [part_out]
+        + [interleave(cut(3 * quarter, ff_part)), interleave(cut(3 * quarter + ff_part, ff_part))],
+        axis=1,
+    )
+    new_mom_dense = MUON_DECAY * mom_dense + grad_dense
+    new_mom_down = MUON_DECAY * mom_down + part_down
+    new_e_mom_gate_up = MUON_DECAY * e_mom_gate_up + part_gate_up[None]
+    new_e_mom_down = MUON_DECAY * e_mom_down + part_edown[None]
+
+    length = 3 * width
+    pad = lambda block: jnp.pad(block, ((0, 0), (0, length - block.shape[1])))
+    edges = (0, 3 * width, 4 * width, 4 * width + ff_shared, 4 * width + 2 * ff_shared)
+    spots = (0, 3 * quarter, 3 * quarter + ff_part, 3 * quarter + 2 * ff_part)
+    near = (MUON_DECAY * old_near + part_near).astype(bf16)
+    near_out = (MUON_DECAY * mom_dense[:, 3 * width : 4 * width] + part_out).astype(bf16)
+    stripe = lambda block: jnp.pad(block, ((0, 0), (0, 3 * quarter - block.shape[1])))
+    stripes = [near[:, spots[i] : spots[i + 1]] for i in range(3)]
+    stripes.append(near_out.reshape(folds, fold_out))
+    stripes = after(jnp.stack([stripe(block) for block in stripes]), *sum_edown.parts[1:])
+    got = exchange_fsdp(stripes, index)
+    whole_out = jnp.concatenate(
+        [block[:, :fold_out].reshape(block_rows, width) for block in got], axis=0
+    )
+    dense_block = jnp.where(index == FS - 1, pad(whole_out), jnp.concatenate(got, axis=1))
+    low_experts = new_e_mom_gate_up[0].astype(bf16)
+    wide = [pad(low_experts[0]), pad(low_experts[1]), dense_block]
+    low_down = after(new_mom_down.astype(bf16), sum_last.got)
+    column_pairs = lambda step, back: [
+        (d * FS + DOWN_COLUMN, d * FS + (DOWN_COLUMN ^ step))[:: 1 if back else -1]
+        for d in range(DP)
+    ]
+    down_block = jnp.concatenate(
+        [
+            low_down if f == DOWN_COLUMN else lax.ppermute(
+                low_down, AXES, column_pairs(DOWN_COLUMN ^ f, False)
+            )
+            for f in range(FS)
+        ],
+        axis=0,
+    )
+    talls = [fold_tall(new_e_mom_down[0].astype(bf16), folds, length), fold_tall(down_block, folds, length)]
+    arrived = to_owners(jnp.stack(wide + talls), OWNERS, dp_index, index)
+    kinds = np.zeros((FS, DP), np.int32)
+    for f in range(FS):
+        for slot, d in enumerate(OWNERS[f]):
+            kinds[f, d] = 2 if slot in TALL_SLOTS else 1
+    info = jnp.stack([jnp.asarray(kinds)[index, dp_index], dp_index.astype(jnp.int32)])
+    shards = orthogonal_shards(info, arrived, width)
+    columns = (0, device_index * block_rows)
+    zeros = jnp.zeros((8 - experts - 2, width), jnp.float32)
+    small = jnp.concatenate(
+        [grad_router[:experts], grad_gain_one[None], grad_gain_two, zeros], axis=0
+    )
+    old = jnp.concatenate(
+        [MUON_DECAY * mom_router.T, GAIN_DECAY * gain_moms, zeros[:, :block_rows]], axis=0
+    )
+    small = small + lax.dynamic_update_slice(jnp.zeros_like(small), old, columns)
+    small = sum_everywhere(after(small, sum_last.both))
+    own_small = lax.dynamic_slice(small, columns, (8, block_rows))
+    new_mom_router = own_small[:experts].T
+    new_gain_moms = own_small[experts : experts + 2]
+    gain_rate = 0.1 / math.sqrt(count * DP)
+    new_gains = gains - gain_rate * new_gain_moms
+    orth_router = orthogonal_router(
+        jnp.concatenate([after(small, *shards)[:experts], jnp.zeros((LANES - experts, width), jnp.float32)], axis=0)
+    )
+    new_router = w_router - ROUTER_RATE * lax.dynamic_slice(
+        orth_router, columns, (experts, block_rows)
+    ).T
+
+    orth_gate, orth_up, orth_block, orth_edown, orth_down_block = from_owners(
+        shards, OWNERS, dp_index, index
+    )
+    orth_edown = unfold_tall(orth_edown, e_down.shape[1])
+    orth_down_block = unfold_tall(orth_down_block, e_down.shape[1])
+    got = exchange_fsdp(orth_block.reshape(FS, block_rows, length), index)
+    striped = lambda block: block.reshape(block_rows, FS, 3 * quarter)
+    orth_qkv = striped(got[0]).reshape(block_rows, FS, 3, quarter).transpose(0, 2, 1, 3)
+    orth_shared = [
+        striped(got[i])[:, :, :ff_part]
+        .reshape(block_rows, FS, DP, down_rows)
+        .transpose(0, 2, 1, 3)
+        .reshape(block_rows, ff_shared)
+        for i in (1, 2)
+    ]
+    orth_dense = [orth_qkv.reshape(block_rows, 3 * width), got[3][:, :width]] + orth_shared
+    orth_down_parts = orth_down_block.reshape(FS, down_rows, width)
+    orth_down = jnp.where(index == DOWN_COLUMN, orth_down_parts[DOWN_COLUMN], 0)
+    for f in range(FS):
+        if f != DOWN_COLUMN:
+            orth_down = orth_down + lax.ppermute(
+                orth_down_parts[f], AXES, column_pairs(DOWN_COLUMN ^ f, True)
+            )
+    new_dense = jnp.concatenate(
+        [
+            w_dense[:, edges[i] : edges[i + 1]] - DENSE_RATES[i] * orth_dense[i].astype(jnp.float32)
+            for i in range(4)
+        ],
+        axis=1,
+    )
+    new_down = w_down - DOWN_RATE * orth_down.astype(jnp.float32)
+    new_e_gate_up = jnp.stack(
+        [
+            e_gate_up[0, i] - EXPERT_RATES[i] * part[:, :ff_width].astype(jnp.float32)
+            for i, part in enumerate((orth_gate, orth_up))
+        ]
+    )[None]
+    new_e_down = e_down - EXPERT_RATES[2] * orth_edown.astype(jnp.float32)[None]
+    return (
+        output,
+        d_tokens,
+        new_gain_moms,
+        new_gains,
+        new_mom_dense,
+        new_dense,
+        new_mom_router,
+        new_router,
+        new_mom_down,
+        new_down,
+        new_e_mom_gate_up,
+        new_e_gate_up,
+        new_e_mom_down,
+        new_e_down,
+    )
+
+
 def solution(mesh):
     placed = (
         P("dp", "fsdp", None),
@@ -497,8 +1664,9 @@
         P("fsdp", "dp", None),
         P("fsdp", "dp", None),
     )
+    fits = dict(mesh.shape) == {"dp": DP, "fsdp": FS}
     return jax.shard_map(
-        per_device,
+        split_plan if fits else general_plan,
         mesh=mesh,
         in_specs=placed,
         out_specs=(

time: 2450 us -> 720 us (0.29)
  the two profiles are of different devices: /device:TPU:26 before, /device:TPU:15 now
where the time goes in v1:
time: 720 us; the launch traced here: 712 us
  waiting for transfers between devices  234 us (32%)
  local copies, waits for them, and re-layouts  135 us (19%)
  starting transfers between devices  119 us (17%)
  Pallas kernels  112 us (16%)
  other arithmetic  77.6 us (11%)
  between operations  34.1 us (5%)
    ppermute x7, waiting for transfers between devices, from_owners(): lax.ppermute(block, AXES, owner_pairs(owners, step, True))  79.9 us
    ppermute x15, waiting for transfers between devices, line_hop(): return lax.ppermute(value, AXES, pairs)  64.9 us
    ppermute x41, starting transfers between devices, fsdp_hop(): return lax.ppermute(value, AXES, pairs)  45.2 us
    pallas_call x1, Pallas kernels, expert_branch(): kernel_call(expert_body, outs + [shape_of((width, 2 * hidden)), halves, h...  43.6 us
    ppermute x5, waiting for transfers between devices, pair_hop(): return lax.ppermute(value, AXES, pairs)  35.3 us
    ppermute x7, waiting for transfers between devices, to_owners(): lax.ppermute(block, AXES, owner_pairs(owners, step, False))  29.7 us
    ppermute x15, starting transfers between devices, line_hop(): return lax.ppermute(value, AXES, pairs)  25.6 us
    ppermute x41, waiting for transfers between devices, fsdp_hop(): return lax.ppermute(value, AXES, pairs)  20.5 us
  transfers between devices with their start and end apart: 89, of which 28 were waited for; matrix products, arithmetic and copies ran while one was open for 27% of the time, Pallas kernels for 15%

profile of v1, /device:TPU:15, one launch (start us, length us, event | category | flops | bytes accessed | tf_op | source)
XLA Modules:
  0.0 711.9 jit_solution(2914379915955518114)
XLA Ops:
  31.1 8.9 %collective-permute-done.8.refs_3_ = bf16[96,896]{1,0:T(8,128)(2,1)S(1)} collective-permute-done((bf16[96,896]{1,0:T(8,128)(2,1)S(1)}, bf16[96,896]{1,0:T(8,128)(2,1)S(1)}, u32[]{:S(2)}, u32[]{:S(2)}) %collective-permute-start.8) | collective-permute-done | bytes 172064 | tf_op jit(solution)/shard_map/ppermute | solution.py:1238
  40.0 4.7 collective-permute-done.7.refs_2_
  44.7 3.7 collective-permute-done.6.refs_1_
  48.9 3.4 collective-permute-start.18
  55.9 13.0 %collective-permute-done.18.refs_3_ = bf16[96,1536]{1,0:T(8,128)(2,1)S(1)} collective-permute-done((bf16[96,1536]{1,0:T(8,128)(2,1)S(1)}, bf16[96,1536]{1,0:T(8,128)(2,1)S(1)}, u32[]{:S(2)}, u32[]{:S(2)}) %collective-permute-start.18) | collective-permute-done | bytes 294944 | tf_op jit(solution)/shard_map/ppermute | solution.py:1238
  69.0 10.5 %collective-permute-start.2 = (bf16[2,128,896]{2,1,0:T(8,128)(2,1)}, bf16[2,128,896]{2,1,0:T(8,128)(2,1)}, u32[]{:S(2)}, u32[]{:S(2)}) collective-permute-start(bf16[2,128,896]{2,1,0:T(8,128)(2,1)} %collective-permute-done), channel_id=1, source_target_pairs={{0,1},{1,0},{2,3},{3,2},{4,5},{5,4},{6,7},{7,6},{8,9},{9,8},{10,11... | collective-permute-start | bytes 1376264 | tf_op jit(solution)/shard_map/ppermute | solution.py:537
  79.5 5.2 collective-permute-done.17.refs_2_
  84.7 17.0 %collective-permute-done.16.refs_1_ = bf16[96,1536]{1,0:T(8,128)(2,1)S(1)} collective-permute-done((bf16[96,1536]{1,0:T(8,128)(2,1)S(1)}, bf16[96,1536]{1,0:T(8,128)(2,1)S(1)}, u32[]{:S(2)}, u32[]{:S(2)}) %collective-permute-start.16) | collective-permute-done | bytes 294944 | tf_op jit(solution)/shard_map/ppermute | solution.py:1238
  104.3 2.6 place_rows.2
  117.5 9.0 %attention_forward.1 = (bf16[768,1024]{1,0:T(8,128)(2,1)}, bf16[2,512,576]{2,1,0:T(8,128)(2,1)}, bf16[2,3,512,512]{3,2,1,0:T(8,128)(2,1)}, bf16[2,512,192]{2,1,0:T(8,128)(2,1)}) custom-call(s32[2]{0:T(128)} %lengths_ref.1, bf16[2,512,768]{2,1,0:T(8,128)(2,1)} %slice.365.x_ref, f32[1,768]{1,0:T(1,128)} %get-tuple-element.290.gain_ref, ...), custom_call_target="tpu_custom_call" | custom-call | flops 6000000000 | bytes 12000000 | tf_op jit(solution)/shard_map/attention_forward/pallas_call | solution.py:645
  132.2 6.8 collective-permute-done.10
  142.7 3.2 place_rows.3
  145.9 2.8 slice.380.gate_ref.up_ref
  156.5 7.7 %middle_forward.1 = (f32[1024,768]{1,0:T(8,128)}, bf16[1024,768]{1,0:T(8,128)(2,1)}, bf16[768,1024]{1,0:T(8,128)(2,1)}, f32[1024,128]{1,0:T(8,128)}) custom-call(bf16[1024,768]{1,0:T(8,128)(2,1)} %bitcast.437, bf16[1024,768]{1,0:T(8,128)(2,1)} %bitcast.441, s32[1024,128]{1,0:T(8,128)} %bitcast_convert_fusion.routes_ref, bf16[768,768]{1,0:T(8,128)(2,1)} %bitcast.435, ...), custom_call_target="tpu_custom_call" | custom-call | flops 1207959552 | bytes 12000000 | tf_op jit(solution)/shard_map/middle_forward/pallas_call | solution.py:763
  164.2 13.0 %shared_branch.1 = (f32[1024,768]{1,0:T(8,128)}, f32[1024,768]{1,0:T(8,128)}, bf16[768,1024]{1,0:T(8,128)(2,1)}, bf16[512,768]{1,0:T(8,128)(2,1)}) custom-call(bf16[1024,768]{1,0:T(8,128)(2,1)} %get-tuple-element.75.normed_ref, bf16[768,1024]{1,0:T(8,128)(2,1)} %get-tuple-element.71.turned_ref, bf16[1024,768]{1,0:T(8,128)(2,1)} %bitcast_select_fusion.d_out_ref, ...), custom_call_target="tpu_custom_call" | custom-call | flops 7247757312 | bytes 14155776 | tf_op jit(solution)/shard_map/shared_branch/pallas_call | solution.py:977
  178.8 2.3 fusion.5
  209.8 2.4 collective-permute-done.26
  220.2 43.6 %expert_branch.1 = (bf16[2,256,768]{2,1,0:T(8,128)(2,1)}, bf16[2,256,768]{2,1,0:T(8,128)(2,1)}, bf16[2,256,896]{2,1,0:T(8,128)(2,1)}, bf16[2,256,896]{2,1,0:T(8,...) custom-call(s32[2]{0:T(128)} %pad_add_fusion.1.place_ref, ...), custom_call_target="tpu_custom_call" | custom-call | flops 28991029248 | bytes 31457280 | tf_op jit(solution)/shard_map/expert_branch/pallas_call | solution.py:1006
  263.8 5.2 collective-permute-start.30
  282.4 4.5 collective-permute-done.31
  287.9 5.9 middle_backward.1
  302.2 3.7 collective-permute-start.56
  310.3 5.4 collective-permute-done.34
  316.7 2.9 collective-permute-done.36
  320.0 15.0 %attention_backward.1 = (bf16[768,576]{1,0:T(8,128)(2,1)}, bf16[2,512,768]{2,1,0:T(8,128)(2,1)}) custom-call(bf16[768,1024]{1,0:T(8,128)(2,1)} %get-tuple-element.81.normed_ref, bf16[2,512,576]{2,1,0:T(8,128)(2,1)} %get-tuple-element.82.qkv_ref, bf16[2,3,512,512]{3,2,1,0:T(8,128)(2,1)} %get-tuple-element.83.prob_ref, ...), custom_call_target="tpu_custom_call" | custom-call | flops 8000000000 | bytes 12000000 | tf_op jit(solution)/shard_map/attention_backward/pallas_call | solution.py:714
  340.7 32.9 %collective-permute-done.37 = bf16[4,96,768]{2,1,0:T(8,128)(2,1)S(1)} collective-permute-done((bf16[4,96,768]{2,1,0:T(8,128)(2,1)S(1)}, bf16[4,96,768]{2,1,0:T(8,128)(2,1)S(1)}, u32[]{:S(2)}, u32[]{:S(2)}) %collective-permute-start.37) | collective-permute-done | bytes 589856 | tf_op jit(solution)/shard_map/ppermute | solution.py:1243
  378.7 5.7 collective-permute-start.47
  392.9 12.0 %collective-permute-done.48 = bf16[96,768]{1,0:T(8,128)(2,1)} collective-permute-done((bf16[96,768]{1,0:T(8,128)(2,1)}, bf16[96,768]{1,0:T(8,128)(2,1)}, u32[]{:S(2)}, u32[]{:S(2)}) %collective-permute-start.48) | collective-permute-done | bytes 147488 | tf_op jit(solution)/shard_map/ppermute | solution.py:1238
  409.4 2.4 collective-permute-start.50
  417.9 4.3 collective-permute-start.58
  473.1 2.7 convert_bitcast_fusion
  478.8 2.9 collective-permute-start.44
  504.0 2.6 reshape.550
  506.6 5.4 slice_reduce_fusion.1
  515.2 3.1 fusion.66
  520.6 2.9 collective-permute-start.72
  530.6 8.6 %collective-permute-start.67 = (bf16[96,2304]{1,0:T(8,128)(2,1)S(1)}, bf16[96,2304]{1,0:T(8,128)(2,1)S(1)}, u32[]{:S(2)}, u32[]{:S(2)}) collective-permute-start(bf16[96,2304]{1,0:T(8,128)(2,1)S(1)} %get-tuple-element.171), channel_id=1, source_target_pairs={{8,0},{20,12},{24,16},{4,28},{13,5},{17,9},{29,21},{1,25},{10,2},{... | collective-permute-start | bytes 1327112 | tf_op jit(solution)/shard_map/ppermute | solution.py:1210
  539.2 24.5 %collective-permute-done.71.refs_6_ = bf16[96,2304]{1,0:T(8,128)(2,1)S(1)} collective-permute-done((bf16[96,2304]{1,0:T(8,128)(2,1)S(1)}, bf16[96,2304]{1,0:T(8,128)(2,1)S(1)}, u32[]{:S(2)}, u32[]{:S(2)}) %collective-permute-start.71) | collective-permute-done | bytes 442400 | tf_op jit(solution)/shard_map/ppermute | solution.py:1210
  567.3 4.0 collective-permute-done.70.refs_5_
  573.1 3.8 orthogonal_shards.1
  584.7 8.7 %orthogonal_router.1 = f32[128,768]{1,0:T(8,128)} custom-call(f32[128,768]{1,0:T(8,128)} %concatenate.138.matrix_ref), custom_call_target="tpu_custom_call" | custom-call | flops 2000000000 | bytes 1000000 | tf_op jit(solution)/shard_map/orthogonal_router/pallas_call | solution.py:1180
  594.7 30.6 %collective-permute-done.73 = bf16[96,2304]{1,0:T(8,128)(2,1)S(1)} collective-permute-done((bf16[96,2304]{1,0:T(8,128)(2,1)}, bf16[96,2304]{1,0:T(8,128)(2,1)S(1)}, u32[]{:S(2)}, u32[]{:S(2)}) %collective-permute-start.73) | collective-permute-done | bytes 442400 | tf_op jit(solution)/shard_map/ppermute | solution.py:1218
  627.3 4.1 collective-permute-done.74
  635.2 8.8 %collective-permute-done.77 = bf16[96,2304]{1,0:T(8,128)(2,1)S(1)} collective-permute-done((bf16[96,2304]{1,0:T(8,128)(2,1)}, bf16[96,2304]{1,0:T(8,128)(2,1)S(1)}, u32[]{:S(2)}, u32[]{:S(2)}) %collective-permute-start.77) | collective-permute-done | bytes 442400 | tf_op jit(solution)/shard_map/ppermute | solution.py:1218
  644.8 13.7 %collective-permute-done.78 = bf16[96,2304]{1,0:T(8,128)(2,1)S(1)} collective-permute-done((bf16[96,2304]{1,0:T(8,128)(2,1)S(1)}, bf16[96,2304]{1,0:T(8,128)(2,1)S(1)}, u32[]{:S(2)}, u32[]{:S(2)}) %collective-permute-start.78) | collective-permute-done | bytes 442400 | tf_op jit(solution)/shard_map/ppermute | solution.py:1218
  659.3 22.8 %collective-permute-done.79 = bf16[96,2304]{1,0:T(8,128)(2,1)S(1)} collective-permute-done((bf16[96,2304]{1,0:T(8,128)(2,1)S(1)}, bf16[96,2304]{1,0:T(8,128)(2,1)S(1)}, u32[]{:S(2)}, u32[]{:S(2)}) %collective-permute-start.79) | collective-permute-done | bytes 442400 | tf_op jit(solution)/shard_map/ppermute | solution.py:1218
  682.9 2.4 dynamic-slice_bitcast_fusion.2
  689.9 2.7 collective-permute-start.83
  (599 shorter events, 264.1 us)
Async XLA Ops:
  7.2 212.5 %all-gather.7.cloned.1.call-start = ((), (), s32[]{:S(2)}) async-start(), calls=%async_computation.3 | async-start | bytes 3538944 | tf_op jit(solution)/shard_map/all_gather | solution.py:1375
  9.3 210.9 %all-gather.5.cloned.1.call-start = ((), (), s32[]{:S(2)}) async-start(), calls=%async_computation.2 | async-start | bytes 7077888 | tf_op jit(solution)/shard_map/all_gather | solution.py:1374
  10.5 493.6 %reduce-scatter.2.cloned.1.call-start = ((), (), s32[]{:S(2)}) async-start(), calls=%async_computation.1 | async-start | bytes 7077888 | tf_op jit(solution)/shard_map/reduce_scatter | solution.py:1441
  25.8 28.7 %collective-permute-start = (bf16[2,128,896]{2,1,0:T(8,128)(2,1)}, bf16[2,128,896]{2,1,0:T(8,128)(2,1)}, u32[]{:S(2)}, u32[]{:S(2)}) collective-permute-start(bf16[2,128,896]{2,1,0:T(8,128)(2,1)} %maximum_maximum_fusion), channel_id=1, source_target_pairs={{0,2},{1,3},{2,0},{3,1},{4,6},{5,7},{6,4},{7,5},{8,10},{9,11},{10,... | collective-permute-start | bytes 1376264 | tf_op jit(solution)/shard_map/ppermute | solution.py:537
  26.6 18.1 %collective-permute-start.7 = (bf16[96,896]{1,0:T(8,128)(2,1)S(1)}, bf16[96,896]{1,0:T(8,128)(2,1)S(1)}, u32[]{:S(2)}, u32[]{:S(2)}) collective-permute-start(bf16[96,896]{1,0:T(8,128)(2,1)S(1)} %pad_maximum_fusion.13.refs_0_), channel_id=1, source_target_pairs={{0,16},{1,17},{2,18},{3,19},{4,20},{5,21},{6,22},{7,23},{8,24},{9,... | collective-permute-start | bytes 516104 | tf_op jit(solution)/shard_map/ppermute | solution.py:1238
  28.9 19.5 %collective-permute-start.6 = (bf16[96,896]{1,0:T(8,128)(2,1)S(1)}, bf16[96,896]{1,0:T(8,128)(2,1)S(1)}, u32[]{:S(2)}, u32[]{:S(2)}) collective-permute-start(bf16[96,896]{1,0:T(8,128)(2,1)S(1)} %pad_maximum_fusion.13.refs_0_), channel_id=1, source_target_pairs={{0,8},{1,9},{2,10},{3,11},{4,12},{5,13},{6,14},{7,15},{8,16},{9,17... | collective-permute-start | bytes 516104 | tf_op jit(solution)/shard_map/ppermute | solution.py:1238
  48.5 54.9 %collective-permute-start.9 = (bf16[4,96,896]{2,1,0:T(8,128)(2,1)S(1)}, bf16[4,96,896]{2,1,0:T(8,128)(2,1)S(1)}, u32[]{:S(2)}, u32[]{:S(2)}) collective-permute-start(bf16[4,96,896]{2,1,0:T(8,128)(2,1)S(1)} %pad_maximum_fusion.5), channel_id=1, source_target_pairs={{0,4},{1,5},{2,6},{3,7},{4,0},{5,1},{6,2},{7,3},{8,12},{9,13},{10,... | collective-permute-start | bytes 2064392 | tf_op jit(solution)/shard_map/ppermute | solution.py:1243
  48.9 20.1 %collective-permute-start.18 = (bf16[96,1536]{1,0:T(8,128)(2,1)S(1)}, bf16[96,1536]{1,0:T(8,128)(2,1)S(1)}, u32[]{:S(2)}, u32[]{:S(2)}) collective-permute-start(bf16[96,1536]{1,0:T(8,128)(2,1)S(1)} %constant_dynamic-update-slice_fusion.refs_0_), channel_id=1, source_target_pairs={{0,24},{1,25},{2,26},{3,27},{4,28},{5,29},{6,30},{7,31},{8,0},{9,1... | collective-permute-start | bytes 884744 | tf_op jit(solution)/shard_map/ppermute | solution.py:1238
  52.3 32.4 %collective-permute-start.17 = (bf16[96,1536]{1,0:T(8,128)(2,1)S(1)}, bf16[96,1536]{1,0:T(8,128)(2,1)S(1)}, u32[]{:S(2)}, u32[]{:S(2)}) collective-permute-start(bf16[96,1536]{1,0:T(8,128)(2,1)S(1)} %constant_dynamic-update-slice_fusion.refs_0_), channel_id=1, source_target_pairs={{0,16},{1,17},{2,18},{3,19},{4,20},{5,21},{6,22},{7,23},{8,24},{9,... | collective-permute-start | bytes 884744 | tf_op jit(solution)/shard_map/ppermute | solution.py:1238
  52.4 49.3 %collective-permute-start.16 = (bf16[96,1536]{1,0:T(8,128)(2,1)S(1)}, bf16[96,1536]{1,0:T(8,128)(2,1)S(1)}, u32[]{:S(2)}, u32[]{:S(2)}) collective-permute-start(bf16[96,1536]{1,0:T(8,128)(2,1)S(1)} %constant_dynamic-update-slice_fusion.refs_0_), channel_id=1, source_target_pairs={{0,8},{1,9},{2,10},{3,11},{4,12},{5,13},{6,14},{7,15},{8,16},{9,17... | collective-permute-start | bytes 884744 | tf_op jit(solution)/shard_map/ppermute | solution.py:1238
  54.5 59.7 %collective-permute-start.1 = (bf16[2,128,896]{2,1,0:T(8,128)(2,1)}, bf16[2,128,896]{2,1,0:T(8,128)(2,1)}, u32[]{:S(2)}, u32[]{:S(2)}) collective-permute-start(bf16[2,128,896]{2,1,0:T(8,128)(2,1)} %maximum_maximum_fusion), channel_id=1, source_target_pairs={{0,1},{1,0},{2,3},{3,2},{4,5},{5,4},{6,7},{7,6},{8,9},{9,8},{10,11... | collective-permute-start | bytes 1376264 | tf_op jit(solution)/shard_map/ppermute | solution.py:537
  69.0 45.2 %collective-permute-start.2 = (bf16[2,128,896]{2,1,0:T(8,128)(2,1)}, bf16[2,128,896]{2,1,0:T(8,128)(2,1)}, u32[]{:S(2)}, u32[]{:S(2)}) collective-permute-start(bf16[2,128,896]{2,1,0:T(8,128)(2,1)} %collective-permute-done), channel_id=1, source_target_pairs={{0,1},{1,0},{2,3},{3,2},{4,5},{5,4},{6,7},{7,6},{8,9},{9,8},{10,11... | collective-permute-start | bytes 1376264 | tf_op jit(solution)/shard_map/ppermute | solution.py:537
  102.9 39.8 %collective-permute-start.19 = (bf16[4,96,1536]{2,1,0:T(8,128)(2,1)}, bf16[4,96,1536]{2,1,0:T(8,128)(2,1)}, u32[]{:S(2)}, u32[]{:S(2)}) collective-permute-start(bf16[4,96,1536]{2,1,0:T(8,128)(2,1)} %pad_maximum_fusion.3), channel_id=1, source_target_pairs={{0,4},{1,5},{2,6},{3,7},{4,0},{5,1},{6,2},{7,3},{8,12},{9,13},{10,... | collective-permute-start | bytes 3538952 | tf_op jit(solution)/shard_map/ppermute | solution.py:1243
  110.8 19.7 %collective-permute-start.20 = (bf16[8,24,768]{2,1,0:T(8,128)(2,1)S(1)}, bf16[8,24,768]{2,1,0:T(8,128)(2,1)S(1)}, u32[]{:S(2)}, u32[]{:S(2)}) collective-permute-start(bf16[8,24,768]{2,1,0:T(8,128)(2,1)S(1)} %reshape.491), channel_id=1, source_target_pairs={{0,2},{1,3},{2,0},{3,1},{4,6},{5,7},{6,4},{7,5},{8,10},{9,11},{10,... | collective-permute-start | bytes 884744 | tf_op jit(solution)/shard_map/ppermute | solution.py:537
  112.1 20.0 %collective-permute-start.23 = (bf16[2,128,768]{2,1,0:T(8,128)(2,1)}, bf16[2,128,768]{2,1,0:T(8,128)(2,1)}, u32[]{:S(2)}, u32[]{:S(2)}) collective-permute-start(bf16[2,128,768]{2,1,0:T(8,128)(2,1)} %param.20), channel_id=1, source_target_pairs={{0,2},{1,3},{2,0},{3,1},{4,6},{5,7},{6,4},{7,5},{8,10},{9,11},{10,... | collective-permute-start | bytes 1179656 | tf_op jit(solution)/shard_map/ppermute | solution.py:537
  131.7 18.3 %collective-permute-start.24 = (bf16[2,128,768]{2,1,0:T(8,128)(2,1)}, bf16[2,128,768]{2,1,0:T(8,128)(2,1)S(1)}, u32[]{:S(2)}, u32[]{:S(2)}) collective-permute-start(bf16[2,128,768]{2,1,0:T(8,128)(2,1)} %param.20), channel_id=1, source_target_pairs={{0,1},{1,0},{2,3},{3,2},{4,5},{5,4},{6,7},{7,6},{8,9},{9,8},{10,11... | collective-permute-start | bytes 1179656 | tf_op jit(solution)/shard_map/ppermute | solution.py:537
  132.1 20.8 %collective-permute-start.11 = (bf16[2,512,192]{2,1,0:T(8,128)(2,1)S(1)}, bf16[2,512,192]{2,1,0:T(8,128)(2,1)}, u32[]{:S(2)}, u32[]{:S(2)}) collective-permute-start(bf16[2,512,192]{2,1,0:T(8,128)(2,1)S(1)} %copy-done.41), channel_id=1, source_target_pairs={{0,1},{1,0},{2,3},{3,2},{4,5},{5,4},{6,7},{7,6},{8,9},{9,8},{10,11... | collective-permute-start | bytes 1179656 | tf_op jit(solution)/shard_map/ppermute | solution.py:537
  181.1 31.1 %collective-permute-start.26 = (bf16[4,96,1536]{2,1,0:T(8,128)(2,1)}, bf16[4,96,1536]{2,1,0:T(8,128)(2,1)}, u32[]{:S(2)}, u32[]{:S(2)}) collective-permute-start(bf16[4,96,1536]{2,1,0:T(8,128)(2,1)} %fusion.5), channel_id=1, source_target_pairs={{0,4},{1,5},{2,6},{3,7},{4,0},{5,1},{6,2},{7,3},{8,12},{9,13},{10,... | collective-permute-start | bytes 3538952 | tf_op jit(solution)/shard_map/ppermute | solution.py:1243
  215.1 48.6 %collective-permute-start.29 = (bf16[96,1536]{1,0:T(8,128)(2,1)S(1)}, bf16[96,1536]{1,0:T(8,128)(2,1)}, u32[]{:S(2)}, u32[]{:S(2)}) collective-permute-start(bf16[96,1536]{1,0:T(8,128)(2,1)S(1)} %get-tuple-element.191), channel_id=1, source_target_pairs={{0,24},{1,25},{2,26},{3,27},{4,28},{5,29},{6,30},{7,31},{8,0},{9,1... | collective-permute-start | bytes 884744 | tf_op jit(solution)/shard_map/ppermute | solution.py:1238
  215.4 48.4 %collective-permute-start.28 = (bf16[96,1536]{1,0:T(8,128)(2,1)S(1)}, bf16[96,1536]{1,0:T(8,128)(2,1)}, u32[]{:S(2)}, u32[]{:S(2)}) collective-permute-start(bf16[96,1536]{1,0:T(8,128)(2,1)S(1)} %get-tuple-element.192), channel_id=1, source_target_pairs={{0,16},{1,17},{2,18},{3,19},{4,20},{5,21},{6,22},{7,23},{8,24},{9,... | collective-permute-start | bytes 884744 | tf_op jit(solution)/shard_map/ppermute | solution.py:1238
  217.6 46.2 %collective-permute-start.27 = (bf16[96,1536]{1,0:T(8,128)(2,1)S(1)}, bf16[96,1536]{1,0:T(8,128)(2,1)}, u32[]{:S(2)}, u32[]{:S(2)}) collective-permute-start(bf16[96,1536]{1,0:T(8,128)(2,1)S(1)} %get-tuple-element.193), channel_id=1, source_target_pairs={{0,8},{1,9},{2,10},{3,11},{4,12},{5,13},{6,14},{7,15},{8,16},{9,17... | collective-permute-start | bytes 884744 | tf_op jit(solution)/shard_map/ppermute | solution.py:1238
  271.5 23.4 %collective-permute-start.53 = (bf16[24,1600]{1,0:T(8,128)(2,1)S(1)}, bf16[24,1600]{1,0:T(8,128)(2,1)S(1)}, u32[]{:S(2)}, u32[]{:S(2)}) collective-permute-start(bf16[24,1600]{1,0:T(8,128)(2,1)S(1)} %get-tuple-element.252), channel_id=1, source_target_pairs={{0,2},{1,3},{2,0},{3,1},{4,6},{5,7},{6,4},{7,5},{8,10},{9,11},{10,... | collective-permute-start | bytes 230408 | tf_op jit(solution)/shard_map/ppermute | solution.py:537
  271.9 23.1 %collective-permute-start.55 = (bf16[24,1600]{1,0:T(8,128)(2,1)S(1)}, bf16[24,1600]{1,0:T(8,128)(2,1)S(1)}, u32[]{:S(2)}, u32[]{:S(2)}) collective-permute-start(bf16[24,1600]{1,0:T(8,128)(2,1)S(1)} %get-tuple-element.253), channel_id=1, source_target_pairs={{0,3},{1,2},{2,1},{3,0},{4,7},{5,6},{6,5},{7,4},{8,11},{9,10},{10,... | collective-permute-start | bytes 230408 | tf_op jit(solution)/shard_map/ppermute | solution.py:537
  273.2 21.7 %collective-permute-start.54 = (bf16[24,1600]{1,0:T(8,128)(2,1)S(1)}, bf16[24,1600]{1,0:T(8,128)(2,1)S(1)}, u32[]{:S(2)}, u32[]{:S(2)}) collective-permute-start(bf16[24,1600]{1,0:T(8,128)(2,1)S(1)} %get-tuple-element.254), channel_id=1, source_target_pairs={{0,1},{1,0},{2,3},{3,2},{4,5},{5,4},{6,7},{7,6},{8,9},{9,8},{10,11... | collective-permute-start | bytes 230408 | tf_op jit(solution)/shard_map/ppermute | solution.py:537
  302.2 82.2 %collective-permute-start.56 = (bf16[4,256,768]{2,1,0:T(8,128)(2,1)}, bf16[4,256,768]{2,1,0:T(8,128)(2,1)S(1)}, u32[]{:S(2)}, u32[]{:S(2)}) collective-permute-start(bf16[4,256,768]{2,1,0:T(8,128)(2,1)} %get-tuple-element.105), channel_id=1, source_target_pairs={{0,4},{1,5},{2,6},{3,7},{4,0},{5,1},{6,2},{7,3},{8,12},{9,13},{10,... | collective-permute-start | bytes 4718600 | tf_op jit(solution)/shard_map/ppermute | solution.py:1243
  336.2 37.4 %collective-permute-start.37 = (bf16[4,96,768]{2,1,0:T(8,128)(2,1)S(1)}, bf16[4,96,768]{2,1,0:T(8,128)(2,1)S(1)}, u32[]{:S(2)}, u32[]{:S(2)}) collective-permute-start(bf16[4,96,768]{2,1,0:T(8,128)(2,1)S(1)} %fusion.31), channel_id=1, source_target_pairs={{0,4},{1,5},{2,6},{3,7},{4,0},{5,1},{6,2},{7,3},{8,12},{9,13},{10,... | collective-permute-start | bytes 1769480 | tf_op jit(solution)/shard_map/ppermute | solution.py:1243
  387.3 17.5 %collective-permute-start.48 = (bf16[96,768]{1,0:T(8,128)(2,1)}, bf16[96,768]{1,0:T(8,128)(2,1)}, u32[]{:S(2)}, u32[]{:S(2)}) collective-permute-start(bf16[96,768]{1,0:T(8,128)(2,1)} %get-tuple-element.209), channel_id=1, source_target_pairs={{0,16},{1,17},{2,18},{3,19},{4,20},{5,21},{6,22},{7,23},{8,24},{9,... | collective-permute-start | bytes 442376 | tf_op jit(solution)/shard_map/ppermute | solution.py:1238
  388.6 26.9 %collective-permute-start.40 = (bf16[2,2,128,768]{3,2,1,0:T(8,128)(2,1)}, bf16[2,2,128,768]{3,2,1,0:T(8,128)(2,1)}, u32[]{:S(2)}, u32[]{:S(2)}) collective-permute-start(bf16[2,2,128,768]{3,2,1,0:T(8,128)(2,1)} %dynamic-slice_bitcast_fusion), channel_id=1, source_target_pairs={{0,1},{1,0},{2,3},{3,2},{4,5},{5,4},{6,7},{7,6},{8,9},{9,8},{10,11... | collective-permute-start | bytes 2359304 | tf_op jit(solution)/shard_map/ppermute | solution.py:537
  390.1 110.5 %collective-permute-start.38 = (bf16[2,256,768]{2,1,0:T(8,128)(2,1)}, bf16[2,256,768]{2,1,0:T(8,128)(2,1)}, u32[]{:S(2)}, u32[]{:S(2)}) collective-permute-start(bf16[2,256,768]{2,1,0:T(8,128)(2,1)} %get-tuple-element.95), channel_id=1, source_target_pairs={{0,1},{1,0},{2,3},{3,2},{4,5},{5,4},{6,7},{7,6},{8,9},{9,8},{10,11... | collective-permute-start | bytes 2359304 | tf_op jit(solution)/shard_map/ppermute | solution.py:537
  391.5 71.2 %collective-permute-start.59 = (bf16[256,768]{1,0:T(8,128)(2,1)}, bf16[256,768]{1,0:T(8,128)(2,1)}, u32[]{:S(2)}, u32[]{:S(2)}) collective-permute-start(bf16[256,768]{1,0:T(8,128)(2,1)} %get-tuple-element.184), channel_id=1, source_target_pairs={{0,24},{1,25},{2,26},{3,27},{4,28},{5,29},{6,30},{7,31},{8,0},{9,1... | collective-permute-start | bytes 1179656 | tf_op jit(solution)/shard_map/ppermute | solution.py:1238
  417.9 44.9 %collective-permute-start.58 = (bf16[256,768]{1,0:T(8,128)(2,1)}, bf16[256,768]{1,0:T(8,128)(2,1)}, u32[]{:S(2)}, u32[]{:S(2)}) collective-permute-start(bf16[256,768]{1,0:T(8,128)(2,1)} %get-tuple-element.185), channel_id=1, source_target_pairs={{0,16},{1,17},{2,18},{3,19},{4,20},{5,21},{6,22},{7,23},{8,24},{9,... | collective-permute-start | bytes 1179656 | tf_op jit(solution)/shard_map/ppermute | solution.py:1238
  422.2 40.6 %collective-permute-start.57 = (bf16[256,768]{1,0:T(8,128)(2,1)}, bf16[256,768]{1,0:T(8,128)(2,1)}, u32[]{:S(2)}, u32[]{:S(2)}) collective-permute-start(bf16[256,768]{1,0:T(8,128)(2,1)} %get-tuple-element.186), channel_id=1, source_target_pairs={{0,8},{1,9},{2,10},{3,11},{4,12},{5,13},{6,14},{7,15},{8,16},{9,17... | collective-permute-start | bytes 1179656 | tf_op jit(solution)/shard_map/ppermute | solution.py:1238
  422.2 40.6 %collective-permute-start.41 = (bf16[2,128,768]{2,1,0:T(8,128)(2,1)}, bf16[2,128,768]{2,1,0:T(8,128)(2,1)}, u32[]{:S(2)}, u32[]{:S(2)}) collective-permute-start(bf16[2,128,768]{2,1,0:T(8,128)(2,1)} %fusion.43), channel_id=1, source_target_pairs={{0,2},{1,3},{2,0},{3,1},{4,6},{5,7},{6,4},{7,5},{8,10},{9,11},{10,... | collective-permute-start | bytes 1179656 | tf_op jit(solution)/shard_map/ppermute | solution.py:537
  503.4 25.4 %collective-permute-start.39 = (bf16[256,768]{1,0:T(8,128)(2,1)}, bf16[256,768]{1,0:T(8,128)(2,1)}, u32[]{:S(2)}, u32[]{:S(2)}) collective-permute-start(bf16[256,768]{1,0:T(8,128)(2,1)} %fusion.42), channel_id=1, source_target_pairs={{0,2},{1,3},{2,0},{3,1},{4,6},{5,7},{6,4},{7,5},{8,10},{9,11},{10,... | collective-permute-start | bytes 1179656 | tf_op jit(solution)/shard_map/ppermute | solution.py:537
  523.5 40.3 %collective-permute-start.71 = (bf16[96,2304]{1,0:T(8,128)(2,1)S(1)}, bf16[96,2304]{1,0:T(8,128)(2,1)S(1)}, u32[]{:S(2)}, u32[]{:S(2)}) collective-permute-start(bf16[96,2304]{1,0:T(8,128)(2,1)S(1)} %get-tuple-element.167), channel_id=1, source_target_pairs={{24,0},{4,12},{8,16},{20,28},{29,5},{1,9},{13,21},{17,25},{26,2},{... | collective-permute-start | bytes 1327112 | tf_op jit(solution)/shard_map/ppermute | solution.py:1210
  526.8 44.5 %collective-permute-start.70 = (bf16[96,2304]{1,0:T(8,128)(2,1)S(1)}, bf16[96,2304]{1,0:T(8,128)(2,1)S(1)}, u32[]{:S(2)}, u32[]{:S(2)}) collective-permute-start(bf16[96,2304]{1,0:T(8,128)(2,1)S(1)} %get-tuple-element.168), channel_id=1, source_target_pairs={{20,0},{0,12},{4,16},{16,28},{25,5},{29,9},{9,21},{13,25},{22,2},{... | collective-permute-start | bytes 1327112 | tf_op jit(solution)/shard_map/ppermute | solution.py:1210
  528.1 43.2 %collective-permute-start.69 = (bf16[96,2304]{1,0:T(8,128)(2,1)S(1)}, bf16[96,2304]{1,0:T(8,128)(2,1)S(1)}, u32[]{:S(2)}, u32[]{:S(2)}) collective-permute-start(bf16[96,2304]{1,0:T(8,128)(2,1)S(1)} %get-tuple-element.169), channel_id=1, source_target_pairs={{16,0},{28,12},{0,16},{12,28},{21,5},{25,9},{5,21},{9,25},{18,2},{... | collective-permute-start | bytes 1327112 | tf_op jit(solution)/shard_map/ppermute | solution.py:1210
  528.8 42.5 %collective-permute-start.68 = (bf16[96,2304]{1,0:T(8,128)(2,1)S(1)}, bf16[96,2304]{1,0:T(8,128)(2,1)S(1)}, u32[]{:S(2)}, u32[]{:S(2)}) collective-permute-start(bf16[96,2304]{1,0:T(8,128)(2,1)S(1)} %get-tuple-element.170), channel_id=1, source_target_pairs={{12,0},{24,12},{28,16},{8,28},{17,5},{21,9},{1,21},{5,25},{14,2},{... | collective-permute-start | bytes 1327112 | tf_op jit(solution)/shard_map/ppermute | solution.py:1210
  530.6 40.7 %collective-permute-start.67 = (bf16[96,2304]{1,0:T(8,128)(2,1)S(1)}, bf16[96,2304]{1,0:T(8,128)(2,1)S(1)}, u32[]{:S(2)}, u32[]{:S(2)}) collective-permute-start(bf16[96,2304]{1,0:T(8,128)(2,1)S(1)} %get-tuple-element.171), channel_id=1, source_target_pairs={{8,0},{20,12},{24,16},{4,28},{13,5},{17,9},{29,21},{1,25},{10,2},{... | collective-permute-start | bytes 1327112 | tf_op jit(solution)/shard_map/ppermute | solution.py:1210
  576.8 48.4 %collective-permute-start.73 = (bf16[96,2304]{1,0:T(8,128)(2,1)}, bf16[96,2304]{1,0:T(8,128)(2,1)S(1)}, u32[]{:S(2)}, u32[]{:S(2)}) collective-permute-start(bf16[96,2304]{1,0:T(8,128)(2,1)} %get-tuple-element.110), channel_id=1, source_target_pairs={{0,4},{12,16},{16,20},{28,0},{5,9},{9,13},{21,25},{25,29},{2,6},{1... | collective-permute-start | bytes 1327112 | tf_op jit(solution)/shard_map/ppermute | solution.py:1218
  578.1 53.4 %collective-permute-start.74 = (bf16[96,2304]{1,0:T(8,128)(2,1)}, bf16[96,2304]{1,0:T(8,128)(2,1)S(1)}, u32[]{:S(2)}, u32[]{:S(2)}) collective-permute-start(bf16[96,2304]{1,0:T(8,128)(2,1)} %get-tuple-element.111), channel_id=1, source_target_pairs={{0,8},{12,20},{16,24},{28,4},{5,13},{9,17},{21,29},{25,1},{2,10},{... | collective-permute-start | bytes 1327112 | tf_op jit(solution)/shard_map/ppermute | solution.py:1218
  579.4 54.2 %collective-permute-start.75 = (bf16[96,2304]{1,0:T(8,128)(2,1)}, bf16[96,2304]{1,0:T(8,128)(2,1)S(1)}, u32[]{:S(2)}, u32[]{:S(2)}) collective-permute-start(bf16[96,2304]{1,0:T(8,128)(2,1)} %get-tuple-element.112), channel_id=1, source_target_pairs={{0,12},{12,24},{16,28},{28,8},{5,17},{9,21},{21,1},{25,5},{2,14},{... | collective-permute-start | bytes 1327112 | tf_op jit(solution)/shard_map/ppermute | solution.py:1218
  580.1 54.3 %collective-permute-start.76 = (bf16[96,2304]{1,0:T(8,128)(2,1)}, bf16[96,2304]{1,0:T(8,128)(2,1)S(1)}, u32[]{:S(2)}, u32[]{:S(2)}) collective-permute-start(bf16[96,2304]{1,0:T(8,128)(2,1)} %get-tuple-element.113), channel_id=1, source_target_pairs={{0,16},{12,28},{16,0},{28,12},{5,21},{9,25},{21,5},{25,9},{2,18},{... | collective-permute-start | bytes 1327112 | tf_op jit(solution)/shard_map/ppermute | solution.py:1218
  580.8 63.2 %collective-permute-start.77 = (bf16[96,2304]{1,0:T(8,128)(2,1)}, bf16[96,2304]{1,0:T(8,128)(2,1)S(1)}, u32[]{:S(2)}, u32[]{:S(2)}) collective-permute-start(bf16[96,2304]{1,0:T(8,128)(2,1)} %get-tuple-element.114), channel_id=1, source_target_pairs={{0,20},{12,0},{16,4},{28,16},{5,25},{9,29},{21,9},{25,13},{2,22},{... | collective-permute-start | bytes 1327112 | tf_op jit(solution)/shard_map/ppermute | solution.py:1218
  625.3 33.2 %collective-permute-start.78 = (bf16[96,2304]{1,0:T(8,128)(2,1)S(1)}, bf16[96,2304]{1,0:T(8,128)(2,1)S(1)}, u32[]{:S(2)}, u32[]{:S(2)}) collective-permute-start(bf16[96,2304]{1,0:T(8,128)(2,1)S(1)} %copy-done.72), channel_id=1, source_target_pairs={{0,24},{12,4},{16,8},{28,20},{5,29},{9,1},{21,13},{25,17},{2,26},{... | collective-permute-start | bytes 1327112 | tf_op jit(solution)/shard_map/ppermute | solution.py:1218
  631.5 50.6 %collective-permute-start.79 = (bf16[96,2304]{1,0:T(8,128)(2,1)S(1)}, bf16[96,2304]{1,0:T(8,128)(2,1)S(1)}, u32[]{:S(2)}, u32[]{:S(2)}) collective-permute-start(bf16[96,2304]{1,0:T(8,128)(2,1)S(1)} %copy-done.71), channel_id=1, source_target_pairs={{0,28},{12,8},{16,12},{28,24},{5,1},{9,5},{21,17},{25,21},{2,30},{... | collective-permute-start | bytes 1327112 | tf_op jit(solution)/shard_map/ppermute | solution.py:1218
  686.0 15.3 %collective-permute-start.80 = (bf16[24,2304]{1,0:T(8,128)(2,1)}, bf16[24,2304]{1,0:T(8,128)(2,1)S(1)}, u32[]{:S(2)}, u32[]{:S(2)}) collective-permute-start(bf16[24,2304]{1,0:T(8,128)(2,1)} %get-tuple-element.225), channel_id=1, source_target_pairs={{0,2},{1,3},{2,0},{3,1},{4,6},{5,7},{6,4},{7,5},{8,10},{9,11},{10,... | collective-permute-start | bytes 331784 | tf_op jit(solution)/shard_map/ppermute | solution.py:537
  686.0 15.3 %collective-permute-start.82 = (bf16[24,2304]{1,0:T(8,128)(2,1)}, bf16[24,2304]{1,0:T(8,128)(2,1)S(1)}, u32[]{:S(2)}, u32[]{:S(2)}) collective-permute-start(bf16[24,2304]{1,0:T(8,128)(2,1)} %get-tuple-element.226), channel_id=1, source_target_pairs={{0,3},{1,2},{2,1},{3,0},{4,7},{5,6},{6,5},{7,4},{8,11},{9,10},{10,... | collective-permute-start | bytes 331784 | tf_op jit(solution)/shard_map/ppermute | solution.py:537
  (123 other events, 1519.2 us)
Sparse Core Ops, SparseCore 0:
  10.8 90.9 all-gather.6
  104.0 116.1 all-gather.4
  299.9 150.3 reduce-scatter.1

commit v2 on v1

--- a/solution.py
+++ b/solution.py
@@ -488,7 +488,6 @@
 FS = 4
 AXES = ("dp", "fsdp")
 LANES = 128
-SEQUENCES = 2
 VMEM_BYTES = 60 * 2**20
 LINE = 4
 OWNERS = ((0, 3, 4, 7), (1, 2, 5, 6), (0, 3, 4, 7), (1, 2, 5, 6, 4))
@@ -562,27 +561,15 @@
     return by_source(*got, index)
 
 
-class FsdpSum:
-    def __init__(self, keep, send, index):
-        self.place, self.keep = index // 2, keep
-        self.near = fsdp_hop(send, 1)
-
-    def cross(self):
-        both = self.keep.astype(jnp.float32) + self.near.astype(jnp.float32)
-        away = lax.dynamic_index_in_dim(both, 1 - self.place, 0, keepdims=False)
-        self.here = lax.dynamic_index_in_dim(both, self.place, 0, keepdims=False)
-        self.far = fsdp_hop(away.astype(self.keep.dtype), 2)
-        return self
-
-    def last(self):
-        return self.here + self.far.astype(jnp.float32)
-
-
-def by_core(blocks, index, *events):
-    if events:
-        blocks = after(blocks, *events)
-    pairs, core = blocks.reshape((2, 2) + blocks.shape[1:]), index % 2
-    return [lax.dynamic_index_in_dim(pairs, c, 1, keepdims=False) for c in (core, 1 - core)]
+def reduce_fsdp(blocks, index):
+    core, place = index % 2, index // 2
+    pairs = blocks.reshape((2, 2) + blocks.shape[1:])
+    send = lax.dynamic_index_in_dim(pairs, 1 - core, 1, keepdims=False)
+    keep = lax.dynamic_index_in_dim(pairs, core, 1, keepdims=False)
+    both = keep.astype(jnp.float32) + fsdp_hop(send, 1).astype(jnp.float32)
+    away = lax.dynamic_index_in_dim(both, 1 - place, 0, keepdims=False).astype(blocks.dtype)
+    here = lax.dynamic_index_in_dim(both, place, 0, keepdims=False)
+    return here + fsdp_hop(away, 2).astype(jnp.float32)
 
 
 def sum_everywhere(value):
@@ -790,8 +777,8 @@
 
 
 def middle_back_body(
-    index_ref, mid_ref, d_out_ref, d_sum_ref, gates_ref, routes_ref, att_ref, normed_ref, wout_ref, router_ref,
-    gain_ref, d_mid_ref, grad_wout_ref, grad_router_ref, grad_gain_ref, *d_att_refs,
+    mid_ref, d_out_ref, d_sum_ref, gates_ref, routes_ref, att_ref, normed_ref, wout_ref, router_ref,
+    gain_ref, d_mid_ref, d_att_ref, grad_wout_ref, grad_router_ref, grad_gain_ref,
 ):
     width = mid_ref.shape[1]
     gates = gates_ref[...]
@@ -822,33 +809,24 @@
     d_mid_ref[...] = d_mid
     d_branch = d_mid.astype(jnp.bfloat16)
     grad_wout_ref[...] = tn_dot(att_ref[...], d_branch).astype(jnp.bfloat16)
-    d_att = nt_dot(d_branch, wout_ref[...]).astype(jnp.bfloat16)
-    quarter = width // FS
-    for f in range(FS):
-        for step, d_att_ref in enumerate(d_att_refs):
-
-            @pl.when(index_ref[0] == f ^ step)
-            def _():
-                d_att_ref[...] = d_att[:, f * quarter : (f + 1) * quarter]
-
-
-def middle_backward(index, *operands):
+    d_att_ref[...] = nt_dot(d_branch, wout_ref[...]).astype(jnp.bfloat16)
+
+
+def middle_backward(*operands):
     count, width = operands[0].shape
-    vmem = pl.BlockSpec(memory_space=pltpu.VMEM)
     return kernel_call(
         middle_back_body,
-        [
+        (
             shape_of((count, width), jnp.float32),
+            shape_of((count, width)),
             shape_of((width, width)),
             shape_of((LANES, width), jnp.float32),
             shape_of((1, width), jnp.float32),
-        ]
-        + [shape_of((count, width // FS))] * FS,
+        ),
         4 * count * width * width,
         8e6,
-        in_specs=[pl.BlockSpec(memory_space=pltpu.SMEM)] + [vmem] * len(operands),
         name="middle_backward",
-    )(index, *operands)
+    )(*operands)
 
 
 def branch_step(normed_ref, turned_ref, d_out_ref, gate_column, weights, grads):
@@ -882,150 +860,98 @@
     return out, nt_dot(d_both, both_weight), d_gate
 
 
-def add_parts(step, totals, parts, first):
+def branch_body(
+    expert_ref, normed_ref, turned_ref, d_out_ref, *refs, routed, chained, last
+):
+    refs = list(refs)
+    gates_ref = refs.pop(0) if routed else None
+    first = [refs.pop(0) for _ in range(3 if routed else 2)] if chained else None
+    gate_ref, up_ref, down_ref, out_ref, back_ref = refs[:5]
+    slope_ref = refs[5] if routed and not last else None
+    grad_pair_ref, grad_down_ref = refs[6:8] if slope_ref is not None else refs[5:7]
+    totals = refs[-3:]
+    step = pl.program_id(0)
+    out, back, d_gate = branch_step(
+        normed_ref,
+        turned_ref,
+        d_out_ref,
+        gates_ref[...] if routed else None,
+        (jnp.concatenate([gate_ref[...], up_ref[...]], axis=1), down_ref[...]),
+        (grad_pair_ref, grad_down_ref),
+    )
+    parts = [out, back] + ([d_gate] if routed else [])
+
     @pl.when(step == 0)
     def _():
         for i, part in enumerate(parts):
-            totals[i][...] = part if first is None else first[i][...] + part
+            kept = chained and i < len(first)
+            totals[i][...] = first[i][...] + part if kept else part
 
     @pl.when(step > 0)
     def _():
         for i, part in enumerate(parts):
             totals[i][...] += part
 
-
-def shared_body(
-    normed_ref, turned_ref, d_out_ref, gate_ref, up_ref, down_ref, out_ref, back_ref, pair_ref,
-    grad_down_ref,
-):
-    out, back, _ = branch_step(
-        normed_ref,
-        turned_ref,
-        d_out_ref,
-        None,
-        (jnp.concatenate([gate_ref[...], up_ref[...]], axis=1), down_ref[...]),
-        (pair_ref, grad_down_ref),
-    )
-    add_parts(pl.program_id(0), (out_ref, back_ref), (out, back), None)
-
-
-def expert_body(
-    place_ref, normed_ref, turned_ref, d_out_ref, gates_ref, first_out_ref, first_back_ref, gate_ref,
-    up_ref, down_ref, out_keep, out_send, back_keep, back_send, pair_ref, down_keep, down_send,
-    out_total, back_total, slope_total, grad_down,
-):
-    step = pl.program_id(0)
-    expert, side = place_ref[0], place_ref[1]
-    out, back, d_gate = branch_step(
-        normed_ref,
-        turned_ref,
-        d_out_ref,
-        gates_ref[...],
-        (jnp.concatenate([gate_ref[...], up_ref[...]], axis=1), down_ref[...]),
-        (pair_ref, grad_down),
-    )
-    half = grad_down.shape[0] // 2
-    for mine in range(2):
-
-        @pl.when(side == mine)
-        def _():
-            down_keep[...] = grad_down[mine * half : (mine + 1) * half, :]
-            down_send[...] = grad_down[(1 - mine) * half : (2 - mine) * half, :]
-
-    add_parts(step, (out_total, back_total), (out, back), (first_out_ref, first_back_ref))
-    add_parts(step, (slope_total,), (d_gate,), None)
-
     @pl.when(step == pl.num_programs(0) - 1)
     def _():
-        width = out_total.shape[1]
-        block = out_keep.shape[1]
-        local = block // SEQUENCES
-        slopes = slope_total[...]
+        if not last:
+            out_ref[...] = totals[0][...]
+            back_ref[...] = totals[1][...]
+            if routed:
+                slope_ref[...] = totals[2][...]
+            return
+        width = out_ref.shape[1]
+        out_ref[...] = totals[0][...].astype(jnp.bfloat16)
+        back_ref[:, :width] = totals[1][...].astype(jnp.bfloat16)
+        slopes = totals[2][...]
         high = slopes.astype(jnp.bfloat16).astype(jnp.float32)
         lane = lax.broadcasted_iota(jnp.int32, (slopes.shape[0], LANES), 1)
-        table = jnp.where(lane == expert, high, 0.0)
-        table = jnp.where(lane == expert + LANES // 2, slopes - high, table).astype(jnp.bfloat16)
-        for f in range(FS):
-            x, core = divmod(f, 2)
-            for r in range(SEQUENCES):
-                start = (r * FS + f) * local
-                here, there = slice(start, start + local), slice(r * local, (r + 1) * local)
-
-                def write(out_ref, back_ref):
-                    out_ref[x, there, :] = out_total[here, :].astype(jnp.bfloat16)
-                    back_ref[x, there, :width] = back_total[here, :].astype(jnp.bfloat16)
-                    back_ref[x, there, width:] = table[here, :]
-
-                pl.when(expert % 2 == core)(functools.partial(write, out_keep, back_keep))
-                pl.when(expert % 2 != core)(functools.partial(write, out_send, back_send))
-
-
-def once(shape):
-    return pl.BlockSpec(shape, lambda *_: (0,) * len(shape), pipeline_mode=pl.Buffered(1))
-
-
-def shared_branch(normed, turned, d_out, both, down, tile):
+        table = jnp.where(lane == expert_ref[0], high, 0.0)
+        table = jnp.where(lane == expert_ref[0] + LANES // 2, slopes - high, table)
+        back_ref[:, width:] = table.astype(jnp.bfloat16)
+
+
+def branch(expert, normed, turned, d_out, gates, first, weights, blocks, last, name):
+    (gate, gate_spec), (up, up_spec), down = weights
     count, width = normed.shape
-    hidden = down.shape[0]
-    tiles = hidden // tile
-    outs = [
-        shape_of((count, width), jnp.float32),
-        shape_of((count, width), jnp.float32),
-        shape_of((width, 2 * hidden)),
-        shape_of((hidden, width)),
-    ]
+    start, end, tile = blocks
+    routed, chained = gates is not None, first is not None
+    hidden = (end - start) * tile
+    once = lambda shape: pl.BlockSpec(
+        shape, lambda *_: (0,) * len(shape), pipeline_mode=pl.Buffered(1)
+    )
+    operands = [expert, normed, turned, d_out]
+    if routed:
+        operands.append(gates)
+    if chained:
+        operands += first
+    full = [once(array.shape) for array in operands[1:]]
+    outs = [shape_of((count, width), jnp.float32), shape_of((count, width), jnp.float32)]
+    if routed and not last:
+        outs.append(shape_of((count, 1), jnp.float32))
+    if last:
+        outs = [shape_of((count, width)), shape_of((count, width + LANES))]
     return kernel_call(
-        shared_body,
-        outs,
+        functools.partial(branch_body, routed=routed, chained=chained, last=last),
+        outs + [shape_of((width, 2 * hidden)), shape_of((hidden, width))],
         18 * count * width * hidden,
-        12 * width * hidden + 12 * count * width,
-        grid=(tiles,),
-        in_specs=[once(normed.shape), once(turned.shape), once(d_out.shape)]
-        + [
-            pl.BlockSpec((width, tile), lambda j: (0, j)),
-            pl.BlockSpec((width, tile), lambda j: (0, tiles + j)),
-            pl.BlockSpec((tile, width), lambda j: (j, 0)),
-        ],
-        out_specs=[once(out.shape) for out in outs[:2]]
+        12 * width * hidden + 16 * count * width,
+        grid=(end - start,),
+        in_specs=[pl.BlockSpec(memory_space=pltpu.SMEM)]
+        + full
+        + [gate_spec, up_spec, pl.BlockSpec((tile, width), lambda j: (start + j, 0))],
+        out_specs=[once(out.shape) for out in outs]
         + [
             pl.BlockSpec((width, 2 * tile), lambda j: (0, j)),
             pl.BlockSpec((tile, width), lambda j: (j, 0)),
         ],
-        name="shared_branch",
-    )(normed, turned, d_out, both, both, down)
-
-
-def expert_branch(place, normed, turned, d_out, gates, first_out, first_back, gate_up, down, tile):
-    count, width = normed.shape
-    hidden = down.shape[0]
-    operands = [normed, turned, d_out, gates, first_out, first_back]
-    split = lambda columns: [shape_of((2, count // FS, columns))] * 2
-    outs = split(width) + split(width + LANES)
-    halves = shape_of((hidden // tile, tile // 2, width))
-    half_spec = pl.BlockSpec((None, tile // 2, width), lambda j: (j, 0, 0))
-    return kernel_call(
-        expert_body,
-        outs + [shape_of((width, 2 * hidden)), halves, halves],
-        18 * count * width * hidden,
-        12 * width * hidden + 16 * count * width,
-        grid=(hidden // tile,),
-        in_specs=[pl.BlockSpec(memory_space=pltpu.SMEM)]
-        + [once(array.shape) for array in operands]
-        + [
-            pl.BlockSpec((None, width, tile), lambda j: (0, 0, j)),
-            pl.BlockSpec((None, width, tile), lambda j: (1, 0, j)),
-            pl.BlockSpec((tile, width), lambda j: (j, 0)),
-        ],
-        out_specs=[once(out.shape) for out in outs]
-        + [pl.BlockSpec((width, 2 * tile), lambda j: (0, j)), half_spec, half_spec],
         scratch_shapes=[
             pltpu.VMEM((count, width), jnp.float32),
             pltpu.VMEM((count, width), jnp.float32),
             pltpu.VMEM((count, 1), jnp.float32),
-            pltpu.VMEM((tile, width), jnp.bfloat16),
         ],
-        name="expert_branch",
-    )(place, *operands, gate_up, gate_up, down)
+        name=name,
+    )(*operands, gate, up, down)
 
 
 def orthogonal_body(info_ref, *refs):
@@ -1284,26 +1210,21 @@
 class Reduce:
     def __init__(self, grads, place):
         _, self.side, self.level = place
-        self.grads = grads
+        rows, columns = grads.shape
+        self.grads = grads.reshape(LINE, 2, rows // DP, columns)
 
     def pick(self, array, i, axis=0):
         return lax.dynamic_index_in_dim(array, i, axis, keepdims=False)
 
     def cross(self, *events):
-        rows, columns = self.grads.shape
-        grads = self.grads.reshape(LINE, 2, rows // DP, columns)
-        if events:
-            grads = after(grads, *events)
-        self.mine = self.pick(grads, self.side, 1)
-        self.sent = self.pick(grads, 1 - self.side, 1)
-        self.got = pair_hop(self.sent)
+        grads = after(self.grads, *events) if events else self.grads
+        self.got = pair_hop(self.pick(grads, 1 - self.side, 1))
         return self.got
 
     def along(self, *events):
         got = after(self.got, *events) if events else self.got
-        mine = self.mine
+        mine = self.pick(self.grads, self.side, 1)
         both = (mine.astype(jnp.float32) + got.astype(jnp.float32)).astype(mine.dtype)
-        self.both = both
         at = lambda step: self.pick(both, lax.rem(self.level + step, LINE))
         self.parts = [at(0)] + [line_hop(at(step), step) for step in range(1, LINE)]
         return self.parts[1]
@@ -1423,25 +1344,33 @@
         gain_two,
     )
     gate_column = lax.dynamic_slice_in_dim(gates_all, index, 1, 1)
-    tile = 2 * e_down.shape[1]
+    expert = index.reshape(1)
+    tile = min(512, ff_part)
+    shared_tiles = ff_part // tile
+    columns_at = lambda start: pl.BlockSpec((width, tile), lambda j: (0, start + j))
+    first_out, first_back, grad_pair, grad_down = branch(
+        expert, normed_all, turned_all, d_out_all, None, None,
+        ((w_shared, columns_at(0)), (w_shared, columns_at(shared_tiles)), down_copy),
+        (0, shared_tiles, tile), False, "shared_branch",
+    )
+    part_at = lambda start, half: pl.BlockSpec(
+        (None, width, tile), lambda j: (half, 0, start + j)
+    )
     ff_width = e_gate_up.shape[3]
-    first_out, first_back, grad_pair, grad_down = shared_branch(
-        normed_all, turned_all, d_out_all, w_shared, down_copy, tile
-    )
     sum_shared = Reduce(
         jnp.concatenate([grad_pair, grad_down.reshape(width, fold_down)], axis=1), place
     )
     sum_shared.cross()
-    out_keep, out_send, back_keep, back_send, grad_pairs, edown_keep, edown_send = expert_branch(
-        jnp.stack([index, dp_index % 2]), after(normed_all, sum_shared.got), turned_all, d_out_all,
-        gate_column, first_out, first_back, gate_up_copy, edown_copy, tile,
+    out_part, message, grad_pairs, grad_edown = branch(
+        expert, after(normed_all, sum_shared.got), turned_all, d_out_all, gate_column,
+        [first_out, first_back, jnp.zeros((count, 1), jnp.float32)],
+        ((gate_up_copy, part_at(0, 0)), (gate_up_copy, part_at(0, 1)), edown_copy),
+        (0, ff_width // tile, tile), True, "expert_branch",
     )
 
     sum_shared.along()
     part_pairs = lax.psum_scatter(grad_pairs, "dp", scatter_dimension=0, tiled=True)
-    d_sum = FsdpSum(back_keep, after(back_send, *sum_shared.parts[1:]), index)
-    sum_edown = Reduce(None, place)
-    sum_edown.mine, sum_edown.got = edown_keep, pair_hop(edown_send)
+    sum_edown = Reduce(grad_edown, place)
 
     def by_place(values):
         return values.reshape(rows, FS, local_len, values.shape[-1]).transpose(1, 0, 2, 3)
@@ -1452,34 +1381,33 @@
         )
         return part.reshape(rows * local_len, values.shape[-1])
 
-    d_sum = d_sum.cross().last().reshape(rows * local_len, width + LANES)
+    d_sum = reduce_fsdp(by_place(after(message, *sum_shared.parts[1:])), index)
+    d_sum = d_sum.reshape(rows * local_len, width + LANES)
+    sum_edown.cross()
     mid = own_rows(mid_all)
     d_out = own_rows(d_out_all)
-    d_mid, grad_wout, grad_router, grad_gain_two, *d_att = middle_backward(
-        index.reshape(1), mid, d_out, d_sum, own_rows(gates_all),
+    d_mid, d_att, grad_wout, grad_router, grad_gain_two = middle_backward(
+        mid, d_out, d_sum, own_rows(gates_all),
         routes.reshape(rows * local_len, -1), own_rows(attended_all), own_rows(normed_all), w_out,
         w_route, gain_two,
     )
-    d_att = [block.reshape(rows, local_len, quarter) for block in d_att]
-    d_att = [d_att[0]] + [fsdp_hop(d_att[step], step) for step in range(1, FS)]
+    d_att = d_att.reshape(rows, local_len, FS, quarter).transpose(2, 0, 1, 3)
+    d_att = jnp.concatenate(exchange_fsdp(d_att, index), axis=1)
     grad_wout = grad_wout.reshape(DP, FS, block_rows, width).transpose(1, 0, 2, 3)
-    sum_wout = FsdpSum(*by_core(grad_wout, index, d_att[1]), index).cross()
-    grad_wout = sum_wout.last().astype(bf16).reshape(width, fold_out)
-    d_att = jnp.concatenate(by_source(*d_att, index), axis=1)
+    grad_wout = reduce_fsdp(grad_wout, index).astype(bf16).reshape(width, fold_out)
     grad_qkv, back_part = attention_backward(
-        normed_one, qkv, probs, after(d_att, sum_wout.far), w_qkv, cosine, sine
+        normed_one, qkv, probs, after(d_att, grad_wout, sum_edown.got), w_qkv, cosine, sine
     )
     sum_last = Reduce(jnp.concatenate([grad_qkv, grad_wout], axis=1), place)
     sum_last.cross()
     sum_last.along()
-    sum_edown.along(sum_last.both)
+    sum_edown.along(sum_last.got)
 
     split_pair = lambda part, half: part.reshape(part.shape[0], -1, 2, tile)[:, :, half].reshape(
         part.shape[0], -1
     )
     part_shared = sum_shared.last()
     part_down = part_shared[:, 2 * ff_part :].reshape(down_rows, width)
-    raw_pairs = part_pairs
     part_pairs = part_pairs.astype(jnp.float32)
     part_gate_up = jnp.stack([split_pair(part_pairs, half) for half in range(2)])
     part_last = sum_last.last()
@@ -1495,17 +1423,37 @@
     )
     part_dense = part_near.astype(bf16)
 
-    out_sum = FsdpSum(out_keep, after(out_send, sum_last.got), index).cross().last()
-    out_sum = out_sum.reshape(rows * local_len, width)
+    out_sum = reduce_fsdp(by_place(out_part), index).reshape(rows * local_len, width)
     valid = (
         (index * local_len + jnp.arange(local_len))[None, :] < lengths[:, None]
     ).astype(jnp.float32)
     output = ((mid + out_sum).reshape(tokens.shape) * valid[..., None]).astype(bf16)
-    d_one = FsdpSum(*by_core(by_place(back_part), index, sum_last.sent), index).cross().last()
-    d_one = d_one.reshape(tokens.shape)
+    d_one = reduce_fsdp(by_place(back_part), index).reshape(tokens.shape)
     scaled_one, inverse_one = statistics(tokens.astype(jnp.float32))
     d_in, grad_gain_one = norm_back(d_one, scaled_one, inverse_one, gain_one)
     d_tokens = (d_mid.reshape(tokens.shape) + d_in).astype(bf16)
+
+    columns = (0, device_index * block_rows)
+    zeros = jnp.zeros((8 - experts - 2, width), jnp.float32)
+    small = jnp.concatenate(
+        [grad_router[:experts], grad_gain_one[None], grad_gain_two, zeros], axis=0
+    )
+    old = jnp.concatenate(
+        [MUON_DECAY * mom_router.T, GAIN_DECAY * gain_moms, zeros[:, :block_rows]], axis=0
+    )
+    small = small + lax.dynamic_update_slice(jnp.zeros_like(small), old, columns)
+    small = sum_everywhere(small)
+    own_small = lax.dynamic_slice(small, columns, (8, block_rows))
+    new_mom_router = own_small[:experts].T
+    new_gain_moms = own_small[experts : experts + 2]
+    gain_rate = 0.1 / math.sqrt(count * DP)
+    new_gains = gains - gain_rate * new_gain_moms
+    orth_router = orthogonal_router(
+        jnp.concatenate([small[:experts], jnp.zeros((LANES - experts, width), jnp.float32)], axis=0)
+    )
+    new_router = w_router - ROUTER_RATE * lax.dynamic_slice(
+        orth_router, columns, (experts, block_rows)
+    ).T
 
     old_near = exchange_fsdp(by_columns(after(mom_dense, normed_all).astype(bf16)), index)
     old_near = jnp.concatenate(old_near, axis=0).astype(jnp.float32)
@@ -1537,15 +1485,14 @@
     stripe = lambda block: jnp.pad(block, ((0, 0), (0, 3 * quarter - block.shape[1])))
     stripes = [near[:, spots[i] : spots[i + 1]] for i in range(3)]
     stripes.append(near_out.reshape(folds, fold_out))
-    stripes = after(jnp.stack([stripe(block) for block in stripes]), *sum_edown.parts[1:])
-    got = exchange_fsdp(stripes, index)
+    got = exchange_fsdp(jnp.stack([stripe(block) for block in stripes]), index)
     whole_out = jnp.concatenate(
         [block[:, :fold_out].reshape(block_rows, width) for block in got], axis=0
     )
     dense_block = jnp.where(index == FS - 1, pad(whole_out), jnp.concatenate(got, axis=1))
-    low_experts = new_e_mom_gate_up[0].astype(bf16)
+    low_experts = after(new_e_mom_gate_up[0].astype(bf16), orth_router)
     wide = [pad(low_experts[0]), pad(low_experts[1]), dense_block]
-    low_down = after(new_mom_down.astype(bf16), sum_last.got)
+    low_down = new_mom_down.astype(bf16)
     column_pairs = lambda step, back: [
         (d * FS + DOWN_COLUMN, d * FS + (DOWN_COLUMN ^ step))[:: 1 if back else -1]
         for d in range(DP)
@@ -1560,35 +1507,13 @@
         axis=0,
     )
     talls = [fold_tall(new_e_mom_down[0].astype(bf16), folds, length), fold_tall(down_block, folds, length)]
-    arrived = to_owners(jnp.stack(wide + talls), OWNERS, dp_index, index)
+    shards = to_owners(jnp.stack(wide + talls), OWNERS, dp_index, index)
     kinds = np.zeros((FS, DP), np.int32)
     for f in range(FS):
         for slot, d in enumerate(OWNERS[f]):
             kinds[f, d] = 2 if slot in TALL_SLOTS else 1
     info = jnp.stack([jnp.asarray(kinds)[index, dp_index], dp_index.astype(jnp.int32)])
-    shards = orthogonal_shards(info, arrived, width)
-    columns = (0, device_index * block_rows)
-    zeros = jnp.zeros((8 - experts - 2, width), jnp.float32)
-    small = jnp.concatenate(
-        [grad_router[:experts], grad_gain_one[None], grad_gain_two, zeros], axis=0
-    )
-    old = jnp.concatenate(
-        [MUON_DECAY * mom_router.T, GAIN_DECAY * gain_moms, zeros[:, :block_rows]], axis=0
-    )
-    small = small + lax.dynamic_update_slice(jnp.zeros_like(small), old, columns)
-    small = sum_everywhere(after(small, sum_last.both))
-    own_small = lax.dynamic_slice(small, columns, (8, block_rows))
-    new_mom_router = own_small[:experts].T
-    new_gain_moms = own_small[experts : experts + 2]
-    gain_rate = 0.1 / math.sqrt(count * DP)
-    new_gains = gains - gain_rate * new_gain_moms
-    orth_router = orthogonal_router(
-        jnp.concatenate([after(small, *shards)[:experts], jnp.zeros((LANES - experts, width), jnp.float32)], axis=0)
-    )
-    new_router = w_router - ROUTER_RATE * lax.dynamic_slice(
-        orth_router, columns, (experts, block_rows)
-    ).T
-
+    shards = orthogonal_shards(info, shards, width)
     orth_gate, orth_up, orth_block, orth_edown, orth_down_block = from_owners(
         shards, OWNERS, dp_index, index
     )

time: 720 us -> 681 us (0.946)
  local copies, waits for them, and re-layouts: 135 us -> 108 us
  other arithmetic: 77.6 us -> 66.4 us
  starting transfers between devices: 119 us -> 129 us
  waiting for transfers between devices: 234 us -> 225 us
    ppermute x15, waiting for transfers between devices: 64.9 us -> 20.4 us  [line_hop(): return lax.ppermute(value, AXES, pairs)]
    ppermute x15, starting transfers between devices: 25.6 us -> 41.6 us  [line_hop(): return lax.ppermute(value, AXES, pairs)]
    ppermute x7, waiting for transfers between devices: 79.9 us -> 94.8 us  [from_owners(): lax.ppermute(block, AXES, owner_pairs(owners, step, True))]
    ppermute x5, waiting for transfers between devices: 35.3 us -> 49.2 us  [pair_hop(): return lax.ppermute(value, AXES, pairs)]
    ppermute x41, waiting for transfers between devices: 20.5 us -> 34.3 us  [fsdp_hop(): return lax.ppermute(value, AXES, pairs)]
    another operation x8, local copies, waits for them, and re-layouts: 12.1 us -> 0.66 us  [split_plan(): jnp.stack([part.reshape(block_rows, DP, down_rows) for part in parts], ax...]
    ppermute x41, starting transfers between devices: 45.2 us -> 33.9 us  [fsdp_hop(): return lax.ppermute(value, AXES, pairs)]
    ppermute x7, waiting for transfers between devices: 29.7 us -> 21.8 us  [to_owners(): lax.ppermute(block, AXES, owner_pairs(owners, step, False))]
  transfers between devices with their start and end apart: 89 -> 89, of which waited for: 28 -> 26; matrix products, arithmetic and copies ran while one was open for 27% -> 22% of each run, Pallas kernels for 15% -> 16%
where the time goes in v2:
time: 681 us; the launch traced here: 674 us
  waiting for transfers between devices  225 us (33%)
  starting transfers between devices  129 us (19%)
  Pallas kernels  111 us (16%)
  local copies, waits for them, and re-layouts  108 us (16%)
  other arithmetic  66.4 us (10%)
  between operations  34.6 us (5%)
    ppermute x7, waiting for transfers between devices, from_owners(): lax.ppermute(block, AXES, owner_pairs(owners, step, True))  94.8 us
    pallas_call x2, Pallas kernels, branch(): kernel_call(functools.partial(branch_body, routed=routed, chained=chained...  56.3 us
    ppermute x5, waiting for transfers between devices, pair_hop(): return lax.ppermute(value, AXES, pairs)  49.2 us
    ppermute x15, starting transfers between devices, line_hop(): return lax.ppermute(value, AXES, pairs)  41.6 us
    ppermute x41, waiting for transfers between devices, fsdp_hop(): return lax.ppermute(value, AXES, pairs)  34.3 us
    ppermute x41, starting transfers between devices, fsdp_hop(): return lax.ppermute(value, AXES, pairs)  33.9 us
    ppermute x7, waiting for transfers between devices, to_owners(): lax.ppermute(block, AXES, owner_pairs(owners, step, False))  21.8 us
    ppermute x7, starting transfers between devices, to_owners(): lax.ppermute(block, AXES, owner_pairs(owners, step, False))  21.6 us
  transfers between devices with their start and end apart: 89, of which 26 were waited for; matrix products, arithmetic and copies ran while one was open for 22% of the time, Pallas kernels for 16%

profile of v2, /device:TPU:15, one launch (start us, length us, event | category | flops | bytes accessed | tf_op | source)
XLA Modules:
  0.0 673.7 jit_solution(2578503795402333837)
XLA Ops:
  29.1 9.5 %collective-permute-done.8.refs_3_ = bf16[96,896]{1,0:T(8,128)(2,1)S(1)} collective-permute-done((bf16[96,896]{1,0:T(8,128)(2,1)S(1)}, bf16[96,896]{1,0:T(8,128)(2,1)S(1)}, u32[]{:S(2)}, u32[]{:S(2)}) %collective-permute-start.8) | collective-permute-done | bytes 172064 | tf_op jit(solution)/shard_map/ppermute | solution.py:1164
  39.9 4.6 collective-permute-done.7.refs_2_
  45.3 3.2 collective-permute-done.6.refs_1_
  75.3 4.0 collective-permute-start.18
  79.3 7.4 %collective-permute-done = bf16[2,128,896]{2,1,0:T(8,128)(2,1)S(1)} collective-permute-done((bf16[2,128,896]{2,1,0:T(8,128)(2,1)}, bf16[2,128,896]{2,1,0:T(8,128)(2,1)S(1)}, u32[]{:S(2)}, u32[]{:S(2)}) %collective-permute-start) | collective-permute-done | bytes 458784 | tf_op jit(solution)/shard_map/ppermute | solution.py:536
  86.7 2.4 collective-permute-start.16
  90.9 2.7 place_rows.2
  104.7 9.0 %attention_forward.1 = (bf16[768,1024]{1,0:T(8,128)(2,1)}, bf16[2,512,576]{2,1,0:T(8,128)(2,1)}, bf16[2,3,512,512]{3,2,1,0:T(8,128)(2,1)}, bf16[2,512,192]{2,1,0:T(8,128)(2,1)}) custom-call(s32[2]{0:T(128)} %lengths_ref.1, bf16[2,512,768]{2,1,0:T(8,128)(2,1)} %slice.363.x_ref, f32[1,768]{1,0:T(1,128)} %get-tuple-element.274.gain_ref, ...), custom_call_target="tpu_custom_call" | custom-call | flops 6000000000 | bytes 12000000 | tf_op jit(solution)/shard_map/attention_forward/pallas_call | solution.py:632
  121.1 6.0 collective-permute-done.10
  133.1 17.7 %collective-permute-done.19.refs_4_ = bf16[4,96,1536]{2,1,0:T(8,128)(2,1)} collective-permute-done((bf16[4,96,1536]{2,1,0:T(8,128)(2,1)S(1)}, bf16[4,96,1536]{2,1,0:T(8,128)(2,1)}, u32[]{:S(2)}, u32[]{:S(2)}) %collective-permute-start.19) | collective-permute-done | bytes 1179680 | tf_op jit(solution)/shard_map/ppermute | solution.py:1169
  150.7 3.2 place_rows.3
  154.0 2.7 slice.378.refs_0_.refs_1_
  163.2 7.4 %middle_forward.1 = (f32[1024,768]{1,0:T(8,128)}, bf16[1024,768]{1,0:T(8,128)(2,1)}, bf16[768,1024]{1,0:T(8,128)(2,1)}, f32[1024,128]{1,0:T(8,128)}) custom-call(bf16[1024,768]{1,0:T(8,128)(2,1)} %bitcast.474, bf16[1024,768]{1,0:T(8,128)(2,1)} %bitcast.477, s32[1024,128]{1,0:T(8,128)} %bitcast_convert_fusion.routes_ref, bf16[768,768]{1,0:T(8,128)(2,1)} %bitcast.472, ...), custom_call_target="tpu_custom_call" | custom-call | flops 1207959552 | bytes 12000000 | tf_op jit(solution)/shard_map/middle_forward/pallas_call | solution.py:750
  170.7 12.9 %shared_branch.1 = (f32[1024,768]{1,0:T(8,128)}, f32[1024,768]{1,0:T(8,128)}, bf16[768,1024]{1,0:T(8,128)(2,1)}, bf16[512,768]{1,0:T(8,128)(2,1)}) custom-call(s32[1]{0:T(128)} %bitcast.32.expert_ref, bf16[1024,768]{1,0:T(8,128)(2,1)} %get-tuple-element.63.normed_ref, bf16[768,1024]{1,0:T(8,128)(2,1)} %get-tuple-element.59.turned_ref, ...), custom_call_target="tpu_custom_call" | custom-call | flops 7247757312 | bytes 17301504 | tf_op jit(solution)/shard_map/shared_branch/pallas_call | solution.py:934
  189.5 2.9 collective-permute-start.56
  198.6 21.2 %collective-permute-done.26 = bf16[4,96,1536]{2,1,0:T(8,128)(2,1)} collective-permute-done((bf16[4,96,1536]{2,1,0:T(8,128)(2,1)}, bf16[4,96,1536]{2,1,0:T(8,128)(2,1)}, u32[]{:S(2)}, u32[]{:S(2)}) %collective-permute-start.26) | collective-permute-done | bytes 1179680 | tf_op jit(solution)/shard_map/ppermute | solution.py:1169
  222.5 2.4 collective-permute-start.30
  227.8 43.4 %expert_branch.1 = (bf16[1024,768]{1,0:T(8,128)(2,1)}, bf16[1024,896]{1,0:T(8,128)(2,1)}, bf16[768,4096]{1,0:T(8,128)(2,1)}, bf16[2048,768]{1,0:T(8,128)(2,1)}) custom-call(s32[1]{0:T(128)} %bitcast.32.expert_ref, bf16[1024,768]{1,0:T(8,128)(2,1)} %get-tuple-element.63.normed_ref, bf16[768,1024]{1,0:T(8,128)(2,1)} %get-tuple-element.59.turned_ref, ...), custom_call_target="tpu_custom_call" | custom-call | flops 28991029248 | bytes 31457280 | tf_op jit(solution)/shard_map/expert_branch/pallas_call | solution.py:934
  278.9 3.7 constant_dynamic-slice_fusion.3
  282.6 2.7 copy.144
  295.2 3.6 collective-permute-done.28
  298.8 2.5 fusion.30
  301.3 7.3 %collective-permute-done.33 = bf16[2,128,896]{2,1,0:T(8,128)(2,1)S(1)} collective-permute-done((bf16[2,128,896]{2,1,0:T(8,128)(2,1)S(1)}, bf16[2,128,896]{2,1,0:T(8,128)(2,1)S(1)}, u32[]{:S(2)}, u32[]{:S(2)}) %collective-permute-start.33) | collective-permute-done | bytes 458784 | tf_op jit(solution)/shard_map/ppermute | solution.py:536
  309.7 5.2 middle_backward.1
  321.4 4.4 collective-permute-done.36
  326.7 10.3 %collective-permute-done.37 = bf16[4,256,768]{1,2,0:T(8,128)(2,1)} collective-permute-done((bf16[4,256,768]{1,2,0:T(8,128)(2,1)}, bf16[4,256,768]{1,2,0:T(8,128)(2,1)}, u32[]{:S(2)}, u32[]{:S(2)}) %collective-permute-start.37) | collective-permute-done | bytes 1572896 | tf_op jit(solution)/shard_map/ppermute | solution.py:1169
  337.0 14.7 %attention_backward.1 = (bf16[768,576]{1,0:T(8,128)(2,1)}, bf16[2,512,768]{2,1,0:T(8,128)(2,1)}) custom-call(bf16[768,1024]{1,0:T(8,128)(2,1)} %get-tuple-element.71.normed_ref, bf16[2,512,576]{2,1,0:T(8,128)(2,1)} %get-tuple-element.72.qkv_ref, bf16[2,3,512,512]{3,2,1,0:T(8,128)(2,1)} %get-tuple-element.73.prob_ref, ...), custom_call_target="tpu_custom_call" | custom-call | flops 8000000000 | bytes 12000000 | tf_op jit(solution)/shard_map/attention_backward/pallas_call | solution.py:701
  362.9 2.8 collective-permute-start.46
  377.3 3.6 collective-permute-done.39
  403.3 7.3 %collective-permute-start.49 = (bf16[96,768]{1,0:T(8,128)(2,1)S(1)}, bf16[96,768]{1,0:T(8,128)(2,1)S(1)}, u32[]{:S(2)}, u32[]{:S(2)}) collective-permute-start(bf16[96,768]{1,0:T(8,128)(2,1)S(1)} %get-tuple-element.189), channel_id=1, source_target_pairs={{0,16},{1,17},{2,18},{3,19},{4,20},{5,21},{6,22},{7,23},{8,24},{9,... | collective-permute-start | bytes 442376 | tf_op jit(solution)/shard_map/ppermute | solution.py:1164
  415.7 2.8 collective-permute-done.44
  418.5 14.2 %collective-permute-start.62 = (bf16[256,768]{0,1:T(8,128)(2,1)}, bf16[256,768]{0,1:T(8,128)(2,1)}, u32[]{:S(2)}, u32[]{:S(2)}) collective-permute-start(bf16[256,768]{0,1:T(8,128)(2,1)} %get-tuple-element.165), channel_id=1, source_target_pairs={{0,24},{1,25},{2,26},{3,27},{4,28},{5,29},{6,30},{7,31},{8,0},{9,1... | collective-permute-start | bytes 1179656 | tf_op jit(solution)/shard_map/ppermute | solution.py:1164
  433.6 8.6 %orthogonal_router.1 = f32[128,768]{1,0:T(8,128)} custom-call(f32[128,768]{1,0:T(8,128)} %concatenate.131.matrix_ref), custom_call_target="tpu_custom_call" | custom-call | flops 2000000000 | bytes 1000000 | tf_op jit(solution)/shard_map/orthogonal_router/pallas_call | solution.py:1106
  454.7 3.3 collective-permute-start.59
  471.7 2.4 fusion.68
  474.1 2.7 reshape.575
  476.8 4.4 slice_reduce_fusion.1
  482.3 2.8 convert_bitcast_fusion
  490.2 5.9 collective-permute-start.71
  504.4 7.3 %collective-permute-start.67 = (bf16[96,2304]{1,0:T(8,128)(2,1)S(1)}, bf16[96,2304]{1,0:T(8,128)(2,1)}, u32[]{:S(2)}, u32[]{:S(2)}) collective-permute-start(bf16[96,2304]{1,0:T(8,128)(2,1)S(1)} %get-tuple-element.151), channel_id=1, source_target_pairs={{8,0},{20,12},{24,16},{4,28},{13,5},{17,9},{29,21},{1,25},{10,2},{... | collective-permute-start | bytes 1327112 | tf_op jit(solution)/shard_map/ppermute | solution.py:1136
  511.7 19.2 %collective-permute-done.71.refs_6_ = bf16[96,2304]{1,0:T(8,128)(2,1)} collective-permute-done((bf16[96,2304]{1,0:T(8,128)(2,1)}, bf16[96,2304]{1,0:T(8,128)(2,1)}, u32[]{:S(2)}, u32[]{:S(2)}) %collective-permute-start.71) | collective-permute-done | bytes 442400 | tf_op jit(solution)/shard_map/ppermute | solution.py:1136
  535.1 2.6 collective-permute-done.70.refs_5_
  538.4 4.0 orthogonal_shards.1
  548.9 45.5 %collective-permute-done.73 = bf16[96,2304]{1,0:T(8,128)(2,1)S(1)} collective-permute-done((bf16[96,2304]{1,0:T(8,128)(2,1)}, bf16[96,2304]{1,0:T(8,128)(2,1)S(1)}, u32[]{:S(2)}, u32[]{:S(2)}) %collective-permute-start.73) | collective-permute-done | bytes 442400 | tf_op jit(solution)/shard_map/ppermute | solution.py:1144
  597.2 11.3 %collective-permute-done.77 = bf16[96,2304]{1,0:T(8,128)(2,1)S(1)} collective-permute-done((bf16[96,2304]{1,0:T(8,128)(2,1)}, bf16[96,2304]{1,0:T(8,128)(2,1)S(1)}, u32[]{:S(2)}, u32[]{:S(2)}) %collective-permute-start.77) | collective-permute-done | bytes 442400 | tf_op jit(solution)/shard_map/ppermute | solution.py:1144
  608.5 15.3 %collective-permute-done.78 = bf16[96,2304]{1,0:T(8,128)(2,1)S(1)} collective-permute-done((bf16[96,2304]{1,0:T(8,128)(2,1)}, bf16[96,2304]{1,0:T(8,128)(2,1)S(1)}, u32[]{:S(2)}, u32[]{:S(2)}) %collective-permute-start.78) | collective-permute-done | bytes 442400 | tf_op jit(solution)/shard_map/ppermute | solution.py:1144
  623.9 22.7 %collective-permute-done.79 = bf16[96,2304]{1,0:T(8,128)(2,1)S(1)} collective-permute-done((bf16[96,2304]{1,0:T(8,128)(2,1)S(1)}, bf16[96,2304]{1,0:T(8,128)(2,1)S(1)}, u32[]{:S(2)}, u32[]{:S(2)}) %collective-permute-start.79) | collective-permute-done | bytes 442400 | tf_op jit(solution)/shard_map/ppermute | solution.py:1144
  651.9 2.7 collective-permute-start.83
  (631 shorter events, 230.8 us)
Async XLA Ops:
  7.2 219.7 %all-gather.7.cloned.1.call-start = ((), (), s32[]{:S(2)}) async-start(), calls=%async_computation.3 | async-start | bytes 3538944 | tf_op jit(solution)/shard_map/all_gather | solution.py:1296
  9.3 217.7 %all-gather.5.cloned.1.call-start = ((), (), s32[]{:S(2)}) async-start(), calls=%async_computation.2 | async-start | bytes 7077888 | tf_op jit(solution)/shard_map/all_gather | solution.py:1295
  14.0 61.1 %collective-permute-start.13 = (bf16[24,1024]{1,0:T(8,128)(2,1)S(1)}, bf16[24,1024]{1,0:T(8,128)(2,1)S(1)}, u32[]{:S(2)}, u32[]{:S(2)}) collective-permute-start(bf16[24,1024]{1,0:T(8,128)(2,1)S(1)} %get-tuple-element.246), channel_id=1, source_target_pairs={{0,2},{1,3},{2,0},{3,1},{4,6},{5,7},{6,4},{7,5},{8,10},{9,11},{10,... | collective-permute-start | bytes 147464 | tf_op jit(solution)/shard_map/ppermute | solution.py:536
  14.3 60.8 %collective-permute-start.15 = (bf16[24,1024]{1,0:T(8,128)(2,1)S(1)}, bf16[24,1024]{1,0:T(8,128)(2,1)S(1)}, u32[]{:S(2)}, u32[]{:S(2)}) collective-permute-start(bf16[24,1024]{1,0:T(8,128)(2,1)S(1)} %get-tuple-element.247), channel_id=1, source_target_pairs={{0,3},{1,2},{2,1},{3,0},{4,7},{5,6},{6,5},{7,4},{8,11},{9,10},{10,... | collective-permute-start | bytes 147464 | tf_op jit(solution)/shard_map/ppermute | solution.py:536
  17.0 457.1 %reduce-scatter.2.cloned.1.call-start = ((), (), s32[]{:S(2)}) async-start(), calls=%async_computation.1 | async-start | bytes 7077888 | tf_op jit(solution)/shard_map/reduce_scatter | solution.py:1372
  24.0 20.6 %collective-permute-start.7 = (bf16[96,896]{1,0:T(8,128)(2,1)S(1)}, bf16[96,896]{1,0:T(8,128)(2,1)S(1)}, u32[]{:S(2)}, u32[]{:S(2)}) collective-permute-start(bf16[96,896]{1,0:T(8,128)(2,1)S(1)} %pad_maximum_fusion.13.refs_0_), channel_id=1, source_target_pairs={{0,16},{1,17},{2,18},{3,19},{4,20},{5,21},{6,22},{7,23},{8,24},{9,... | collective-permute-start | bytes 516104 | tf_op jit(solution)/shard_map/ppermute | solution.py:1164
  26.3 22.2 %collective-permute-start.6 = (bf16[96,896]{1,0:T(8,128)(2,1)S(1)}, bf16[96,896]{1,0:T(8,128)(2,1)S(1)}, u32[]{:S(2)}, u32[]{:S(2)}) collective-permute-start(bf16[96,896]{1,0:T(8,128)(2,1)S(1)} %pad_maximum_fusion.13.refs_0_), channel_id=1, source_target_pairs={{0,8},{1,9},{2,10},{3,11},{4,12},{5,13},{6,14},{7,15},{8,16},{9,17... | collective-permute-start | bytes 516104 | tf_op jit(solution)/shard_map/ppermute | solution.py:1164
  38.7 36.5 %collective-permute-start.14 = (bf16[24,1024]{1,0:T(8,128)(2,1)S(1)}, bf16[24,1024]{1,0:T(8,128)(2,1)S(1)}, u32[]{:S(2)}, u32[]{:S(2)}) collective-permute-start(bf16[24,1024]{1,0:T(8,128)(2,1)S(1)} %get-tuple-element.248), channel_id=1, source_target_pairs={{0,1},{1,0},{2,3},{3,2},{4,5},{5,4},{6,7},{7,6},{8,9},{9,8},{10,11... | collective-permute-start | bytes 147464 | tf_op jit(solution)/shard_map/ppermute | solution.py:536
  44.5 54.7 %collective-permute-start.1 = (bf16[2,128,896]{2,1,0:T(8,128)(2,1)}, bf16[2,128,896]{2,1,0:T(8,128)(2,1)}, u32[]{:S(2)}, u32[]{:S(2)}) collective-permute-start(bf16[2,128,896]{2,1,0:T(8,128)(2,1)} %maximum_maximum_fusion), channel_id=1, source_target_pairs={{0,1},{1,0},{2,3},{3,2},{4,5},{5,4},{6,7},{7,6},{8,9},{9,8},{10,11... | collective-permute-start | bytes 1376264 | tf_op jit(solution)/shard_map/ppermute | solution.py:536
  49.4 39.6 %collective-permute-start.9 = (bf16[4,96,896]{2,1,0:T(8,128)(2,1)}, bf16[4,96,896]{2,1,0:T(8,128)(2,1)}, u32[]{:S(2)}, u32[]{:S(2)}) collective-permute-start(bf16[4,96,896]{2,1,0:T(8,128)(2,1)} %pad_maximum_fusion.5), channel_id=1, source_target_pairs={{0,4},{1,5},{2,6},{3,7},{4,0},{5,1},{6,2},{7,3},{8,12},{9,13},{10,... | collective-permute-start | bytes 2064392 | tf_op jit(solution)/shard_map/ppermute | solution.py:1169
  75.3 38.4 %collective-permute-start.18 = (bf16[96,1536]{1,0:T(8,128)(2,1)S(1)}, bf16[96,1536]{1,0:T(8,128)(2,1)S(1)}, u32[]{:S(2)}, u32[]{:S(2)}) collective-permute-start(bf16[96,1536]{1,0:T(8,128)(2,1)S(1)} %constant_dynamic-update-slice_fusion.refs_0_), channel_id=1, source_target_pairs={{0,24},{1,25},{2,26},{3,27},{4,28},{5,29},{6,30},{7,31},{8,0},{9,1... | collective-permute-start | bytes 884744 | tf_op jit(solution)/shard_map/ppermute | solution.py:1164
  79.3 34.6 %collective-permute-start.17 = (bf16[96,1536]{1,0:T(8,128)(2,1)S(1)}, bf16[96,1536]{1,0:T(8,128)(2,1)S(1)}, u32[]{:S(2)}, u32[]{:S(2)}) collective-permute-start(bf16[96,1536]{1,0:T(8,128)(2,1)S(1)} %constant_dynamic-update-slice_fusion.refs_0_), channel_id=1, source_target_pairs={{0,16},{1,17},{2,18},{3,19},{4,20},{5,21},{6,22},{7,23},{8,24},{9,... | collective-permute-start | bytes 884744 | tf_op jit(solution)/shard_map/ppermute | solution.py:1164
  86.7 28.1 %collective-permute-start.16 = (bf16[96,1536]{1,0:T(8,128)(2,1)S(1)}, bf16[96,1536]{1,0:T(8,128)(2,1)S(1)}, u32[]{:S(2)}, u32[]{:S(2)}) collective-permute-start(bf16[96,1536]{1,0:T(8,128)(2,1)S(1)} %constant_dynamic-update-slice_fusion.refs_0_), channel_id=1, source_target_pairs={{0,8},{1,9},{2,10},{3,11},{4,12},{5,13},{6,14},{7,15},{8,16},{9,17... | collective-permute-start | bytes 884744 | tf_op jit(solution)/shard_map/ppermute | solution.py:1164
  99.2 19.8 %collective-permute-start.20 = (bf16[8,24,768]{2,1,0:T(8,128)(2,1)S(1)}, bf16[8,24,768]{2,1,0:T(8,128)(2,1)}, u32[]{:S(2)}, u32[]{:S(2)}) collective-permute-start(bf16[8,24,768]{2,1,0:T(8,128)(2,1)S(1)} %reshape.511), channel_id=1, source_target_pairs={{0,2},{1,3},{2,0},{3,1},{4,6},{5,7},{6,4},{7,5},{8,10},{9,11},{10,... | collective-permute-start | bytes 884744 | tf_op jit(solution)/shard_map/ppermute | solution.py:536
  100.1 20.8 %collective-permute-start.23 = (bf16[2,128,768]{2,1,0:T(8,128)(2,1)}, bf16[2,128,768]{2,1,0:T(8,128)(2,1)}, u32[]{:S(2)}, u32[]{:S(2)}) collective-permute-start(bf16[2,128,768]{2,1,0:T(8,128)(2,1)} %param.20), channel_id=1, source_target_pairs={{0,2},{1,3},{2,0},{3,1},{4,6},{5,7},{6,4},{7,5},{8,10},{9,11},{10,... | collective-permute-start | bytes 1179656 | tf_op jit(solution)/shard_map/ppermute | solution.py:536
  115.0 35.8 %collective-permute-start.19 = (bf16[4,96,1536]{2,1,0:T(8,128)(2,1)S(1)}, bf16[4,96,1536]{2,1,0:T(8,128)(2,1)}, u32[]{:S(2)}, u32[]{:S(2)}) collective-permute-start(bf16[4,96,1536]{2,1,0:T(8,128)(2,1)S(1)} %pad_maximum_fusion.3), channel_id=1, source_target_pairs={{0,4},{1,5},{2,6},{3,7},{4,0},{5,1},{6,2},{7,3},{8,12},{9,13},{10,... | collective-permute-start | bytes 3538952 | tf_op jit(solution)/shard_map/ppermute | solution.py:1169
  120.9 38.6 %collective-permute-start.11 = (bf16[2,512,192]{2,1,0:T(8,128)(2,1)}, bf16[2,512,192]{2,1,0:T(8,128)(2,1)S(1)}, u32[]{:S(2)}, u32[]{:S(2)}) collective-permute-start(bf16[2,512,192]{2,1,0:T(8,128)(2,1)} %get-tuple-element.54), channel_id=1, source_target_pairs={{0,1},{1,0},{2,3},{3,2},{4,5},{5,4},{6,7},{7,6},{8,9},{9,8},{10,11... | collective-permute-start | bytes 1179656 | tf_op jit(solution)/shard_map/ppermute | solution.py:536
  128.4 31.1 %collective-permute-start.12 = (bf16[2,512,192]{2,1,0:T(8,128)(2,1)}, bf16[2,512,192]{2,1,0:T(8,128)(2,1)}, u32[]{:S(2)}, u32[]{:S(2)}) collective-permute-start(bf16[2,512,192]{2,1,0:T(8,128)(2,1)} %collective-permute-done.10), channel_id=1, source_target_pairs={{0,1},{1,0},{2,3},{3,2},{4,5},{5,4},{6,7},{7,6},{8,9},{9,8},{10,11... | collective-permute-start | bytes 1179656 | tf_op jit(solution)/shard_map/ppermute | solution.py:536
  186.4 33.3 %collective-permute-start.26 = (bf16[4,96,1536]{2,1,0:T(8,128)(2,1)}, bf16[4,96,1536]{2,1,0:T(8,128)(2,1)}, u32[]{:S(2)}, u32[]{:S(2)}) collective-permute-start(bf16[4,96,1536]{2,1,0:T(8,128)(2,1)} %fusion.6), channel_id=1, source_target_pairs={{0,4},{1,5},{2,6},{3,7},{4,0},{5,1},{6,2},{7,3},{8,12},{9,13},{10,... | collective-permute-start | bytes 3538952 | tf_op jit(solution)/shard_map/ppermute | solution.py:1169
  189.3 88.8 %collective-permute-start.54 = (bf16[24,1600]{1,0:T(8,128)(2,1)S(1)}, bf16[24,1600]{1,0:T(8,128)(2,1)S(1)}, u32[]{:S(2)}, u32[]{:S(2)}) collective-permute-start(bf16[24,1600]{1,0:T(8,128)(2,1)S(1)} %get-tuple-element.236), channel_id=1, source_target_pairs={{0,2},{1,3},{2,0},{3,1},{4,6},{5,7},{6,4},{7,5},{8,10},{9,11},{10,... | collective-permute-start | bytes 230408 | tf_op jit(solution)/shard_map/ppermute | solution.py:536
  189.5 88.6 %collective-permute-start.56 = (bf16[24,1600]{1,0:T(8,128)(2,1)S(1)}, bf16[24,1600]{1,0:T(8,128)(2,1)S(1)}, u32[]{:S(2)}, u32[]{:S(2)}) collective-permute-start(bf16[24,1600]{1,0:T(8,128)(2,1)S(1)} %get-tuple-element.237), channel_id=1, source_target_pairs={{0,3},{1,2},{2,1},{3,0},{4,7},{5,6},{6,5},{7,4},{8,11},{9,10},{10,... | collective-permute-start | bytes 230408 | tf_op jit(solution)/shard_map/ppermute | solution.py:536
  222.4 51.4 %collective-permute-start.31 = (bf16[96,1536]{1,0:T(8,128)(2,1)S(1)}, bf16[96,1536]{1,0:T(8,128)(2,1)S(1)}, u32[]{:S(2)}, u32[]{:S(2)}) collective-permute-start(bf16[96,1536]{1,0:T(8,128)(2,1)S(1)} %get-tuple-element.171), channel_id=1, source_target_pairs={{0,24},{1,25},{2,26},{3,27},{4,28},{5,29},{6,30},{7,31},{8,0},{9,1... | collective-permute-start | bytes 884744 | tf_op jit(solution)/shard_map/ppermute | solution.py:1164
  222.5 53.1 %collective-permute-start.30 = (bf16[96,1536]{1,0:T(8,128)(2,1)S(1)}, bf16[96,1536]{1,0:T(8,128)(2,1)S(1)}, u32[]{:S(2)}, u32[]{:S(2)}) collective-permute-start(bf16[96,1536]{1,0:T(8,128)(2,1)S(1)} %get-tuple-element.172), channel_id=1, source_target_pairs={{0,16},{1,17},{2,18},{3,19},{4,20},{5,21},{6,22},{7,23},{8,24},{9,... | collective-permute-start | bytes 884744 | tf_op jit(solution)/shard_map/ppermute | solution.py:1164
  224.9 50.8 %collective-permute-start.29 = (bf16[96,1536]{1,0:T(8,128)(2,1)S(1)}, bf16[96,1536]{1,0:T(8,128)(2,1)S(1)}, u32[]{:S(2)}, u32[]{:S(2)}) collective-permute-start(bf16[96,1536]{1,0:T(8,128)(2,1)S(1)} %get-tuple-element.173), channel_id=1, source_target_pairs={{0,8},{1,9},{2,10},{3,11},{4,12},{5,13},{6,14},{7,15},{8,16},{9,17... | collective-permute-start | bytes 884744 | tf_op jit(solution)/shard_map/ppermute | solution.py:1164
  285.4 51.6 %collective-permute-start.37 = (bf16[4,256,768]{1,2,0:T(8,128)(2,1)}, bf16[4,256,768]{1,2,0:T(8,128)(2,1)}, u32[]{:S(2)}, u32[]{:S(2)}) collective-permute-start(bf16[4,256,768]{1,2,0:T(8,128)(2,1)} %bitcast.500), channel_id=1, source_target_pairs={{0,4},{1,5},{2,6},{3,7},{4,0},{5,1},{6,2},{7,3},{8,12},{9,13},{10,... | collective-permute-start | bytes 4718600 | tf_op jit(solution)/shard_map/ppermute | solution.py:1169
  320.9 40.8 %collective-permute-start.45 = (bf16[2,8,24,768]{3,2,1,0:T(8,128)(2,1)}, bf16[2,8,24,768]{3,2,1,0:T(8,128)(2,1)}, u32[]{:S(2)}, u32[]{:S(2)}) collective-permute-start(bf16[2,8,24,768]{3,2,1,0:T(8,128)(2,1)} %dynamic-slice_bitcast_fusion.3), channel_id=1, source_target_pairs={{0,1},{1,0},{2,3},{3,2},{4,5},{5,4},{6,7},{7,6},{8,9},{9,8},{10,11... | collective-permute-start | bytes 1769480 | tf_op jit(solution)/shard_map/ppermute | solution.py:536
  355.7 31.3 %collective-permute-start.65 = (bf16[64,768]{1,0:T(8,128)(2,1)}, bf16[64,768]{1,0:T(8,128)(2,1)}, u32[]{:S(2)}, u32[]{:S(2)}) collective-permute-start(bf16[64,768]{1,0:T(8,128)(2,1)} %get-tuple-element.129), channel_id=1, source_target_pairs={{2,3},{6,7},{10,11},{14,15},{18,19},{22,23},{26,27},{30,31}} | collective-permute-start | bytes 294920 | tf_op jit(solution)/shard_map/ppermute | solution.py:1502
  357.0 30.0 %collective-permute-start.64 = (bf16[64,768]{1,0:T(8,128)(2,1)}, bf16[64,768]{1,0:T(8,128)(2,1)}, u32[]{:S(2)}, u32[]{:S(2)}) collective-permute-start(bf16[64,768]{1,0:T(8,128)(2,1)} %get-tuple-element.129), channel_id=1, source_target_pairs={{1,3},{5,7},{9,11},{13,15},{17,19},{21,23},{25,27},{29,31}} | collective-permute-start | bytes 294920 | tf_op jit(solution)/shard_map/ppermute | solution.py:1502
  358.3 28.7 %collective-permute-start.63 = (bf16[64,768]{1,0:T(8,128)(2,1)}, bf16[64,768]{1,0:T(8,128)(2,1)}, u32[]{:S(2)}, u32[]{:S(2)}) collective-permute-start(bf16[64,768]{1,0:T(8,128)(2,1)} %get-tuple-element.129), channel_id=1, source_target_pairs={{0,3},{4,7},{8,11},{12,15},{16,19},{20,23},{24,27},{28,31}} | collective-permute-start | bytes 294920 | tf_op jit(solution)/shard_map/ppermute | solution.py:1502
  375.5 23.2 %collective-permute-start.47 = (bf16[4,96,768]{2,1,0:T(8,128)(2,1)}, bf16[4,96,768]{2,1,0:T(8,128)(2,1)}, u32[]{:S(2)}, u32[]{:S(2)}) collective-permute-start(bf16[4,96,768]{2,1,0:T(8,128)(2,1)} %fusion.32), channel_id=1, source_target_pairs={{0,4},{1,5},{2,6},{3,7},{4,0},{5,1},{6,2},{7,3},{8,12},{9,13},{10,... | collective-permute-start | bytes 1769480 | tf_op jit(solution)/shard_map/ppermute | solution.py:1169
  401.0 43.7 %collective-permute-start.48 = (bf16[96,768]{1,0:T(8,128)(2,1)}, bf16[96,768]{1,0:T(8,128)(2,1)S(1)}, u32[]{:S(2)}, u32[]{:S(2)}) collective-permute-start(bf16[96,768]{1,0:T(8,128)(2,1)} %get-tuple-element.187), channel_id=1, source_target_pairs={{0,8},{1,9},{2,10},{3,11},{4,12},{5,13},{6,14},{7,15},{8,16},{9,17... | collective-permute-start | bytes 442376 | tf_op jit(solution)/shard_map/ppermute | solution.py:1164
  403.3 41.4 %collective-permute-start.50 = (bf16[96,768]{1,0:T(8,128)(2,1)}, bf16[96,768]{1,0:T(8,128)(2,1)S(1)}, u32[]{:S(2)}, u32[]{:S(2)}) collective-permute-start(bf16[96,768]{1,0:T(8,128)(2,1)} %get-tuple-element.188), channel_id=1, source_target_pairs={{0,24},{1,25},{2,26},{3,27},{4,28},{5,29},{6,30},{7,31},{8,0},{9,1... | collective-permute-start | bytes 442376 | tf_op jit(solution)/shard_map/ppermute | solution.py:1164
  403.3 41.4 %collective-permute-start.49 = (bf16[96,768]{1,0:T(8,128)(2,1)S(1)}, bf16[96,768]{1,0:T(8,128)(2,1)S(1)}, u32[]{:S(2)}, u32[]{:S(2)}) collective-permute-start(bf16[96,768]{1,0:T(8,128)(2,1)S(1)} %get-tuple-element.189), channel_id=1, source_target_pairs={{0,16},{1,17},{2,18},{3,19},{4,20},{5,21},{6,22},{7,23},{8,24},{9,... | collective-permute-start | bytes 442376 | tf_op jit(solution)/shard_map/ppermute | solution.py:1164
  415.7 53.8 %collective-permute-start.60 = (bf16[256,768]{0,1:T(8,128)(2,1)}, bf16[256,768]{0,1:T(8,128)(2,1)}, u32[]{:S(2)}, u32[]{:S(2)}) collective-permute-start(bf16[256,768]{0,1:T(8,128)(2,1)} %get-tuple-element.164), channel_id=1, source_target_pairs={{0,8},{1,9},{2,10},{3,11},{4,12},{5,13},{6,14},{7,15},{8,16},{9,17... | collective-permute-start | bytes 1179656 | tf_op jit(solution)/shard_map/ppermute | solution.py:1164
  418.5 51.0 %collective-permute-start.62 = (bf16[256,768]{0,1:T(8,128)(2,1)}, bf16[256,768]{0,1:T(8,128)(2,1)}, u32[]{:S(2)}, u32[]{:S(2)}) collective-permute-start(bf16[256,768]{0,1:T(8,128)(2,1)} %get-tuple-element.165), channel_id=1, source_target_pairs={{0,24},{1,25},{2,26},{3,27},{4,28},{5,29},{6,30},{7,31},{8,0},{9,1... | collective-permute-start | bytes 1179656 | tf_op jit(solution)/shard_map/ppermute | solution.py:1164
  452.0 19.7 %collective-permute-start.61 = (bf16[256,768]{0,1:T(8,128)(2,1)}, bf16[256,768]{0,1:T(8,128)(2,1)}, u32[]{:S(2)}, u32[]{:S(2)}) collective-permute-start(bf16[256,768]{0,1:T(8,128)(2,1)} %get-tuple-element.166), channel_id=1, source_target_pairs={{0,16},{1,17},{2,18},{3,19},{4,20},{5,21},{6,22},{7,23},{8,24},{9,... | collective-permute-start | bytes 1179656 | tf_op jit(solution)/shard_map/ppermute | solution.py:1164
  490.2 40.8 %collective-permute-start.71 = (bf16[96,2304]{1,0:T(8,128)(2,1)}, bf16[96,2304]{1,0:T(8,128)(2,1)}, u32[]{:S(2)}, u32[]{:S(2)}) collective-permute-start(bf16[96,2304]{1,0:T(8,128)(2,1)} %get-tuple-element.147), channel_id=1, source_target_pairs={{24,0},{4,12},{8,16},{20,28},{29,5},{1,9},{13,21},{17,25},{26,2},{... | collective-permute-start | bytes 1327112 | tf_op jit(solution)/shard_map/ppermute | solution.py:1136
  500.2 37.4 %collective-permute-start.70 = (bf16[96,2304]{1,0:T(8,128)(2,1)}, bf16[96,2304]{1,0:T(8,128)(2,1)S(1)}, u32[]{:S(2)}, u32[]{:S(2)}) collective-permute-start(bf16[96,2304]{1,0:T(8,128)(2,1)} %get-tuple-element.148), channel_id=1, source_target_pairs={{20,0},{0,12},{4,16},{16,28},{25,5},{29,9},{9,21},{13,25},{22,2},{... | collective-permute-start | bytes 1327112 | tf_op jit(solution)/shard_map/ppermute | solution.py:1136
  501.5 36.1 %collective-permute-start.69 = (bf16[96,2304]{1,0:T(8,128)(2,1)}, bf16[96,2304]{1,0:T(8,128)(2,1)}, u32[]{:S(2)}, u32[]{:S(2)}) collective-permute-start(bf16[96,2304]{1,0:T(8,128)(2,1)} %get-tuple-element.149), channel_id=1, source_target_pairs={{16,0},{28,12},{0,16},{12,28},{21,5},{25,9},{5,21},{9,25},{18,2},{... | collective-permute-start | bytes 1327112 | tf_op jit(solution)/shard_map/ppermute | solution.py:1136
  503.0 34.7 %collective-permute-start.68 = (bf16[96,2304]{1,0:T(8,128)(2,1)}, bf16[96,2304]{1,0:T(8,128)(2,1)}, u32[]{:S(2)}, u32[]{:S(2)}) collective-permute-start(bf16[96,2304]{1,0:T(8,128)(2,1)} %get-tuple-element.150), channel_id=1, source_target_pairs={{12,0},{24,12},{28,16},{8,28},{17,5},{21,9},{1,21},{5,25},{14,2},{... | collective-permute-start | bytes 1327112 | tf_op jit(solution)/shard_map/ppermute | solution.py:1136
  504.4 33.2 %collective-permute-start.67 = (bf16[96,2304]{1,0:T(8,128)(2,1)S(1)}, bf16[96,2304]{1,0:T(8,128)(2,1)}, u32[]{:S(2)}, u32[]{:S(2)}) collective-permute-start(bf16[96,2304]{1,0:T(8,128)(2,1)S(1)} %get-tuple-element.151), channel_id=1, source_target_pairs={{8,0},{20,12},{24,16},{4,28},{13,5},{17,9},{29,21},{1,25},{10,2},{... | collective-permute-start | bytes 1327112 | tf_op jit(solution)/shard_map/ppermute | solution.py:1136
  542.4 52.0 %collective-permute-start.73 = (bf16[96,2304]{1,0:T(8,128)(2,1)}, bf16[96,2304]{1,0:T(8,128)(2,1)S(1)}, u32[]{:S(2)}, u32[]{:S(2)}) collective-permute-start(bf16[96,2304]{1,0:T(8,128)(2,1)} %get-tuple-element.87), channel_id=1, source_target_pairs={{0,4},{12,16},{16,20},{28,0},{5,9},{9,13},{21,25},{25,29},{2,6},{1... | collective-permute-start | bytes 1327112 | tf_op jit(solution)/shard_map/ppermute | solution.py:1144
  543.8 51.9 %collective-permute-start.74 = (bf16[96,2304]{1,0:T(8,128)(2,1)}, bf16[96,2304]{1,0:T(8,128)(2,1)S(1)}, u32[]{:S(2)}, u32[]{:S(2)}) collective-permute-start(bf16[96,2304]{1,0:T(8,128)(2,1)} %get-tuple-element.88), channel_id=1, source_target_pairs={{0,8},{12,20},{16,24},{28,4},{5,13},{9,17},{21,29},{25,1},{2,10},{... | collective-permute-start | bytes 1327112 | tf_op jit(solution)/shard_map/ppermute | solution.py:1144
  545.1 51.9 %collective-permute-start.75 = (bf16[96,2304]{1,0:T(8,128)(2,1)}, bf16[96,2304]{1,0:T(8,128)(2,1)S(1)}, u32[]{:S(2)}, u32[]{:S(2)}) collective-permute-start(bf16[96,2304]{1,0:T(8,128)(2,1)} %get-tuple-element.89), channel_id=1, source_target_pairs={{0,12},{12,24},{16,28},{28,8},{5,17},{9,21},{21,1},{25,5},{2,14},{... | collective-permute-start | bytes 1327112 | tf_op jit(solution)/shard_map/ppermute | solution.py:1144
  545.8 51.3 %collective-permute-start.76 = (bf16[96,2304]{1,0:T(8,128)(2,1)}, bf16[96,2304]{1,0:T(8,128)(2,1)S(1)}, u32[]{:S(2)}, u32[]{:S(2)}) collective-permute-start(bf16[96,2304]{1,0:T(8,128)(2,1)} %get-tuple-element.90), channel_id=1, source_target_pairs={{0,16},{12,28},{16,0},{28,12},{5,21},{9,25},{21,5},{25,9},{2,18},{... | collective-permute-start | bytes 1327112 | tf_op jit(solution)/shard_map/ppermute | solution.py:1144
  546.5 61.9 %collective-permute-start.77 = (bf16[96,2304]{1,0:T(8,128)(2,1)}, bf16[96,2304]{1,0:T(8,128)(2,1)S(1)}, u32[]{:S(2)}, u32[]{:S(2)}) collective-permute-start(bf16[96,2304]{1,0:T(8,128)(2,1)} %get-tuple-element.91), channel_id=1, source_target_pairs={{0,20},{12,0},{16,4},{28,16},{5,25},{9,29},{21,9},{25,13},{2,22},{... | collective-permute-start | bytes 1327112 | tf_op jit(solution)/shard_map/ppermute | solution.py:1144
  594.4 29.4 %collective-permute-start.78 = (bf16[96,2304]{1,0:T(8,128)(2,1)}, bf16[96,2304]{1,0:T(8,128)(2,1)S(1)}, u32[]{:S(2)}, u32[]{:S(2)}) collective-permute-start(bf16[96,2304]{1,0:T(8,128)(2,1)} %get-tuple-element.92), channel_id=1, source_target_pairs={{0,24},{12,4},{16,8},{28,20},{5,29},{9,1},{21,13},{25,17},{2,26},{... | collective-permute-start | bytes 1327112 | tf_op jit(solution)/shard_map/ppermute | solution.py:1144
  595.7 50.8 %collective-permute-start.79 = (bf16[96,2304]{1,0:T(8,128)(2,1)S(1)}, bf16[96,2304]{1,0:T(8,128)(2,1)S(1)}, u32[]{:S(2)}, u32[]{:S(2)}) collective-permute-start(bf16[96,2304]{1,0:T(8,128)(2,1)S(1)} %copy-done.88), channel_id=1, source_target_pairs={{0,28},{12,8},{16,12},{28,24},{5,1},{9,5},{21,17},{25,21},{2,30},{... | collective-permute-start | bytes 1327112 | tf_op jit(solution)/shard_map/ppermute | solution.py:1144
  (132 other events, 1107.5 us)
Sparse Core Ops, SparseCore 0:
  10.8 96.6 all-gather.6
  109.7 108.0 all-gather.4
  279.0 117.7 reduce-scatter.1

commit v3 on v2

--- a/solution.py
+++ b/solution.py
@@ -1448,13 +1448,6 @@
     new_gain_moms = own_small[experts : experts + 2]
     gain_rate = 0.1 / math.sqrt(count * DP)
     new_gains = gains - gain_rate * new_gain_moms
-    orth_router = orthogonal_router(
-        jnp.concatenate([small[:experts], jnp.zeros((LANES - experts, width), jnp.float32)], axis=0)
-    )
-    new_router = w_router - ROUTER_RATE * lax.dynamic_slice(
-        orth_router, columns, (experts, block_rows)
-    ).T
-
     old_near = exchange_fsdp(by_columns(after(mom_dense, normed_all).astype(bf16)), index)
     old_near = jnp.concatenate(old_near, axis=0).astype(jnp.float32)
     got = exchange_fsdp(part_dense.reshape(FS, block_rows, part_dense.shape[1]), index)
@@ -1490,7 +1483,7 @@
         [block[:, :fold_out].reshape(block_rows, width) for block in got], axis=0
     )
     dense_block = jnp.where(index == FS - 1, pad(whole_out), jnp.concatenate(got, axis=1))
-    low_experts = after(new_e_mom_gate_up[0].astype(bf16), orth_router)
+    low_experts = after(new_e_mom_gate_up[0].astype(bf16), small)
     wide = [pad(low_experts[0]), pad(low_experts[1]), dense_block]
     low_down = new_mom_down.astype(bf16)
     column_pairs = lambda step, back: [
@@ -1514,6 +1507,13 @@
             kinds[f, d] = 2 if slot in TALL_SLOTS else 1
     info = jnp.stack([jnp.asarray(kinds)[index, dp_index], dp_index.astype(jnp.int32)])
     shards = orthogonal_shards(info, shards, width)
+    orth_router = orthogonal_router(
+        jnp.concatenate([after(small, *shards)[:experts], jnp.zeros((LANES - experts, width), jnp.float32)], axis=0)
+    )
+    new_router = w_router - ROUTER_RATE * lax.dynamic_slice(
+        orth_router, columns, (experts, block_rows)
+    ).T
+
     orth_gate, orth_up, orth_block, orth_edown, orth_down_block = from_owners(
         shards, OWNERS, dp_index, index
     )

time: 681 us -> 671 us (0.985)
  waiting for transfers between devices: 225 us -> 210 us
  local copies, waits for them, and re-layouts: 108 us -> 115 us
    ppermute x7, waiting for transfers between devices: 94.8 us -> 78.7 us  [from_owners(): lax.ppermute(block, AXES, owner_pairs(owners, step, True))]
    unnamed x204 -> x206, local copies, waits for them, and re-layouts: 18.3 us -> 23.5 us
  transfers between devices with their start and end apart: 89 -> 89, of which waited for: 26 -> 27; matrix products, arithmetic and copies ran while one was open for 22% -> 23% of each run, Pallas kernels for 16% -> 16%
where the time goes in v3:
time: 671 us; the launch traced here: 663 us
  waiting for transfers between devices  210 us (31%)
  starting transfers between devices  128 us (19%)
  local copies, waits for them, and re-layouts  115 us (17%)
  Pallas kernels  111 us (17%)
  other arithmetic  64.9 us (10%)
  between operations  34.6 us (5%)
    ppermute x7, waiting for transfers between devices, from_owners(): lax.ppermute(block, AXES, owner_pairs(owners, step, True))  78.7 us
    pallas_call x2, Pallas kernels, branch(): kernel_call(functools.partial(branch_body, routed=routed, chained=chained...  56.3 us
    ppermute x5, waiting for transfers between devices, pair_hop(): return lax.ppermute(value, AXES, pairs)  49.5 us
    ppermute x15, starting transfers between devices, line_hop(): return lax.ppermute(value, AXES, pairs)  41.5 us
    ppermute x41, waiting for transfers between devices, fsdp_hop(): return lax.ppermute(value, AXES, pairs)  34.6 us
    ppermute x41, starting transfers between devices, fsdp_hop(): return lax.ppermute(value, AXES, pairs)  33.5 us
    unnamed x206, local copies, waits for them, and re-layouts  23.5 us
    ppermute x7, waiting for transfers between devices, to_owners(): lax.ppermute(block, AXES, owner_pairs(owners, step, False))  21.9 us
  transfers between devices with their start and end apart: 89, of which 27 were waited for; matrix products, arithmetic and copies ran while one was open for 23% of the time, Pallas kernels for 16%

profile of v3, /device:TPU:15, one launch (start us, length us, event | category | flops | bytes accessed | tf_op | source)
XLA Modules:
  0.0 663.3 jit_solution(5084963497829964188)
XLA Ops:
  28.6 8.7 %collective-permute-done.8.refs_3_ = bf16[96,896]{1,0:T(8,128)(2,1)S(1)} collective-permute-done((bf16[96,896]{1,0:T(8,128)(2,1)S(1)}, bf16[96,896]{1,0:T(8,128)(2,1)S(1)}, u32[]{:S(2)}, u32[]{:S(2)}) %collective-permute-start.8) | collective-permute-done | bytes 172064 | tf_op jit(solution)/shard_map/ppermute | solution.py:1164
  39.0 5.6 collective-permute-done.7.refs_2_
  45.1 3.5 collective-permute-done.6.refs_1_
  75.4 4.0 collective-permute-start.18
  79.3 7.5 %collective-permute-done = bf16[2,128,896]{2,1,0:T(8,128)(2,1)S(1)} collective-permute-done((bf16[2,128,896]{2,1,0:T(8,128)(2,1)}, bf16[2,128,896]{2,1,0:T(8,128)(2,1)S(1)}, u32[]{:S(2)}, u32[]{:S(2)}) %collective-permute-start) | collective-permute-done | bytes 458784 | tf_op jit(solution)/shard_map/ppermute | solution.py:536
  86.9 2.4 collective-permute-start.16
  91.0 2.6 place_rows.2
  104.8 9.0 %attention_forward.1 = (bf16[768,1024]{1,0:T(8,128)(2,1)}, bf16[2,512,576]{2,1,0:T(8,128)(2,1)}, bf16[2,3,512,512]{3,2,1,0:T(8,128)(2,1)}, bf16[2,512,192]{2,1,0:T(8,128)(2,1)}) custom-call(s32[2]{0:T(128)} %lengths_ref.1, bf16[2,512,768]{2,1,0:T(8,128)(2,1)} %slice.363.x_ref, f32[1,768]{1,0:T(1,128)} %get-tuple-element.276.gain_ref, ...), custom_call_target="tpu_custom_call" | custom-call | flops 6000000000 | bytes 12000000 | tf_op jit(solution)/shard_map/attention_forward/pallas_call | solution.py:632
  121.3 5.8 collective-permute-done.10
  133.2 18.0 %collective-permute-done.19.refs_4_ = bf16[4,96,1536]{2,1,0:T(8,128)(2,1)} collective-permute-done((bf16[4,96,1536]{2,1,0:T(8,128)(2,1)S(1)}, bf16[4,96,1536]{2,1,0:T(8,128)(2,1)}, u32[]{:S(2)}, u32[]{:S(2)}) %collective-permute-start.19) | collective-permute-done | bytes 1179680 | tf_op jit(solution)/shard_map/ppermute | solution.py:1169
  151.1 3.2 place_rows.3
  154.3 2.7 slice.378.refs_0_.refs_1_
  163.8 7.4 %middle_forward.1 = (f32[1024,768]{1,0:T(8,128)}, bf16[1024,768]{1,0:T(8,128)(2,1)}, bf16[768,1024]{1,0:T(8,128)(2,1)}, f32[1024,128]{1,0:T(8,128)}) custom-call(bf16[1024,768]{1,0:T(8,128)(2,1)} %bitcast.474, bf16[1024,768]{1,0:T(8,128)(2,1)} %bitcast.477, s32[1024,128]{1,0:T(8,128)} %bitcast_convert_fusion.routes_ref, bf16[768,768]{1,0:T(8,128)(2,1)} %bitcast.472, ...), custom_call_target="tpu_custom_call" | custom-call | flops 1207959552 | bytes 12000000 | tf_op jit(solution)/shard_map/middle_forward/pallas_call | solution.py:750
  171.3 12.9 %shared_branch.1 = (f32[1024,768]{1,0:T(8,128)}, f32[1024,768]{1,0:T(8,128)}, bf16[768,1024]{1,0:T(8,128)(2,1)}, bf16[512,768]{1,0:T(8,128)(2,1)}) custom-call(s32[1]{0:T(128)} %bitcast.32.expert_ref, bf16[1024,768]{1,0:T(8,128)(2,1)} %get-tuple-element.64.normed_ref, bf16[768,1024]{1,0:T(8,128)(2,1)} %get-tuple-element.60.turned_ref, ...), custom_call_target="tpu_custom_call" | custom-call | flops 7247757312 | bytes 17301504 | tf_op jit(solution)/shard_map/shared_branch/pallas_call | solution.py:934
  189.8 2.8 collective-permute-start.56
  198.7 21.2 %collective-permute-done.26 = bf16[4,96,1536]{2,1,0:T(8,128)(2,1)} collective-permute-done((bf16[4,96,1536]{2,1,0:T(8,128)(2,1)}, bf16[4,96,1536]{2,1,0:T(8,128)(2,1)}, u32[]{:S(2)}, u32[]{:S(2)}) %collective-permute-start.26) | collective-permute-done | bytes 1179680 | tf_op jit(solution)/shard_map/ppermute | solution.py:1169
  227.8 43.4 %expert_branch.1 = (bf16[1024,768]{1,0:T(8,128)(2,1)}, bf16[1024,896]{1,0:T(8,128)(2,1)}, bf16[768,4096]{1,0:T(8,128)(2,1)}, bf16[2048,768]{1,0:T(8,128)(2,1)}) custom-call(s32[1]{0:T(128)} %bitcast.32.expert_ref, bf16[1024,768]{1,0:T(8,128)(2,1)} %get-tuple-element.64.normed_ref, bf16[768,1024]{1,0:T(8,128)(2,1)} %get-tuple-element.60.turned_ref, ...), custom_call_target="tpu_custom_call" | custom-call | flops 28991029248 | bytes 31457280 | tf_op jit(solution)/shard_map/expert_branch/pallas_call | solution.py:934
  278.9 3.7 constant_dynamic-slice_fusion.3
  282.6 2.7 copy.144
  295.2 3.6 collective-permute-done.28
  298.8 2.5 fusion.30
  301.3 7.3 %collective-permute-done.33 = bf16[2,128,896]{2,1,0:T(8,128)(2,1)S(1)} collective-permute-done((bf16[2,128,896]{2,1,0:T(8,128)(2,1)S(1)}, bf16[2,128,896]{2,1,0:T(8,128)(2,1)S(1)}, u32[]{:S(2)}, u32[]{:S(2)}) %collective-permute-start.33) | collective-permute-done | bytes 458784 | tf_op jit(solution)/shard_map/ppermute | solution.py:536
  309.7 5.2 middle_backward.1
  321.4 4.4 collective-permute-done.36
  326.7 10.3 %collective-permute-done.37 = bf16[4,256,768]{1,2,0:T(8,128)(2,1)} collective-permute-done((bf16[4,256,768]{1,2,0:T(8,128)(2,1)}, bf16[4,256,768]{1,2,0:T(8,128)(2,1)}, u32[]{:S(2)}, u32[]{:S(2)}) %collective-permute-start.37) | collective-permute-done | bytes 1572896 | tf_op jit(solution)/shard_map/ppermute | solution.py:1169
  337.0 14.7 %attention_backward.1 = (bf16[768,576]{1,0:T(8,128)(2,1)}, bf16[2,512,768]{2,1,0:T(8,128)(2,1)}) custom-call(bf16[768,1024]{1,0:T(8,128)(2,1)} %get-tuple-element.72.normed_ref, bf16[2,512,576]{2,1,0:T(8,128)(2,1)} %get-tuple-element.73.qkv_ref, bf16[2,3,512,512]{3,2,1,0:T(8,128)(2,1)} %get-tuple-element.74.prob_ref, ...), custom_call_target="tpu_custom_call" | custom-call | flops 8000000000 | bytes 12000000 | tf_op jit(solution)/shard_map/attention_backward/pallas_call | solution.py:701
  362.7 2.7 collective-permute-start.46
  377.1 3.6 collective-permute-done.39
  402.3 7.3 %collective-permute-start.49 = (bf16[96,768]{1,0:T(8,128)(2,1)S(1)}, bf16[96,768]{1,0:T(8,128)(2,1)S(1)}, u32[]{:S(2)}, u32[]{:S(2)}) collective-permute-start(bf16[96,768]{1,0:T(8,128)(2,1)S(1)} %get-tuple-element.191), channel_id=1, source_target_pairs={{0,16},{1,17},{2,18},{3,19},{4,20},{5,21},{6,22},{7,23},{8,24},{9,... | collective-permute-start | bytes 442376 | tf_op jit(solution)/shard_map/ppermute | solution.py:1164
  414.7 2.8 collective-permute-done.44
  417.5 14.2 %collective-permute-start.62 = (bf16[256,768]{0,1:T(8,128)(2,1)}, bf16[256,768]{0,1:T(8,128)(2,1)}, u32[]{:S(2)}, u32[]{:S(2)}) collective-permute-start(bf16[256,768]{0,1:T(8,128)(2,1)} %get-tuple-element.167), channel_id=1, source_target_pairs={{0,24},{1,25},{2,26},{3,27},{4,28},{5,29},{6,30},{7,31},{8,0},{9,1... | collective-permute-start | bytes 1179656 | tf_op jit(solution)/shard_map/ppermute | solution.py:1164
  442.1 3.3 collective-permute-start.59
  459.0 2.4 fusion.68
  461.4 3.0 reshape.575
  464.4 4.4 slice_reduce_fusion.1
  469.9 2.8 convert_bitcast_fusion
  477.7 5.9 collective-permute-start.71
  492.0 7.3 %collective-permute-start.67 = (bf16[96,2304]{1,0:T(8,128)(2,1)S(1)}, bf16[96,2304]{1,0:T(8,128)(2,1)}, u32[]{:S(2)}, u32[]{:S(2)}) collective-permute-start(bf16[96,2304]{1,0:T(8,128)(2,1)S(1)} %get-tuple-element.153), channel_id=1, source_target_pairs={{8,0},{20,12},{24,16},{4,28},{13,5},{17,9},{29,21},{1,25},{10,2},{... | collective-permute-start | bytes 1327112 | tf_op jit(solution)/shard_map/ppermute | solution.py:1136
  499.3 19.2 %collective-permute-done.71.refs_6_ = bf16[96,2304]{1,0:T(8,128)(2,1)} collective-permute-done((bf16[96,2304]{1,0:T(8,128)(2,1)}, bf16[96,2304]{1,0:T(8,128)(2,1)}, u32[]{:S(2)}, u32[]{:S(2)}) %collective-permute-start.71) | collective-permute-done | bytes 442400 | tf_op jit(solution)/shard_map/ppermute | solution.py:1136
  522.6 2.6 collective-permute-done.70.refs_5_
  525.9 4.0 orthogonal_shards.1
  537.8 8.7 %orthogonal_router.1 = f32[128,768]{1,0:T(8,128)} custom-call(f32[128,768]{1,0:T(8,128)} %concatenate.138.matrix_ref), custom_call_target="tpu_custom_call" | custom-call | flops 2000000000 | bytes 1000000 | tf_op jit(solution)/shard_map/orthogonal_router/pallas_call | solution.py:1106
  547.8 34.0 %collective-permute-done.73 = bf16[96,2304]{1,0:T(8,128)(2,1)S(1)} collective-permute-done((bf16[96,2304]{1,0:T(8,128)(2,1)}, bf16[96,2304]{1,0:T(8,128)(2,1)S(1)}, u32[]{:S(2)}, u32[]{:S(2)}) %collective-permute-start.73) | collective-permute-done | bytes 442400 | tf_op jit(solution)/shard_map/ppermute | solution.py:1144
  587.6 8.2 %collective-permute-done.77 = bf16[96,2304]{1,0:T(8,128)(2,1)S(1)} collective-permute-done((bf16[96,2304]{1,0:T(8,128)(2,1)}, bf16[96,2304]{1,0:T(8,128)(2,1)S(1)}, u32[]{:S(2)}, u32[]{:S(2)}) %collective-permute-start.77) | collective-permute-done | bytes 442400 | tf_op jit(solution)/shard_map/ppermute | solution.py:1144
  596.6 15.1 %collective-permute-done.78 = bf16[96,2304]{1,0:T(8,128)(2,1)S(1)} collective-permute-done((bf16[96,2304]{1,0:T(8,128)(2,1)S(1)}, bf16[96,2304]{1,0:T(8,128)(2,1)S(1)}, u32[]{:S(2)}, u32[]{:S(2)}) %collective-permute-start.78) | collective-permute-done | bytes 442400 | tf_op jit(solution)/shard_map/ppermute | solution.py:1144
  612.4 21.4 %collective-permute-done.79 = bf16[96,2304]{1,0:T(8,128)(2,1)S(1)} collective-permute-done((bf16[96,2304]{1,0:T(8,128)(2,1)S(1)}, bf16[96,2304]{1,0:T(8,128)(2,1)S(1)}, u32[]{:S(2)}, u32[]{:S(2)}) %collective-permute-start.79) | collective-permute-done | bytes 442400 | tf_op jit(solution)/shard_map/ppermute | solution.py:1144
  634.7 2.4 dynamic-slice_bitcast_fusion.4
  641.6 2.7 collective-permute-start.83
  (634 shorter events, 235.6 us)
Async XLA Ops:
  7.2 219.7 %all-gather.7.cloned.1.call-start = ((), (), s32[]{:S(2)}) async-start(), calls=%async_computation.3 | async-start | bytes 3538944 | tf_op jit(solution)/shard_map/all_gather | solution.py:1296
  9.3 217.7 %all-gather.5.cloned.1.call-start = ((), (), s32[]{:S(2)}) async-start(), calls=%async_computation.2 | async-start | bytes 7077888 | tf_op jit(solution)/shard_map/all_gather | solution.py:1295
  14.0 61.2 %collective-permute-start.13 = (bf16[24,1024]{1,0:T(8,128)(2,1)S(1)}, bf16[24,1024]{1,0:T(8,128)(2,1)S(1)}, u32[]{:S(2)}, u32[]{:S(2)}) collective-permute-start(bf16[24,1024]{1,0:T(8,128)(2,1)S(1)} %get-tuple-element.248), channel_id=1, source_target_pairs={{0,2},{1,3},{2,0},{3,1},{4,6},{5,7},{6,4},{7,5},{8,10},{9,11},{10,... | collective-permute-start | bytes 147464 | tf_op jit(solution)/shard_map/ppermute | solution.py:536
  14.3 60.9 %collective-permute-start.15 = (bf16[24,1024]{1,0:T(8,128)(2,1)S(1)}, bf16[24,1024]{1,0:T(8,128)(2,1)S(1)}, u32[]{:S(2)}, u32[]{:S(2)}) collective-permute-start(bf16[24,1024]{1,0:T(8,128)(2,1)S(1)} %get-tuple-element.249), channel_id=1, source_target_pairs={{0,3},{1,2},{2,1},{3,0},{4,7},{5,6},{6,5},{7,4},{8,11},{9,10},{10,... | collective-permute-start | bytes 147464 | tf_op jit(solution)/shard_map/ppermute | solution.py:536
  17.0 444.5 %reduce-scatter.2.cloned.1.call-start = ((), (), s32[]{:S(2)}) async-start(), calls=%async_computation.1 | async-start | bytes 7077888 | tf_op jit(solution)/shard_map/reduce_scatter | solution.py:1372
  23.4 21.2 %collective-permute-start.7 = (bf16[96,896]{1,0:T(8,128)(2,1)S(1)}, bf16[96,896]{1,0:T(8,128)(2,1)S(1)}, u32[]{:S(2)}, u32[]{:S(2)}) collective-permute-start(bf16[96,896]{1,0:T(8,128)(2,1)S(1)} %pad_maximum_fusion.13.refs_0_), channel_id=1, source_target_pairs={{0,16},{1,17},{2,18},{3,19},{4,20},{5,21},{6,22},{7,23},{8,24},{9,... | collective-permute-start | bytes 516104 | tf_op jit(solution)/shard_map/ppermute | solution.py:1164
  25.7 22.9 %collective-permute-start.6 = (bf16[96,896]{1,0:T(8,128)(2,1)S(1)}, bf16[96,896]{1,0:T(8,128)(2,1)S(1)}, u32[]{:S(2)}, u32[]{:S(2)}) collective-permute-start(bf16[96,896]{1,0:T(8,128)(2,1)S(1)} %pad_maximum_fusion.13.refs_0_), channel_id=1, source_target_pairs={{0,8},{1,9},{2,10},{3,11},{4,12},{5,13},{6,14},{7,15},{8,16},{9,17... | collective-permute-start | bytes 516104 | tf_op jit(solution)/shard_map/ppermute | solution.py:1164
  37.3 38.0 %collective-permute-start.14 = (bf16[24,1024]{1,0:T(8,128)(2,1)S(1)}, bf16[24,1024]{1,0:T(8,128)(2,1)S(1)}, u32[]{:S(2)}, u32[]{:S(2)}) collective-permute-start(bf16[24,1024]{1,0:T(8,128)(2,1)S(1)} %get-tuple-element.250), channel_id=1, source_target_pairs={{0,1},{1,0},{2,3},{3,2},{4,5},{5,4},{6,7},{7,6},{8,9},{9,8},{10,11... | collective-permute-start | bytes 147464 | tf_op jit(solution)/shard_map/ppermute | solution.py:536
  44.6 54.7 %collective-permute-start.1 = (bf16[2,128,896]{2,1,0:T(8,128)(2,1)}, bf16[2,128,896]{2,1,0:T(8,128)(2,1)}, u32[]{:S(2)}, u32[]{:S(2)}) collective-permute-start(bf16[2,128,896]{2,1,0:T(8,128)(2,1)} %maximum_maximum_fusion), channel_id=1, source_target_pairs={{0,1},{1,0},{2,3},{3,2},{4,5},{5,4},{6,7},{7,6},{8,9},{9,8},{10,11... | collective-permute-start | bytes 1376264 | tf_op jit(solution)/shard_map/ppermute | solution.py:536
  49.5 39.8 %collective-permute-start.9 = (bf16[4,96,896]{2,1,0:T(8,128)(2,1)}, bf16[4,96,896]{2,1,0:T(8,128)(2,1)}, u32[]{:S(2)}, u32[]{:S(2)}) collective-permute-start(bf16[4,96,896]{2,1,0:T(8,128)(2,1)} %pad_maximum_fusion.5), channel_id=1, source_target_pairs={{0,4},{1,5},{2,6},{3,7},{4,0},{5,1},{6,2},{7,3},{8,12},{9,13},{10,... | collective-permute-start | bytes 2064392 | tf_op jit(solution)/shard_map/ppermute | solution.py:1169
  75.4 38.5 %collective-permute-start.18 = (bf16[96,1536]{1,0:T(8,128)(2,1)S(1)}, bf16[96,1536]{1,0:T(8,128)(2,1)S(1)}, u32[]{:S(2)}, u32[]{:S(2)}) collective-permute-start(bf16[96,1536]{1,0:T(8,128)(2,1)S(1)} %constant_dynamic-update-slice_fusion.refs_0_), channel_id=1, source_target_pairs={{0,24},{1,25},{2,26},{3,27},{4,28},{5,29},{6,30},{7,31},{8,0},{9,1... | collective-permute-start | bytes 884744 | tf_op jit(solution)/shard_map/ppermute | solution.py:1164
  79.3 34.6 %collective-permute-start.17 = (bf16[96,1536]{1,0:T(8,128)(2,1)S(1)}, bf16[96,1536]{1,0:T(8,128)(2,1)S(1)}, u32[]{:S(2)}, u32[]{:S(2)}) collective-permute-start(bf16[96,1536]{1,0:T(8,128)(2,1)S(1)} %constant_dynamic-update-slice_fusion.refs_0_), channel_id=1, source_target_pairs={{0,16},{1,17},{2,18},{3,19},{4,20},{5,21},{6,22},{7,23},{8,24},{9,... | collective-permute-start | bytes 884744 | tf_op jit(solution)/shard_map/ppermute | solution.py:1164
  86.9 28.0 %collective-permute-start.16 = (bf16[96,1536]{1,0:T(8,128)(2,1)S(1)}, bf16[96,1536]{1,0:T(8,128)(2,1)S(1)}, u32[]{:S(2)}, u32[]{:S(2)}) collective-permute-start(bf16[96,1536]{1,0:T(8,128)(2,1)S(1)} %constant_dynamic-update-slice_fusion.refs_0_), channel_id=1, source_target_pairs={{0,8},{1,9},{2,10},{3,11},{4,12},{5,13},{6,14},{7,15},{8,16},{9,17... | collective-permute-start | bytes 884744 | tf_op jit(solution)/shard_map/ppermute | solution.py:1164
  99.3 19.9 %collective-permute-start.20 = (bf16[8,24,768]{2,1,0:T(8,128)(2,1)S(1)}, bf16[8,24,768]{2,1,0:T(8,128)(2,1)}, u32[]{:S(2)}, u32[]{:S(2)}) collective-permute-start(bf16[8,24,768]{2,1,0:T(8,128)(2,1)S(1)} %reshape.511), channel_id=1, source_target_pairs={{0,2},{1,3},{2,0},{3,1},{4,6},{5,7},{6,4},{7,5},{8,10},{9,11},{10,... | collective-permute-start | bytes 884744 | tf_op jit(solution)/shard_map/ppermute | solution.py:536
  100.1 21.1 %collective-permute-start.23 = (bf16[2,128,768]{2,1,0:T(8,128)(2,1)}, bf16[2,128,768]{2,1,0:T(8,128)(2,1)}, u32[]{:S(2)}, u32[]{:S(2)}) collective-permute-start(bf16[2,128,768]{2,1,0:T(8,128)(2,1)} %param.20), channel_id=1, source_target_pairs={{0,2},{1,3},{2,0},{3,1},{4,6},{5,7},{6,4},{7,5},{8,10},{9,11},{10,... | collective-permute-start | bytes 1179656 | tf_op jit(solution)/shard_map/ppermute | solution.py:536
  115.0 36.1 %collective-permute-start.19 = (bf16[4,96,1536]{2,1,0:T(8,128)(2,1)S(1)}, bf16[4,96,1536]{2,1,0:T(8,128)(2,1)}, u32[]{:S(2)}, u32[]{:S(2)}) collective-permute-start(bf16[4,96,1536]{2,1,0:T(8,128)(2,1)S(1)} %pad_maximum_fusion.3), channel_id=1, source_target_pairs={{0,4},{1,5},{2,6},{3,7},{4,0},{5,1},{6,2},{7,3},{8,12},{9,13},{10,... | collective-permute-start | bytes 3538952 | tf_op jit(solution)/shard_map/ppermute | solution.py:1169
  121.2 38.7 %collective-permute-start.11 = (bf16[2,512,192]{2,1,0:T(8,128)(2,1)}, bf16[2,512,192]{2,1,0:T(8,128)(2,1)S(1)}, u32[]{:S(2)}, u32[]{:S(2)}) collective-permute-start(bf16[2,512,192]{2,1,0:T(8,128)(2,1)} %get-tuple-element.55), channel_id=1, source_target_pairs={{0,1},{1,0},{2,3},{3,2},{4,5},{5,4},{6,7},{7,6},{8,9},{9,8},{10,11... | collective-permute-start | bytes 1179656 | tf_op jit(solution)/shard_map/ppermute | solution.py:536
  128.5 31.4 %collective-permute-start.12 = (bf16[2,512,192]{2,1,0:T(8,128)(2,1)}, bf16[2,512,192]{2,1,0:T(8,128)(2,1)}, u32[]{:S(2)}, u32[]{:S(2)}) collective-permute-start(bf16[2,512,192]{2,1,0:T(8,128)(2,1)} %collective-permute-done.10), channel_id=1, source_target_pairs={{0,1},{1,0},{2,3},{3,2},{4,5},{5,4},{6,7},{7,6},{8,9},{9,8},{10,11... | collective-permute-start | bytes 1179656 | tf_op jit(solution)/shard_map/ppermute | solution.py:536
  187.0 32.9 %collective-permute-start.26 = (bf16[4,96,1536]{2,1,0:T(8,128)(2,1)}, bf16[4,96,1536]{2,1,0:T(8,128)(2,1)}, u32[]{:S(2)}, u32[]{:S(2)}) collective-permute-start(bf16[4,96,1536]{2,1,0:T(8,128)(2,1)} %fusion.6), channel_id=1, source_target_pairs={{0,4},{1,5},{2,6},{3,7},{4,0},{5,1},{6,2},{7,3},{8,12},{9,13},{10,... | collective-permute-start | bytes 3538952 | tf_op jit(solution)/shard_map/ppermute | solution.py:1169
  189.5 88.6 %collective-permute-start.54 = (bf16[24,1600]{1,0:T(8,128)(2,1)S(1)}, bf16[24,1600]{1,0:T(8,128)(2,1)S(1)}, u32[]{:S(2)}, u32[]{:S(2)}) collective-permute-start(bf16[24,1600]{1,0:T(8,128)(2,1)S(1)} %get-tuple-element.238), channel_id=1, source_target_pairs={{0,2},{1,3},{2,0},{3,1},{4,6},{5,7},{6,4},{7,5},{8,10},{9,11},{10,... | collective-permute-start | bytes 230408 | tf_op jit(solution)/shard_map/ppermute | solution.py:536
  189.8 88.4 %collective-permute-start.56 = (bf16[24,1600]{1,0:T(8,128)(2,1)S(1)}, bf16[24,1600]{1,0:T(8,128)(2,1)S(1)}, u32[]{:S(2)}, u32[]{:S(2)}) collective-permute-start(bf16[24,1600]{1,0:T(8,128)(2,1)S(1)} %get-tuple-element.239), channel_id=1, source_target_pairs={{0,3},{1,2},{2,1},{3,0},{4,7},{5,6},{6,5},{7,4},{8,11},{9,10},{10,... | collective-permute-start | bytes 230408 | tf_op jit(solution)/shard_map/ppermute | solution.py:536
  222.6 51.3 %collective-permute-start.31 = (bf16[96,1536]{1,0:T(8,128)(2,1)S(1)}, bf16[96,1536]{1,0:T(8,128)(2,1)S(1)}, u32[]{:S(2)}, u32[]{:S(2)}) collective-permute-start(bf16[96,1536]{1,0:T(8,128)(2,1)S(1)} %get-tuple-element.173), channel_id=1, source_target_pairs={{0,24},{1,25},{2,26},{3,27},{4,28},{5,29},{6,30},{7,31},{8,0},{9,1... | collective-permute-start | bytes 884744 | tf_op jit(solution)/shard_map/ppermute | solution.py:1164
  222.6 53.1 %collective-permute-start.30 = (bf16[96,1536]{1,0:T(8,128)(2,1)S(1)}, bf16[96,1536]{1,0:T(8,128)(2,1)S(1)}, u32[]{:S(2)}, u32[]{:S(2)}) collective-permute-start(bf16[96,1536]{1,0:T(8,128)(2,1)S(1)} %get-tuple-element.174), channel_id=1, source_target_pairs={{0,16},{1,17},{2,18},{3,19},{4,20},{5,21},{6,22},{7,23},{8,24},{9,... | collective-permute-start | bytes 884744 | tf_op jit(solution)/shard_map/ppermute | solution.py:1164
  225.0 50.8 %collective-permute-start.29 = (bf16[96,1536]{1,0:T(8,128)(2,1)S(1)}, bf16[96,1536]{1,0:T(8,128)(2,1)S(1)}, u32[]{:S(2)}, u32[]{:S(2)}) collective-permute-start(bf16[96,1536]{1,0:T(8,128)(2,1)S(1)} %get-tuple-element.175), channel_id=1, source_target_pairs={{0,8},{1,9},{2,10},{3,11},{4,12},{5,13},{6,14},{7,15},{8,16},{9,17... | collective-permute-start | bytes 884744 | tf_op jit(solution)/shard_map/ppermute | solution.py:1164
  285.4 51.6 %collective-permute-start.37 = (bf16[4,256,768]{1,2,0:T(8,128)(2,1)}, bf16[4,256,768]{1,2,0:T(8,128)(2,1)}, u32[]{:S(2)}, u32[]{:S(2)}) collective-permute-start(bf16[4,256,768]{1,2,0:T(8,128)(2,1)} %bitcast.500), channel_id=1, source_target_pairs={{0,4},{1,5},{2,6},{3,7},{4,0},{5,1},{6,2},{7,3},{8,12},{9,13},{10,... | collective-permute-start | bytes 4718600 | tf_op jit(solution)/shard_map/ppermute | solution.py:1169
  320.9 40.6 %collective-permute-start.45 = (bf16[2,8,24,768]{3,2,1,0:T(8,128)(2,1)}, bf16[2,8,24,768]{3,2,1,0:T(8,128)(2,1)}, u32[]{:S(2)}, u32[]{:S(2)}) collective-permute-start(bf16[2,8,24,768]{3,2,1,0:T(8,128)(2,1)} %dynamic-slice_bitcast_fusion.3), channel_id=1, source_target_pairs={{0,1},{1,0},{2,3},{3,2},{4,5},{5,4},{6,7},{7,6},{8,9},{9,8},{10,11... | collective-permute-start | bytes 1769480 | tf_op jit(solution)/shard_map/ppermute | solution.py:536
  355.7 31.1 %collective-permute-start.65 = (bf16[64,768]{1,0:T(8,128)(2,1)}, bf16[64,768]{1,0:T(8,128)(2,1)}, u32[]{:S(2)}, u32[]{:S(2)}) collective-permute-start(bf16[64,768]{1,0:T(8,128)(2,1)} %get-tuple-element.131), channel_id=1, source_target_pairs={{2,3},{6,7},{10,11},{14,15},{18,19},{22,23},{26,27},{30,31}} | collective-permute-start | bytes 294920 | tf_op jit(solution)/shard_map/ppermute | solution.py:1495
  357.0 29.8 %collective-permute-start.64 = (bf16[64,768]{1,0:T(8,128)(2,1)}, bf16[64,768]{1,0:T(8,128)(2,1)}, u32[]{:S(2)}, u32[]{:S(2)}) collective-permute-start(bf16[64,768]{1,0:T(8,128)(2,1)} %get-tuple-element.131), channel_id=1, source_target_pairs={{1,3},{5,7},{9,11},{13,15},{17,19},{21,23},{25,27},{29,31}} | collective-permute-start | bytes 294920 | tf_op jit(solution)/shard_map/ppermute | solution.py:1495
  358.3 28.5 %collective-permute-start.63 = (bf16[64,768]{1,0:T(8,128)(2,1)}, bf16[64,768]{1,0:T(8,128)(2,1)}, u32[]{:S(2)}, u32[]{:S(2)}) collective-permute-start(bf16[64,768]{1,0:T(8,128)(2,1)} %get-tuple-element.131), channel_id=1, source_target_pairs={{0,3},{4,7},{8,11},{12,15},{16,19},{20,23},{24,27},{28,31}} | collective-permute-start | bytes 294920 | tf_op jit(solution)/shard_map/ppermute | solution.py:1495
  375.3 23.3 %collective-permute-start.47 = (bf16[4,96,768]{2,1,0:T(8,128)(2,1)}, bf16[4,96,768]{2,1,0:T(8,128)(2,1)}, u32[]{:S(2)}, u32[]{:S(2)}) collective-permute-start(bf16[4,96,768]{2,1,0:T(8,128)(2,1)} %fusion.32), channel_id=1, source_target_pairs={{0,4},{1,5},{2,6},{3,7},{4,0},{5,1},{6,2},{7,3},{8,12},{9,13},{10,... | collective-permute-start | bytes 1769480 | tf_op jit(solution)/shard_map/ppermute | solution.py:1169
  400.0 33.0 %collective-permute-start.48 = (bf16[96,768]{1,0:T(8,128)(2,1)S(1)}, bf16[96,768]{1,0:T(8,128)(2,1)S(1)}, u32[]{:S(2)}, u32[]{:S(2)}) collective-permute-start(bf16[96,768]{1,0:T(8,128)(2,1)S(1)} %get-tuple-element.189), channel_id=1, source_target_pairs={{0,8},{1,9},{2,10},{3,11},{4,12},{5,13},{6,14},{7,15},{8,16},{9,17... | collective-permute-start | bytes 442376 | tf_op jit(solution)/shard_map/ppermute | solution.py:1164
  402.3 30.6 %collective-permute-start.50 = (bf16[96,768]{1,0:T(8,128)(2,1)S(1)}, bf16[96,768]{1,0:T(8,128)(2,1)S(1)}, u32[]{:S(2)}, u32[]{:S(2)}) collective-permute-start(bf16[96,768]{1,0:T(8,128)(2,1)S(1)} %get-tuple-element.190), channel_id=1, source_target_pairs={{0,24},{1,25},{2,26},{3,27},{4,28},{5,29},{6,30},{7,31},{8,0},{9,1... | collective-permute-start | bytes 442376 | tf_op jit(solution)/shard_map/ppermute | solution.py:1164
  402.3 30.6 %collective-permute-start.49 = (bf16[96,768]{1,0:T(8,128)(2,1)S(1)}, bf16[96,768]{1,0:T(8,128)(2,1)S(1)}, u32[]{:S(2)}, u32[]{:S(2)}) collective-permute-start(bf16[96,768]{1,0:T(8,128)(2,1)S(1)} %get-tuple-element.191), channel_id=1, source_target_pairs={{0,16},{1,17},{2,18},{3,19},{4,20},{5,21},{6,22},{7,23},{8,24},{9,... | collective-permute-start | bytes 442376 | tf_op jit(solution)/shard_map/ppermute | solution.py:1164
  414.7 42.1 %collective-permute-start.60 = (bf16[256,768]{0,1:T(8,128)(2,1)}, bf16[256,768]{0,1:T(8,128)(2,1)}, u32[]{:S(2)}, u32[]{:S(2)}) collective-permute-start(bf16[256,768]{0,1:T(8,128)(2,1)} %get-tuple-element.166), channel_id=1, source_target_pairs={{0,8},{1,9},{2,10},{3,11},{4,12},{5,13},{6,14},{7,15},{8,16},{9,17... | collective-permute-start | bytes 1179656 | tf_op jit(solution)/shard_map/ppermute | solution.py:1164
  417.5 39.4 %collective-permute-start.62 = (bf16[256,768]{0,1:T(8,128)(2,1)}, bf16[256,768]{0,1:T(8,128)(2,1)}, u32[]{:S(2)}, u32[]{:S(2)}) collective-permute-start(bf16[256,768]{0,1:T(8,128)(2,1)} %get-tuple-element.167), channel_id=1, source_target_pairs={{0,24},{1,25},{2,26},{3,27},{4,28},{5,29},{6,30},{7,31},{8,0},{9,1... | collective-permute-start | bytes 1179656 | tf_op jit(solution)/shard_map/ppermute | solution.py:1164
  439.3 19.7 %collective-permute-start.61 = (bf16[256,768]{0,1:T(8,128)(2,1)}, bf16[256,768]{0,1:T(8,128)(2,1)}, u32[]{:S(2)}, u32[]{:S(2)}) collective-permute-start(bf16[256,768]{0,1:T(8,128)(2,1)} %get-tuple-element.168), channel_id=1, source_target_pairs={{0,16},{1,17},{2,18},{3,19},{4,20},{5,21},{6,22},{7,23},{8,24},{9,... | collective-permute-start | bytes 1179656 | tf_op jit(solution)/shard_map/ppermute | solution.py:1164
  477.7 40.8 %collective-permute-start.71 = (bf16[96,2304]{1,0:T(8,128)(2,1)}, bf16[96,2304]{1,0:T(8,128)(2,1)}, u32[]{:S(2)}, u32[]{:S(2)}) collective-permute-start(bf16[96,2304]{1,0:T(8,128)(2,1)} %get-tuple-element.149), channel_id=1, source_target_pairs={{24,0},{4,12},{8,16},{20,28},{29,5},{1,9},{13,21},{17,25},{26,2},{... | collective-permute-start | bytes 1327112 | tf_op jit(solution)/shard_map/ppermute | solution.py:1136
  487.8 37.4 %collective-permute-start.70 = (bf16[96,2304]{1,0:T(8,128)(2,1)}, bf16[96,2304]{1,0:T(8,128)(2,1)S(1)}, u32[]{:S(2)}, u32[]{:S(2)}) collective-permute-start(bf16[96,2304]{1,0:T(8,128)(2,1)} %get-tuple-element.150), channel_id=1, source_target_pairs={{20,0},{0,12},{4,16},{16,28},{25,5},{29,9},{9,21},{13,25},{22,2},{... | collective-permute-start | bytes 1327112 | tf_op jit(solution)/shard_map/ppermute | solution.py:1136
  489.1 36.1 %collective-permute-start.69 = (bf16[96,2304]{1,0:T(8,128)(2,1)}, bf16[96,2304]{1,0:T(8,128)(2,1)}, u32[]{:S(2)}, u32[]{:S(2)}) collective-permute-start(bf16[96,2304]{1,0:T(8,128)(2,1)} %get-tuple-element.151), channel_id=1, source_target_pairs={{16,0},{28,12},{0,16},{12,28},{21,5},{25,9},{5,21},{9,25},{18,2},{... | collective-permute-start | bytes 1327112 | tf_op jit(solution)/shard_map/ppermute | solution.py:1136
  490.5 34.6 %collective-permute-start.68 = (bf16[96,2304]{1,0:T(8,128)(2,1)}, bf16[96,2304]{1,0:T(8,128)(2,1)}, u32[]{:S(2)}, u32[]{:S(2)}) collective-permute-start(bf16[96,2304]{1,0:T(8,128)(2,1)} %get-tuple-element.152), channel_id=1, source_target_pairs={{12,0},{24,12},{28,16},{8,28},{17,5},{21,9},{1,21},{5,25},{14,2},{... | collective-permute-start | bytes 1327112 | tf_op jit(solution)/shard_map/ppermute | solution.py:1136
  492.0 33.2 %collective-permute-start.67 = (bf16[96,2304]{1,0:T(8,128)(2,1)S(1)}, bf16[96,2304]{1,0:T(8,128)(2,1)}, u32[]{:S(2)}, u32[]{:S(2)}) collective-permute-start(bf16[96,2304]{1,0:T(8,128)(2,1)S(1)} %get-tuple-element.153), channel_id=1, source_target_pairs={{8,0},{20,12},{24,16},{4,28},{13,5},{17,9},{29,21},{1,25},{10,2},{... | collective-permute-start | bytes 1327112 | tf_op jit(solution)/shard_map/ppermute | solution.py:1136
  529.9 51.9 %collective-permute-start.73 = (bf16[96,2304]{1,0:T(8,128)(2,1)}, bf16[96,2304]{1,0:T(8,128)(2,1)S(1)}, u32[]{:S(2)}, u32[]{:S(2)}) collective-permute-start(bf16[96,2304]{1,0:T(8,128)(2,1)} %get-tuple-element.88), channel_id=1, source_target_pairs={{0,4},{12,16},{16,20},{28,0},{5,9},{9,13},{21,25},{25,29},{2,6},{1... | collective-permute-start | bytes 1327112 | tf_op jit(solution)/shard_map/ppermute | solution.py:1144
  531.2 52.7 %collective-permute-start.74 = (bf16[96,2304]{1,0:T(8,128)(2,1)}, bf16[96,2304]{1,0:T(8,128)(2,1)S(1)}, u32[]{:S(2)}, u32[]{:S(2)}) collective-permute-start(bf16[96,2304]{1,0:T(8,128)(2,1)} %get-tuple-element.89), channel_id=1, source_target_pairs={{0,8},{12,20},{16,24},{28,4},{5,13},{9,17},{21,29},{25,1},{2,10},{... | collective-permute-start | bytes 1327112 | tf_op jit(solution)/shard_map/ppermute | solution.py:1144
  532.5 53.5 %collective-permute-start.75 = (bf16[96,2304]{1,0:T(8,128)(2,1)}, bf16[96,2304]{1,0:T(8,128)(2,1)S(1)}, u32[]{:S(2)}, u32[]{:S(2)}) collective-permute-start(bf16[96,2304]{1,0:T(8,128)(2,1)} %get-tuple-element.90), channel_id=1, source_target_pairs={{0,12},{12,24},{16,28},{28,8},{5,17},{9,21},{21,1},{25,5},{2,14},{... | collective-permute-start | bytes 1327112 | tf_op jit(solution)/shard_map/ppermute | solution.py:1144
  533.2 53.6 %collective-permute-start.76 = (bf16[96,2304]{1,0:T(8,128)(2,1)}, bf16[96,2304]{1,0:T(8,128)(2,1)S(1)}, u32[]{:S(2)}, u32[]{:S(2)}) collective-permute-start(bf16[96,2304]{1,0:T(8,128)(2,1)} %get-tuple-element.91), channel_id=1, source_target_pairs={{0,16},{12,28},{16,0},{28,12},{5,21},{9,25},{21,5},{25,9},{2,18},{... | collective-permute-start | bytes 1327112 | tf_op jit(solution)/shard_map/ppermute | solution.py:1144
  533.9 61.9 %collective-permute-start.77 = (bf16[96,2304]{1,0:T(8,128)(2,1)}, bf16[96,2304]{1,0:T(8,128)(2,1)S(1)}, u32[]{:S(2)}, u32[]{:S(2)}) collective-permute-start(bf16[96,2304]{1,0:T(8,128)(2,1)} %get-tuple-element.92), channel_id=1, source_target_pairs={{0,20},{12,0},{16,4},{28,16},{5,25},{9,29},{21,9},{25,13},{2,22},{... | collective-permute-start | bytes 1327112 | tf_op jit(solution)/shard_map/ppermute | solution.py:1144
  581.8 29.8 %collective-permute-start.78 = (bf16[96,2304]{1,0:T(8,128)(2,1)S(1)}, bf16[96,2304]{1,0:T(8,128)(2,1)S(1)}, u32[]{:S(2)}, u32[]{:S(2)}) collective-permute-start(bf16[96,2304]{1,0:T(8,128)(2,1)S(1)} %copy-done.89), channel_id=1, source_target_pairs={{0,24},{12,4},{16,8},{28,20},{5,29},{9,1},{21,13},{25,17},{2,26},{... | collective-permute-start | bytes 1327112 | tf_op jit(solution)/shard_map/ppermute | solution.py:1144
  583.9 50.0 %collective-permute-start.79 = (bf16[96,2304]{1,0:T(8,128)(2,1)S(1)}, bf16[96,2304]{1,0:T(8,128)(2,1)S(1)}, u32[]{:S(2)}, u32[]{:S(2)}) collective-permute-start(bf16[96,2304]{1,0:T(8,128)(2,1)S(1)} %copy-done.88), channel_id=1, source_target_pairs={{0,28},{12,8},{16,12},{28,24},{5,1},{9,5},{21,17},{25,21},{2,30},{... | collective-permute-start | bytes 1327112 | tf_op jit(solution)/shard_map/ppermute | solution.py:1144
  (134 other events, 1181.7 us)
Sparse Core Ops, SparseCore 0:
  10.8 96.9 all-gather.6
  110.0 107.7 all-gather.4
  279.0 117.5 reduce-scatter.1
